TPU v7x, 32 devices: a whole 2x2x4 slice. The times are simulated.
32 devices in a mesh: dp: 16 (over z, x, core), seq: 2 (over y).
Axes of the slice: x: 2, y: 2, z: 4, core: 2. Of those that a mesh axis runs over, the one named last changes fastest.
Arguments:
- tokens: bfloat16 [16, 1024, 768], P('dp', 'seq'), may hold values from -6 to 6
- split_points: int32 [16], P('dp'), may hold values from 128 to 896, as said below
- cotangent: bfloat16 [16, 1024, 768], P('dp', 'seq'), may hold values from -6 to 6
- norm_gain: bfloat16 [2, 768], P(None, ('dp', 'seq')), may hold values from 0.5 to 1.5
- in_weight: bfloat16 [2, 768, 2304], P(None, ('dp', 'seq')), may hold values from -0.21875 to 0.21875
- short_taps: bfloat16 [2, 5, 2304], P(None, None, ('dp', 'seq')), may hold values from -2.5 to 2.5
- cond_taps: bfloat16 [2, 5, 768], P(None, None, ('dp', 'seq')), may hold values from -2.5 to 2.5
- out_weight: bfloat16 [2, 768, 768], P(None, ('dp', 'seq')), may hold values from -0.21875 to 0.21875
- mlp_gain: bfloat16 [2, 768], P(None, ('dp', 'seq')), may hold values from 0.5 to 1.5
- gate_up: bfloat16 [2, 768, 6144], P(None, ('dp', 'seq')), may hold values from -0.21875 to 0.21875
- down_weight: bfloat16 [2, 3072, 768], P(None, ('dp', 'seq')), may hold values from -0.21875 to 0.21875
Outputs:
- activations: bfloat16 [16, 1024, 768], P('dp', 'seq')
- token_grad: float32 [16, 1024, 768], P('dp', 'seq')
- norm_gain_grad: float32 [2, 768], P(None, ('dp', 'seq'))
- in_weight_grad: float32 [2, 768, 2304], P(None, ('dp', 'seq'))
- short_taps_grad: float32 [2, 5, 2304], P(None, None, ('dp', 'seq'))
- cond_taps_grad: float32 [2, 5, 768], P(None, None, ('dp', 'seq'))
- out_weight_grad: float32 [2, 768, 768], P(None, ('dp', 'seq'))
- mlp_gain_grad: float32 [2, 768], P(None, ('dp', 'seq'))
- gate_up_grad: float32 [2, 768, 6144], P(None, ('dp', 'seq'))
- down_weight_grad: float32 [2, 3072, 768], P(None, ('dp', 'seq'))
Inputs may be any that keep to these rules, and one draw needn't show every extreme that they name: `split_points`: each split point lies at least 128 rows from both ends of its pair and from row 512.
All inputs are finite; a program needn't handle non-finite values.
Results may differ from a plain program's by a relative error of at most 0.025.
Values may be sent and summed in bfloat16 or wider, within the bound.
A program may use at most 448 MiB of HBM per device.

v0:
```python
import functools
import math

import jax
import jax.numpy as jnp
from jax import lax
from jax.sharding import PartitionSpec as P

transform_precision = lax.Precision.HIGH
epsilon = 1e-05


def with_halo(cells, sides, width):
    for axis, dim in sides:
        count = lax.axis_size(axis)
        ends = count - 1
        head = lax.slice_in_dim(cells, 0, width, axis=dim)
        tail = lax.slice_in_dim(cells, cells.shape[dim] - width, cells.shape[dim], axis=dim)
        cells = jnp.concatenate(
            [
                lax.ppermute(tail, axis, [(i, (i + 1) % count) for i in range(ends)]),
                cells,
                lax.ppermute(head, axis, [((i + 1) % count, i) for i in range(ends)]),
            ],
            axis=dim,
        )
    return cells


def normalize(inputs, gain):
    center = inputs - jnp.mean(inputs, axis=-1, keepdims=True)
    spread = jnp.mean(center * center, axis=-1, keepdims=True)
    return center * lax.rsqrt(spread + epsilon) * gain


def decay_table(positions, channels, length, features):
    rates = jnp.exp(math.log(1.0 / length) + channels / (features - 1) * math.log(4.0))
    every = jnp.arange(length).astype(jnp.float32)
    scales = lax.rsqrt(jnp.sum(jnp.exp(-2.0 * every[:, None] * rates[None, :]), axis=0))
    return jnp.exp(-positions[:, None] * rates[None, :]) * scales[None, :]


def tap_masks(split_at, row_start, row_count, length):
    places = row_start - 2 + jnp.arange(row_count + 4)
    inside = (places >= 0) & (places < length)
    segment = jnp.where(
        inside[None, :], (places[None, :] >= split_at[:, None]).astype(jnp.int32), -1
    )
    center = segment[:, 2 : 2 + row_count]
    return jnp.stack(
        [
            (segment[:, offset : offset + row_count] == center).astype(jnp.float32)
            for offset in range(5)
        ]
    )


def taps_apply(padded, tap_weights, tap_mask):
    row_count = tap_mask.shape[2]
    summed = jnp.zeros(padded.shape[:1] + (row_count,) + padded.shape[2:], jnp.float32)
    for offset in range(5):
        summed = (
            summed
            + tap_weights[offset]
            * padded[:, offset : offset + row_count]
            * tap_mask[offset][:, :, None]
        )
    return summed


def spectral(filters, signal, split_at, out_rows):
    length = filters.shape[1]
    period = 2 * length
    frequency = jnp.arange(length + 1)
    lag_index = jnp.arange(length)
    step_angle = 2.0 * math.pi / period
    forward_angle = (frequency[:, None] * lag_index[None, :] % period).astype(
        jnp.float32
    ) * step_angle
    cos_fwd = jnp.cos(forward_angle)
    sin_fwd = jnp.sin(forward_angle)
    back_angle = (out_rows[:, None] * frequency[None, :] % period).astype(jnp.float32) * step_angle
    weights_k = jnp.where((frequency == 0) | (frequency == length), 1.0, 2.0) / period
    cos_back = jnp.cos(back_angle) * weights_k[None, :]
    sin_back = jnp.sin(back_angle) * weights_k[None, :]
    filt_re = jnp.einsum("kt,btc->bkc", cos_fwd, filters, precision=transform_precision)
    filt_im = -jnp.einsum("kt,btc->bkc", sin_fwd, filters, precision=transform_precision)
    first_in = (lag_index[None, :] < split_at[:, None]).astype(jnp.float32)
    first_out = (out_rows[None, :] < split_at[:, None]).astype(jnp.float32)
    summed = jnp.zeros(signal.shape[:1] + out_rows.shape + signal.shape[2:], jnp.float32)
    for inside, outside in ((first_in, first_out), (1.0 - first_in, 1.0 - first_out)):
        part = signal * inside[:, :, None]
        part_re = jnp.einsum("kt,btc->bkc", cos_fwd, part, precision=transform_precision)
        part_im = -jnp.einsum("kt,btc->bkc", sin_fwd, part, precision=transform_precision)
        prod_re = filt_re * part_re - filt_im * part_im
        prod_im = filt_re * part_im + filt_im * part_re
        result = jnp.einsum(
            "nk,bkc->bnc", cos_back, prod_re, precision=transform_precision
        ) - jnp.einsum("nk,bkc->bnc", sin_back, prod_im, precision=transform_precision)
        summed = summed + result * outside[:, :, None]
    return summed


def mlp_gate(pre_act, hidden_count):
    return jax.nn.gelu(pre_act[..., :hidden_count], approximate=True) * pre_act[..., hidden_count:]


def rim_edges(grad_pad):
    return jnp.concatenate([grad_pad[:, :2], grad_pad[:, -2:]], axis=1)


def rim_fold(grad_pad, arrived):
    own_rows = grad_pad[:, 2:-2]
    return jnp.concatenate(
        [own_rows[:, :2] + arrived[:, :2], own_rows[:, 2:-2], own_rows[:, -2:] + arrived[:, -2:]],
        axis=1,
    )


def rim_attach(rows, arrived):
    return jnp.concatenate([arrived[:, :2], rows, arrived[:, -2:]], axis=1)


def shards(
    tokens,
    split_points,
    cotangent,
    norm_gain,
    in_weight,
    short_taps,
    cond_taps,
    out_weight,
    mlp_gain,
    gate_up,
    down_weight,
):
    row_count = tokens.shape[1]
    feature_count = tokens.shape[2]
    seq_count = lax.axis_size("seq")
    length = row_count * seq_count
    row_start = lax.axis_index("seq") * row_count
    own_rows = row_start + jnp.arange(row_count)
    tap_mask = tap_masks(split_points, row_start, row_count, length)
    decay = decay_table(
        own_rows.astype(jnp.float32),
        jnp.arange(feature_count).astype(jnp.float32),
        length,
        feature_count,
    )
    layer_count = in_weight.shape[0]
    stream = tokens.astype(jnp.float32)
    stored = []
    for layer_index in range(layer_count):
        gathered = (
            lax.all_gather(norm_gain[layer_index], ("dp", "seq"), axis=0, tiled=True),
            lax.all_gather(in_weight[layer_index], ("dp", "seq"), axis=0, tiled=True),
            lax.all_gather(short_taps[layer_index], ("dp", "seq"), axis=1, tiled=True),
            lax.all_gather(cond_taps[layer_index], ("dp", "seq"), axis=1, tiled=True),
            lax.all_gather(out_weight[layer_index], ("dp", "seq"), axis=0, tiled=True),
            lax.all_gather(mlp_gain[layer_index], ("dp", "seq"), axis=0, tiled=True),
            lax.all_gather(gate_up[layer_index], ("dp", "seq"), axis=0, tiled=True),
            lax.all_gather(down_weight[layer_index], ("dp", "seq"), axis=0, tiled=True),
        )
        norm_g, in_w, short_w, cond_w, out_w, mlp_g, gate_w, down_w = gathered
        hidden_count = down_w.shape[0]
        normed, norm_back = jax.vjp(normalize, stream, norm_g.astype(jnp.float32))
        normed_low = normed.astype(jnp.bfloat16)
        branches = jnp.einsum(
            "btd,de->bte", normed_low, in_w, preferred_element_type=jnp.float32
        ).astype(jnp.bfloat16)
        branch_near = with_halo(rim_edges(branches), (("seq", 1),), 2)
        branch_pad = rim_attach(branches, branch_near)
        mixed, short_back = jax.vjp(
            functools.partial(taps_apply, tap_mask=tap_mask),
            branch_pad.astype(jnp.float32),
            short_w.astype(jnp.float32),
        )
        query = mixed[..., :feature_count]
        key_low = mixed[..., feature_count : 2 * feature_count].astype(jnp.bfloat16)
        value_low = mixed[..., 2 * feature_count :].astype(jnp.bfloat16)
        key_near = with_halo(rim_edges(key_low), (("seq", 1),), 2)
        key_pad = rim_attach(key_low, key_near)
        cond, cond_back = jax.vjp(
            functools.partial(taps_apply, tap_mask=tap_mask),
            key_pad.astype(jnp.float32),
            cond_w.astype(jnp.float32),
        )
        filters = (cond * decay).astype(jnp.bfloat16)
        whole_filt, whole_value = (
            lax.all_gather(filters, "seq", axis=1, tiled=True),
            lax.all_gather(value_low, "seq", axis=1, tiled=True),
        )
        convolved, spec_back = jax.vjp(
            functools.partial(spectral, split_at=split_points, out_rows=own_rows),
            whole_filt.astype(jnp.float32),
            whole_value.astype(jnp.float32),
        )
        gated = (query * convolved).astype(jnp.bfloat16)
        middle = stream + jnp.einsum(
            "btd,de->bte", gated, out_w, preferred_element_type=jnp.float32
        )
        normed_mlp, mlp_norm_back = jax.vjp(normalize, middle, mlp_g.astype(jnp.float32))
        normed_mlp_low = normed_mlp.astype(jnp.bfloat16)
        pre_act = jnp.einsum(
            "btd,de->bte", normed_mlp_low, gate_w, preferred_element_type=jnp.float32
        )
        hidden, gate_back = jax.vjp(functools.partial(mlp_gate, hidden_count=hidden_count), pre_act)
        hidden_low = hidden.astype(jnp.bfloat16)
        stream = middle + jnp.einsum(
            "btf,fd->btd", hidden_low, down_w, preferred_element_type=jnp.float32
        )
        stored.append(
            (
                gathered,
                norm_back,
                normed_low,
                branch_pad,
                short_back,
                key_pad,
                cond_back,
                spec_back,
                query,
                convolved,
                gated,
                mlp_norm_back,
                normed_mlp_low,
                gate_back,
                hidden_low,
            )
        )
    activations = stream.astype(jnp.bfloat16)
    upstream = cotangent.astype(jnp.float32)
    shares_list = []
    for layer_index in reversed(range(layer_count)):
        (
            gathered,
            norm_back,
            normed_low,
            branch_pad,
            short_back,
            key_pad,
            cond_back,
            spec_back,
            query,
            convolved,
            gated,
            mlp_norm_back,
            normed_mlp_low,
            gate_back,
            hidden_low,
        ) = stored[layer_index]
        gathered = (
            lax.all_gather(norm_gain[layer_index], ("dp", "seq"), axis=0, tiled=True),
            lax.all_gather(in_weight[layer_index], ("dp", "seq"), axis=0, tiled=True),
            lax.all_gather(short_taps[layer_index], ("dp", "seq"), axis=1, tiled=True),
            lax.all_gather(cond_taps[layer_index], ("dp", "seq"), axis=1, tiled=True),
            lax.all_gather(out_weight[layer_index], ("dp", "seq"), axis=0, tiled=True),
            lax.all_gather(mlp_gain[layer_index], ("dp", "seq"), axis=0, tiled=True),
            lax.all_gather(gate_up[layer_index], ("dp", "seq"), axis=0, tiled=True),
            lax.all_gather(down_weight[layer_index], ("dp", "seq"), axis=0, tiled=True),
        )
        norm_g, in_w, short_w, cond_w, out_w, mlp_g, gate_w, down_w = gathered
        grad_low = upstream.astype(jnp.bfloat16)
        d_down = jnp.einsum("btf,btd->fd", hidden_low, grad_low, preferred_element_type=jnp.float32)
        d_hidden = jnp.einsum("btd,fd->btf", grad_low, down_w, preferred_element_type=jnp.float32)
        (d_pre,) = gate_back(d_hidden)
        d_pre_low = d_pre.astype(jnp.bfloat16)
        d_gate_up = jnp.einsum(
            "btd,bte->de", normed_mlp_low, d_pre_low, preferred_element_type=jnp.float32
        )
        d_normed_mlp = jnp.einsum(
            "bte,de->btd", d_pre_low, gate_w, preferred_element_type=jnp.float32
        )
        d_middle_part, d_mlp_gain = mlp_norm_back(d_normed_mlp)
        d_middle = upstream + d_middle_part
        middle_low = d_middle.astype(jnp.bfloat16)
        d_out = jnp.einsum("btd,bte->de", gated, middle_low, preferred_element_type=jnp.float32)
        d_gated = jnp.einsum("bte,de->btd", middle_low, out_w, preferred_element_type=jnp.float32)
        d_query = d_gated * convolved
        d_conv = d_gated * query
        whole_dfilt, whole_dvalue = spec_back(d_conv)
        d_filters, d_value = (
            lax.psum_scatter(
                whole_dfilt.astype(jnp.bfloat16), "seq", scatter_dimension=1, tiled=True
            ).astype(jnp.float32),
            lax.psum_scatter(
                whole_dvalue.astype(jnp.bfloat16), "seq", scatter_dimension=1, tiled=True
            ).astype(jnp.float32),
        )
        d_key_pad, d_cond_taps = cond_back(d_filters * decay)
        key_arrived = with_halo(rim_edges(d_key_pad), (("seq", 1),), 2)
        d_key = rim_fold(d_key_pad, key_arrived)
        d_mixed = jnp.concatenate([d_query, d_key, d_value], axis=2)
        d_branch_pad, d_short_taps = short_back(d_mixed)
        branch_arrived = with_halo(
            rim_edges(d_branch_pad).astype(jnp.bfloat16), (("seq", 1),), 2
        ).astype(jnp.float32)
        d_branches = rim_fold(d_branch_pad, branch_arrived).astype(jnp.bfloat16)
        d_in = jnp.einsum("btd,bte->de", normed_low, d_branches, preferred_element_type=jnp.float32)
        d_normed = jnp.einsum("bte,de->btd", d_branches, in_w, preferred_element_type=jnp.float32)
        d_stream_part, d_norm_gain = norm_back(d_normed)
        upstream = d_middle + d_stream_part
        shares = (
            lax.psum_scatter(d_norm_gain, ("dp", "seq"), scatter_dimension=0, tiled=True),
            lax.psum_scatter(d_in, ("dp", "seq"), scatter_dimension=0, tiled=True),
            lax.psum_scatter(d_short_taps, ("dp", "seq"), scatter_dimension=1, tiled=True),
            lax.psum_scatter(d_cond_taps, ("dp", "seq"), scatter_dimension=1, tiled=True),
            lax.psum_scatter(d_out, ("dp", "seq"), scatter_dimension=0, tiled=True),
            lax.psum_scatter(d_mlp_gain, ("dp", "seq"), scatter_dimension=0, tiled=True),
            lax.psum_scatter(d_gate_up, ("dp", "seq"), scatter_dimension=0, tiled=True),
            lax.psum_scatter(d_down, ("dp", "seq"), scatter_dimension=0, tiled=True),
        )
        shares_list.append(shares)
    shares_list = shares_list[::-1]
    stacked = [jnp.stack([shares[position] for shares in shares_list]) for position in range(8)]
    return (
        activations,
        upstream,
        stacked[0],
        stacked[1],
        stacked[2],
        stacked[3],
        stacked[4],
        stacked[5],
        stacked[6],
        stacked[7],
    )


def solution(mesh):
    placed = (
        P("dp", "seq", None),
        P("dp"),
        P("dp", "seq", None),
        P(None, ("dp", "seq")),
        P(None, ("dp", "seq"), None),
        P(None, None, ("dp", "seq")),
        P(None, None, ("dp", "seq")),
        P(None, ("dp", "seq"), None),
        P(None, ("dp", "seq")),
        P(None, ("dp", "seq"), None),
        P(None, ("dp", "seq"), None),
    )
    return jax.shard_map(
        shards,
        mesh=mesh,
        in_specs=placed,
        out_specs=(
            P("dp", "seq", None),
            P("dp", "seq", None),
            P(None, ("dp", "seq")),
            P(None, ("dp", "seq"), None),
            P(None, None, ("dp", "seq")),
            P(None, None, ("dp", "seq")),
            P(None, ("dp", "seq"), None),
            P(None, ("dp", "seq")),
            P(None, ("dp", "seq"), None),
            P(None, ("dp", "seq"), None),
        ),
        check_vma=False,
    )
```

profile of v0, /device:TPU:1, one launch (start us, length us, event | category | flops | bytes accessed | tf_op | source)
XLA Modules:
  0.0 2807.7 jit_solution(2026745355068643337)
XLA Ops:
  11.3 41.4 %all-reduce.57 = (bf16[768]{0:T(1024)(128)(2,1)S(1)}, bf16[768]{0:T(1024)(128)(2,1)S(1)}, bf16[768]{0:T(1024)(128)(2,1)S(1)}, bf16[768]{0:T(1024)(128)(2,1)}) all-reduce(bf16[768]{0:T(1024)(128)(2,1)S(1)} %dynamic-update-slice, bf16[768]{0:T(1024)(128)(2,1)S(1)} %dynamic-update-slice.1, ...), channel_id=3, replica_groups=mesh['dp'=16,'seq'=2] {'dp','seq'}, use_global_device_ids=true, to_apply=%add.44 | all-reduce | flops 3072 | bytes 12288
  54.3 71.6 %all-gather = bf16[1,5,2304]{1,0,2:T(2,128)(2,1)S(1)} all-gather(bf16[1,5,72]{1,0,2:T(2,128)(2,1)S(1)} %copy.170), channel_id=2, replica_groups=mesh['dp'=16,'seq'=2] {'dp','seq'}, dimensions={2}, use_global_device_ids=true | all-gather | bytes 23760 | tf_op jit(solution)/shard_map/all_gather | solution.py:157
  128.4 34.9 %slice_reduce_fusion.9 = (f32[2304]{0:T(1024)S(1)}, f32[2304]{0:T(1024)S(1)}, f32[2304]{0:T(1024)S(1)}, f32[2304]{0:T(1024)S(1)}, f32[2304]{0:T(1024)S(1)}) fusion(f32[1,5,2304]{1,0,2:T(1,128)S(1)} %convert_element_type.438), kind=kLoop, calls=%fused_computation.414 | loop fusion | bytes 92160 | tf_op jit(solution)/shard_map/jvp()/slice | solution.py:64
  182.0 67.3 %all-gather.3 = bf16[1,5,768]{1,0,2:T(2,128)(2,1)S(1)} all-gather(bf16[1,5,24]{1,0,2:T(2,128)(2,1)S(1)} %copy.171), channel_id=5, replica_groups=mesh['dp'=16,'seq'=2] {'dp','seq'}, dimensions={2}, use_global_device_ids=true | all-gather | bytes 7920 | tf_op jit(solution)/shard_map/all_gather | solution.py:158
  278.5 74.7 %all-gather.8 = bf16[1,5,2304]{1,0,2:T(2,128)(2,1)S(1)} all-gather(bf16[1,5,72]{1,0,2:T(2,128)(2,1)S(1)} %copy.172), channel_id=10, replica_groups=mesh['dp'=16,'seq'=2] {'dp','seq'}, dimensions={2}, use_global_device_ids=true | all-gather | bytes 23760 | tf_op jit(solution)/shard_map/all_gather | solution.py:157
  354.8 23.9 fusion.153
  586.8 34.8 %slice_reduce_fusion.4 = (f32[2304]{0:T(1024)S(1)}, f32[2304]{0:T(1024)S(1)}, f32[2304]{0:T(1024)S(1)}, f32[2304]{0:T(1024)S(1)}, f32[2304]{0:T(1024)S(1)}) fusion(f32[1,5,2304]{1,0,2:T(1,128)S(1)} %convert_element_type.442), kind=kLoop, calls=%fused_computation.409 | loop fusion | bytes 92160 | tf_op jit(solution)/shard_map/jvp()/slice | solution.py:64
  630.5 66.5 %all-gather.11 = bf16[1,5,768]{1,0,2:T(2,128)(2,1)S(1)} all-gather(bf16[1,5,24]{1,0,2:T(2,128)(2,1)S(1)} %copy.173), channel_id=13, replica_groups=mesh['dp'=16,'seq'=2] {'dp','seq'}, dimensions={2}, use_global_device_ids=true | all-gather | bytes 7920 | tf_op jit(solution)/shard_map/all_gather | solution.py:158
  718.7 24.1 fusion.163
  765.3 22.8 fusion.168
  788.0 22.8 fusion.170
  919.0 33.7 %all-gather.51.cloned.1.call-done = bf16[1,3072,768]{2,1,0:T(8,128)(2,1)} async-done(((bf16[1,96,768]{2,1,0:T(8,128)(2,1)}), bf16[1,3072,768]{2,1,0:T(8,128)(2,1)}) %all-gather.51.cloned.1.call-update) | async-done | bytes 4718608 | tf_op jit(solution)/shard_map/all_gather | solution.py:162
  1035.2 23.8 fusion.102
  1059.0 24.6 fusion.111
  1083.6 25.4 fusion.319
  1109.1 26.4 fusion.93
  1135.5 23.3 fusion.97
  1159.0 24.6 fusion.333
  1323.5 23.8 fusion.67
  1347.4 26.4 fusion.76
  1373.8 25.7 fusion.324
  1399.6 27.0 fusion.58
  1426.7 22.9 fusion.62
  1449.6 24.4 fusion.338
  1625.0 83.4 %reduce-scatter.29.cloned.1.call-done = f32[24,768]{1,0:T(8,128)} async-done(((f32[768,768]{1,0:T(8,128)}), f32[24,768]{1,0:T(8,128)}) %reduce-scatter.29.cloned.1.call-update) | async-done | bytes 73744 | tf_op jit(solution)/shard_map/reduce_scatter | solution.py:308
  1713.3 128.9 %all-reduce.60.cloned.1.call-done = (f32[768]{0:T(1024)}, f32[768]{0:T(1024)}, f32[5,2304]{1,0:T(8,128)}, f32[5,2304]{1,0:T(8,128)}, f32[5,768]{1,0:T(8,128)}, /...) async-done(((f32[768]{0:T(1024)}, f32[768]{0:T(1024)}, f32[5,2304]{1,0:T(8,128)}, f32[5,2304]{1,0:T(8,128)}, f32[5,768]{1,0:T(8,128)}, /*index=5*/f32[5,768]{1,0:T(8,128)}, ...) | async-done | bytes 135184
  1847.6 135.2 %reduce-scatter.39.cloned.1.call-done = f32[96,768]{1,0:T(8,128)} async-done(((f32[3072,768]{1,0:T(8,128)}), f32[96,768]{1,0:T(8,128)}) %reduce-scatter.39.cloned.1.call-update) | async-done | bytes 294928 | tf_op jit(solution)/shard_map/reduce_scatter | solution.py:311
  1982.8 141.5 %reduce-scatter.37.cloned.1.call-done = f32[96,768]{1,0:T(8,128)} async-done(((f32[3072,768]{1,0:T(8,128)}), f32[96,768]{1,0:T(8,128)}) %reduce-scatter.37.cloned.1.call-update) | async-done | bytes 294928 | tf_op jit(solution)/shard_map/reduce_scatter | solution.py:311
  2126.3 122.4 %reduce-scatter.27.cloned.1.call-done = f32[24,2304]{1,0:T(8,128)} async-done(((f32[768,2304]{1,0:T(8,128)}), f32[24,2304]{1,0:T(8,128)}) %reduce-scatter.27.cloned.1.call-update) | async-done | bytes 221200 | tf_op jit(solution)/shard_map/reduce_scatter | solution.py:305
  2248.6 125.0 %reduce-scatter.25.cloned.1.call-done = f32[24,2304]{1,0:T(8,128)} async-done(((f32[768,2304]{1,0:T(8,128)}), f32[24,2304]{1,0:T(8,128)}) %reduce-scatter.25.cloned.1.call-update) | async-done | bytes 221200 | tf_op jit(solution)/shard_map/reduce_scatter | solution.py:305
  2375.4 210.9 %reduce-scatter.35.cloned.1.call-done = f32[24,6144]{1,0:T(8,128)} async-done(((f32[768,6144]{1,0:T(8,128)}), f32[24,6144]{1,0:T(8,128)}) %reduce-scatter.35.cloned.1.call-update) | async-done | bytes 589840 | tf_op jit(solution)/shard_map/reduce_scatter | solution.py:310
  2586.3 212.1 %reduce-scatter.33.cloned.1.call-done = f32[24,6144]{1,0:T(8,128)} async-done(((f32[768,6144]{1,0:T(8,128)}), f32[24,6144]{1,0:T(8,128)}) %reduce-scatter.33.cloned.1.call-update) | async-done | bytes 589840 | tf_op jit(solution)/shard_map/reduce_scatter | solution.py:310
  (777 shorter events, 812.5 us)
Async XLA Ops:
  7.2 156.2 %all-gather.37.cloned.1.call-start = ((), (), s32[]{:S(2)}) async-start(), calls=%async_computation.28 | async-start | bytes 3649536 | tf_op jit(solution)/shard_map/all_gather | solution.py:156
  9.0 345.9 %all-gather.31.cloned.1.call-start = ((), (), s32[]{:S(2)}) async-start(), calls=%async_computation.13 | async-start | bytes 2359296 | tf_op jit(solution)/shard_map/all_gather | solution.py:191
  181.8 264.9 %all-gather.29.cloned.1.call-start = ((), (), s32[]{:S(2)}) async-start(), calls=%async_computation.12 | async-start | bytes 2359296 | tf_op jit(solution)/shard_map/all_gather | solution.py:190
  273.8 265.9 %all-gather.39.cloned.1.call-start = ((), (), s32[]{:S(2)}) async-start(), calls=%async_computation.29 | async-start | bytes 1216512 | tf_op jit(solution)/shard_map/all_gather | solution.py:159
  274.5 267.9 %all-gather.41.cloned.1.call-start = ((), (), s32[]{:S(2)}) async-start(), calls=%async_computation.30 | async-start | bytes 9732096 | tf_op jit(solution)/shard_map/all_gather | solution.py:161
  275.4 283.5 %all-gather.43.cloned.1.call-start = ((), (), s32[]{:S(2)}) async-start(), calls=%async_computation.31 | async-start | bytes 4866048 | tf_op jit(solution)/shard_map/all_gather | solution.py:162
  276.2 302.1 %all-gather.45.cloned.1.call-start = ((), (), s32[]{:S(2)}) async-start(), calls=%async_computation.32 | async-start | bytes 3649536 | tf_op jit(solution)/shard_map/all_gather | solution.py:156
  277.0 441.7 %all-gather.35.cloned.1.call-start = ((), (), s32[]{:S(2)}) async-start(), calls=%async_computation.15 | async-start | bytes 2359296 | tf_op jit(solution)/shard_map/all_gather | solution.py:191
  582.4 39.3 %collective-permute-start.4 = (bf16[1,2,2304]{2,1,0:T(2,128)(2,1)S(1)}, bf16[1,2,2304]{2,1,0:T(2,128)(2,1)S(1)}, u32[]{:S(2)}, u32[]{:S(2)}) collective-permute-start(bf16[1,2,2304]{2,1,0:T(2,128)(2,1)S(1)} %get-tuple-element.165), channel_id=1, source_target_pairs={{0,1},{2,3},{4,5},{6,7},{8,9},{10,11},{12,13},{14,15},{16,17},{18,... | collective-permute-start | bytes 27656 | tf_op jit(solution)/shard_map/ppermute | solution.py:21
  585.5 36.2 %collective-permute-start.5 = (bf16[1,2,2304]{2,1,0:T(2,128)(2,1)S(1)}, bf16[1,2,2304]{2,1,0:T(2,128)(2,1)S(1)}, u32[]{:S(2)}, u32[]{:S(2)}) collective-permute-start(bf16[1,2,2304]{2,1,0:T(2,128)(2,1)S(1)} %get-tuple-element.166), channel_id=1, source_target_pairs={{1,0},{3,2},{5,4},{7,6},{9,8},{11,10},{13,12},{15,14},{17,16},{19,... | collective-permute-start | bytes 27656 | tf_op jit(solution)/shard_map/ppermute | solution.py:23
  630.3 180.6 %all-gather.33.cloned.1.call-start = ((), (), s32[]{:S(2)}) async-start(), calls=%async_computation.14 | async-start | bytes 2359296 | tf_op jit(solution)/shard_map/all_gather | solution.py:190
  698.1 14.6 collective-permute-start.6
  699.4 13.3 collective-permute-start.7
  716.7 186.2 %all-gather.47.cloned.1.call-start = ((), (), s32[]{:S(2)}) async-start(), calls=%async_computation.33 | async-start | bytes 1216512 | tf_op jit(solution)/shard_map/all_gather | solution.py:159
  717.2 189.6 %all-gather.49.cloned.1.call-start = ((), (), s32[]{:S(2)}) async-start(), calls=%async_computation.34 | async-start | bytes 9732096 | tf_op jit(solution)/shard_map/all_gather | solution.py:161
  718.0 234.7 %all-gather.51.cloned.1.call-start = ((), (), s32[]{:S(2)}) async-start(), calls=%async_computation.35 | async-start | bytes 4866048 | tf_op jit(solution)/shard_map/all_gather | solution.py:162
  718.6 465.5 %reduce-scatter.17.cloned.1.call-start = ((), (), s32[]{:S(2)}) async-start(), calls=%async_computation.16 | async-start | bytes 2359296 | tf_op jit(solution)/shard_map/reduce_scatter | solution.py:283
  1109.0 99.4 %reduce-scatter.19.cloned.1.call-start = ((), (), s32[]{:S(2)}) async-start(), calls=%async_computation.17 | async-start | bytes 2359296 | tf_op jit(solution)/shard_map/reduce_scatter | solution.py:286
  1183.6 309.3 %reduce-scatter.21.cloned.1.call-start = ((), (), s32[]{:S(2)}) async-start(), calls=%async_computation.18 | async-start | bytes 2359296 | tf_op jit(solution)/shard_map/reduce_scatter | solution.py:283
  1190.3 19.5 collective-permute-start.9
  1399.5 111.3 %reduce-scatter.23.cloned.1.call-start = ((), (), s32[]{:S(2)}) async-start(), calls=%async_computation.19 | async-start | bytes 2359296 | tf_op jit(solution)/shard_map/reduce_scatter | solution.py:286
  1474.1 150.9 %reduce-scatter.31.cloned.1.call-start = ((), (), s32[]{:S(2)}) async-start(), calls=%async_computation.23 | async-start | bytes 2433024 | tf_op jit(solution)/shard_map/reduce_scatter | solution.py:308
  1478.2 230.2 %reduce-scatter.29.cloned.1.call-start = ((), (), s32[]{:S(2)}) async-start(), calls=%async_computation.22 | async-start | bytes 2433024 | tf_op jit(solution)/shard_map/reduce_scatter | solution.py:308
  1492.8 349.4 %all-reduce.60.cloned.1.call-start = ((), (), s32[]{:S(2)}) async-start(), calls=%async_computation.36 | async-start | bytes 425984
  1536.8 9.6 collective-permute-start.14
  1540.8 5.6 collective-permute-start.15
  1554.1 428.7 %reduce-scatter.39.cloned.1.call-start = ((), (), s32[]{:S(2)}) async-start(), calls=%async_computation.27 | async-start | bytes 9732096 | tf_op jit(solution)/shard_map/reduce_scatter | solution.py:311
  1562.8 561.6 %reduce-scatter.37.cloned.1.call-start = ((), (), s32[]{:S(2)}) async-start(), calls=%async_computation.26 | async-start | bytes 9732096 | tf_op jit(solution)/shard_map/reduce_scatter | solution.py:311
  1572.4 676.2 %reduce-scatter.27.cloned.1.call-start = ((), (), s32[]{:S(2)}) async-start(), calls=%async_computation.21 | async-start | bytes 7299072 | tf_op jit(solution)/shard_map/reduce_scatter | solution.py:305
  1580.5 793.1 %reduce-scatter.25.cloned.1.call-start = ((), (), s32[]{:S(2)}) async-start(), calls=%async_computation.20 | async-start | bytes 7299072 | tf_op jit(solution)/shard_map/reduce_scatter | solution.py:305
  1587.4 998.9 %reduce-scatter.35.cloned.1.call-start = ((), (), s32[]{:S(2)}) async-start(), calls=%async_computation.25 | async-start | bytes 19464192 | tf_op jit(solution)/shard_map/reduce_scatter | solution.py:310
  1602.7 1195.8 %reduce-scatter.33.cloned.1.call-start = ((), (), s32[]{:S(2)}) async-start(), calls=%async_computation.24 | async-start | bytes 19464192 | tf_op jit(solution)/shard_map/reduce_scatter | solution.py:310
  (243 other events, 7776.8 us)
Sparse Core Ops, SparseCore 0:
  11.5 65.6 all-gather.36
  182.0 29.5 all-gather.30
  273.9 34.8 all-gather.28
  312.1 54.7 all-gather.38
  370.2 80.8 all-gather.40
  453.9 62.3 all-gather.42
  519.2 58.9 all-gather.44
  630.4 29.1 all-gather.34
  716.8 28.3 all-gather.32
  748.0 54.5 all-gather.46
  806.1 80.9 all-gather.48
  890.4 62.2 all-gather.50
  1109.1 24.4 reduce-scatter.16
  1183.7 24.5 reduce-scatter.18
  1399.6 27.5 reduce-scatter.20
  1474.2 27.4 reduce-scatter.22
  1506.8 97.4 reduce-scatter.30
  1610.3 97.9 reduce-scatter.28
  1715.9 126.2 all-reduce.59
  1847.9 134.8 reduce-scatter.38
  1989.7 134.5 reduce-scatter.36
  2130.0 118.5 reduce-scatter.26
  2255.2 118.3 reduce-scatter.24
  2379.9 206.4 reduce-scatter.34
  2592.7 205.6 reduce-scatter.32
where the time goes:
time: 2820 us; the launch traced here: 2810 us
  waiting for transfers between devices  1230 us (44%)
  matrix products  936 us (33%)
  blocking collectives  321 us (11%)
  local copies, waits for them, and re-layouts  151 us (5%)
  other arithmetic  114 us (4%)
  starting transfers between devices  33 us (1%)
    reduce_scatter x2, waiting for transfers between devices, shards(): lax.psum_scatter(d_gate_up, ('dp', 'seq'), scatter_dimension=0, tiled=True)  423 us
    reduce_scatter x2, waiting for transfers between devices, shards(): lax.psum_scatter(d_down, ('dp', 'seq'), scatter_dimension=0, tiled=True)  277 us
    reduce_scatter x2, waiting for transfers between devices, shards(): lax.psum_scatter(d_in, ('dp', 'seq'), scatter_dimension=0, tiled=True)  247 us
    dot_general x8, matrix products, spectral(): jnp.einsum('kt,btc->bkc', cos_fwd, part, precision=transform_precision)  192 us
    dot_general x8, matrix products, spectral(): jnp.einsum('kt,btc->bkc', sin_fwd, part, precision=transform_precision)  189 us
    all_gather x2, blocking collectives, shards(): lax.all_gather(short_taps[layer_index], ('dp', 'seq'), axis=1, tiled=True)  146 us
    all_gather x2, blocking collectives, shards(): lax.all_gather(cond_taps[layer_index], ('dp', 'seq'), axis=1, tiled=True)  134 us
    unnamed x26, waiting for transfers between devices  132 us
  transfers between devices with their start and end apart: 41, of which 16 were waited for; matrix products, arithmetic and copies ran while one was open for 29% of the time, Pallas kernels for 0%

commit v1 on v0

v1 whole, which is shorter than its diff:
```python
import functools
import math

import numpy as np
import jax
import jax.numpy as jnp
from jax import lax
from jax.experimental import pallas as pl
from jax.experimental.pallas import tpu as pltpu
from jax.sharding import PartitionSpec as P

BF = jnp.bfloat16
F32 = jnp.float32
EPS = 1e-05
AXES = ("dp", "seq")
GAP = 128
VMEM_LIMIT = 60 * 2**20
STRIP = 128
CHUNK = 64


def transform_matrix(length):
    half = length - GAP
    freq = np.arange(half)[:, None]
    place = np.arange(length)[None, :]
    angle = ((2 * freq + 1) * place % (4 * half)).astype(np.float64) * (math.pi / (2 * half))
    both = np.stack([np.cos(angle), -np.sin(angle)])
    both = both.reshape(2, half // 128, 128, length).transpose(1, 0, 2, 3)
    return both.reshape(2 * half, length).astype(np.float32)


def decay_table(length, features):
    channels = jnp.arange(features).astype(F32)
    positions = jnp.arange(length).astype(F32)
    rates = jnp.exp(math.log(1.0 / length) + channels / (features - 1) * math.log(4.0))
    scales = lax.rsqrt(jnp.sum(jnp.exp(-2.0 * positions[:, None] * rates[None, :]), axis=0))
    return jnp.exp(-positions[:, None] * rates[None, :]) * scales[None, :]


def dot(a, b, dims=((1,), (0,))):
    return lax.dot_general(a, b, (dims, ((), ())), preferred_element_type=F32)


def tap_same(row0, split):
    t = row0 + lax.broadcasted_iota(jnp.int32, (CHUNK, STRIP), 0)
    here = t >= split
    return [
        None if off == 2 else jnp.where(((t + (off - 2)) >= split) == here, 1.0, 0.0)
        for off in range(5)
    ]


def shifted(ref, row0, cols, same):
    block = ref[pl.ds(row0, CHUNK + 16), cols]
    out = []
    for off in range(5):
        turned = pltpu.roll(block, (2 - off) % (CHUNK + 16), 0) if off != 2 else block
        rows = turned[8 : 8 + CHUNK]
        out.append(rows if same[off] is None else rows * same[off])
    return out


def clear_ends(ref, length):
    ref[0:8, :] = jnp.zeros((8, ref.shape[1]), F32)
    ref[8 + length : 16 + length, :] = jnp.zeros((8, ref.shape[1]), F32)


def mixer_forward_kernel(
    split_ref, br_ref, sw_ref, cw_ref, decay_ref, fwd_ref, inv_ref,
    gated_ref, q_ref, key_ref, conv_ref, fh_ref, uh_ref,
    pad, kpad, filt, u, prod,
):
    length, width = q_ref.shape
    half = length - GAP
    split = split_ref[0]
    strips = width // STRIP
    clear_ends(pad, length)
    clear_ends(kpad, length)
    pad[pl.ds(8, length), :] = br_ref[...].astype(F32)

    @pl.loop(0, length // CHUNK)
    def _(i):
        row0 = pl.multiple_of(i * CHUNK, CHUNK)
        rows = pl.ds(row0, CHUNK)
        same = tap_same(row0, split)
        first = row0 + lax.broadcasted_iota(jnp.int32, (CHUNK, STRIP), 0) < split
        for part in range(3):
            for strip in range(strips):
                cols = pl.ds(part * width + strip * STRIP, STRIP)
                own = pl.ds(strip * STRIP, STRIP)
                total = None
                for off, x in enumerate(shifted(pad, row0, cols, same)):
                    term = x * sw_ref[off : off + 1, cols]
                    total = term if total is None else total + term
                low = total.astype(BF)
                if part == 0:
                    q_ref[rows, own] = low
                elif part == 1:
                    key_ref[rows, own] = low
                    kpad[pl.ds(row0 + 8, CHUNK), own] = low.astype(F32)
                else:
                    low = low.astype(F32)
                    u[0, rows, own] = jnp.where(first, low, 0.0).astype(BF)
                    u[1, rows, own] = jnp.where(first, 0.0, low).astype(BF)

    @pl.loop(0, length // CHUNK)
    def _(i):
        row0 = pl.multiple_of(i * CHUNK, CHUNK)
        rows = pl.ds(row0, CHUNK)
        same = tap_same(row0, split)
        for strip in range(strips):
            cols = pl.ds(strip * STRIP, STRIP)
            total = None
            for off, x in enumerate(shifted(kpad, row0, cols, same)):
                term = x * cw_ref[off : off + 1, cols]
                total = term if total is None else total + term
            filt[rows, cols] = (total * decay_ref[rows, cols]).astype(BF)

    scale = 1.0 / half

    @pl.loop(0, half // 128)
    def _(i):
        rows = pl.ds(pl.multiple_of(i * 256, 256), 256)
        f = dot(fwd_ref[rows, pl.ds(0, half)], filt[pl.ds(0, half), :])
        fr, fi = f[:128], f[128:]
        fh_ref[rows, :] = f.astype(BF)
        for m in range(2):
            s = dot(fwd_ref[rows, :], u[m])
            uh_ref[m, rows, :] = s.astype(BF)
            sr, si = s[:128], s[128:]
            prod[m, rows, :] = jnp.concatenate(
                [(fr * sr - fi * si) * scale, (fr * si + fi * sr) * scale], axis=0
            ).astype(BF)

    corner = split // 256

    @pl.loop(0, length // 256)
    def _(i):
        rows = pl.ds(pl.multiple_of(i * 256, 256), 256)
        pick = (i > corner).astype(jnp.int32)
        conv_ref[rows, :] = dot(inv_ref[rows, :], prod[pick]).astype(BF)

        @pl.when(i == corner)
        def _():
            later = i * 256 + lax.broadcasted_iota(jnp.int32, (256, width), 0) >= split
            other = dot(inv_ref[rows, :], prod[1])
            conv_ref[rows, :] = jnp.where(later, other, conv_ref[rows, :].astype(F32)).astype(BF)

        gated_ref[rows, :] = (q_ref[rows, :].astype(F32) * conv_ref[rows, :].astype(F32)).astype(BF)


def mixer_backward_kernel(
    split_ref, mid_ref, ow_ref, br_ref, sw_ref, cw_ref, decay_ref, fwd_ref, inv_ref,
    q_ref, key_ref, conv_ref, fh_ref, uh_ref,
    dbr_ref, dsw_ref, dcw_ref,
    pad, epad, kpad, g, prod,
):
    length, width = q_ref.shape
    half = length - GAP
    split = split_ref[0]
    strips = width // STRIP
    clear_ends(pad, length)
    clear_ends(epad, length)
    clear_ends(kpad, length)
    kpad[pl.ds(8, length), :] = key_ref[...].astype(F32)

    @pl.loop(0, length // 256)
    def _(i):
        row0 = pl.multiple_of(i * 256, 256)
        rows = pl.ds(row0, 256)
        dg = dot(mid_ref[rows, :], ow_ref[...], ((1,), (1,)))
        first = row0 + lax.broadcasted_iota(jnp.int32, (256, width), 0) < split
        pad[pl.ds(row0 + 8, 256), pl.ds(0, width)] = dg * conv_ref[rows, :].astype(F32)
        dc = dg * q_ref[rows, :].astype(F32)
        g[0, rows, :] = jnp.where(first, dc, 0.0).astype(BF)
        g[1, rows, :] = jnp.where(first, 0.0, dc).astype(BF)

    scale = 1.0 / half

    @pl.loop(0, half // 128)
    def _(i):
        rows = pl.ds(pl.multiple_of(i * 256, 256), 256)
        f = fh_ref[rows, :].astype(F32)
        fr, fi = f[:128], f[128:]
        er = None
        for m in range(2):
            s = dot(fwd_ref[rows, :], g[m])
            sr, si = s[:128], s[128:]
            prod[m, rows, :] = jnp.concatenate(
                [(fr * sr + fi * si) * scale, (fr * si - fi * sr) * scale], axis=0
            ).astype(BF)
            w = uh_ref[m, rows, :].astype(F32)
            wr, wi = w[:128], w[128:]
            tr = wr * sr + wi * si
            ti = wr * si - wi * sr
            er, ei = (tr, ti) if er is None else (er + tr, ei + ti)
        prod[2, rows, :] = jnp.concatenate([er * scale, ei * scale], axis=0).astype(BF)

    corner = split // 256
    value_cols = pl.ds(2 * width, width)

    @pl.loop(0, length // 256)
    def _(i):
        row0 = pl.multiple_of(i * 256, 256)
        rows = pl.ds(row0, 256)
        spot = pl.ds(row0 + 8, 256)
        pick = (i > corner).astype(jnp.int32)
        pad[spot, value_cols] = dot(inv_ref[rows, :], prod[pick])

        @pl.when(i == corner)
        def _():
            later = i * 256 + lax.broadcasted_iota(jnp.int32, (256, width), 0) >= split
            other = dot(inv_ref[rows, :], prod[1])
            pad[spot, value_cols] = jnp.where(later, other, pad[spot, value_cols])

        inside = row0 + lax.broadcasted_iota(jnp.int32, (256, width), 0) < half
        d_filt = dot(inv_ref[rows, :], prod[2])
        epad[spot, :] = jnp.where(inside, d_filt, 0.0) * decay_ref[rows, :]

    dsw_ref[...] = jnp.zeros(dsw_ref.shape, F32)
    dcw_ref[...] = jnp.zeros(dcw_ref.shape, F32)

    @pl.loop(0, length // CHUNK)
    def _(i):
        row0 = pl.multiple_of(i * CHUNK, CHUNK)
        spot = pl.ds(row0 + 8, CHUNK)
        same = tap_same(row0, split)
        for strip in range(strips):
            cols = pl.ds(strip * STRIP, STRIP)
            e = epad[spot, cols]
            total = None
            for off, x in enumerate(shifted(epad, row0, cols, same)):
                term = x * cw_ref[4 - off : 5 - off, cols]
                total = term if total is None else total + term
            pad[spot, pl.ds(width + strip * STRIP, STRIP)] = total
            for off, x in enumerate(shifted(kpad, row0, cols, same)):
                dcw_ref[pl.ds(off * 8, 8), cols] += (x * e).reshape(CHUNK // 8, 8, STRIP).sum(0)

    @pl.loop(0, 3 * strips)
    def _(strip):
        cols = pl.ds(pl.multiple_of(strip * STRIP, STRIP), STRIP)
        kpad[pl.ds(8, length), pl.ds(0, STRIP)] = br_ref[:, cols].astype(F32)

        @pl.loop(0, length // CHUNK)
        def _(i):
            row0 = pl.multiple_of(i * CHUNK, CHUNK)
            same = tap_same(row0, split)
            e = pad[pl.ds(row0 + 8, CHUNK), cols]
            total = None
            for off, x in enumerate(shifted(pad, row0, cols, same)):
                term = x * sw_ref[4 - off : 5 - off, cols]
                total = term if total is None else total + term
            dbr_ref[pl.ds(row0, CHUNK), cols] = total.astype(BF)
            for off, x in enumerate(shifted(kpad, row0, pl.ds(0, STRIP), same)):
                dsw_ref[pl.ds(off * 8, 8), cols] += (x * e).reshape(CHUNK // 8, 8, STRIP).sum(0)


def local_call(kernel, outs, scratch, n_in):
    vmem = pl.BlockSpec(memory_space=pltpu.VMEM)
    return pl.pallas_call(
        kernel,
        out_shape=[jax.ShapeDtypeStruct(shape, dtype) for shape, dtype in outs],
        in_specs=[pl.BlockSpec(memory_space=pltpu.SMEM)] + [vmem] * (n_in - 1),
        out_specs=[vmem] * len(outs),
        scratch_shapes=[pltpu.VMEM(shape, dtype) for shape, dtype in scratch],
        compiler_params=pltpu.CompilerParams(vmem_limit_bytes=VMEM_LIMIT),
    )


def mixer_forward(split, branches, sw, cw, decay, fwd, inv):
    length, width = decay.shape
    bins = fwd.shape[0]
    tall = (length, width)
    return local_call(
        mixer_forward_kernel,
        [(tall, BF)] * 4 + [((bins, width), BF), ((2, bins, width), BF)],
        [
            ((length + 16, 3 * width), F32),
            ((length + 16, width), F32),
            (tall, BF),
            ((2,) + tall, BF),
            ((2, bins, width), BF),
        ],
        7,
    )(split, branches, sw, cw, decay, fwd, inv)


def mixer_backward(split, mid, ow, branches, sw, cw, decay, fwd, inv, q, key, conv, fh, uh):
    length, width = decay.shape
    bins = fwd.shape[0]
    dbr, dsw, dcw = local_call(
        mixer_backward_kernel,
        [((length, 3 * width), BF), ((40, 3 * width), F32), ((40, width), F32)],
        [
            ((length + 16, 3 * width), F32),
            ((length + 16, width), F32),
            ((length + 16, width), F32),
            ((2, length, width), BF),
            ((3, bins, width), BF),
        ],
        14,
    )(split, mid, ow, branches, sw, cw, decay, fwd, inv, q, key, conv, fh, uh)
    return dbr, dsw.reshape(5, 8, -1).sum(1), dcw.reshape(5, 8, -1).sum(1)


def cube(dp_count):
    bits = (dp_count // 2).bit_length() - 1
    core, seq = bits, bits + 1
    last, rest = [bits - 1], list(range(bits - 1))
    return bits, core, seq, (rest + [seq] + last, rest + last + [seq], last + [seq] + rest)


def place(bits):
    dp, seq = lax.axis_index("dp"), lax.axis_index("seq")
    coords = [(dp // (2 << (bits - 1 - d))) % 2 for d in range(bits)] + [dp % 2, seq]

    def neighbour(d):
        if d == bits + 1:
            return dp, 1 - seq
        step = 1 if d == bits else 2 << (bits - 1 - d)
        return dp + step * (1 - 2 * coords[d]), seq

    return coords, neighbour


def region(fixed, dims):
    return tuple(fixed[d] if d in fixed else slice(None) for d in range(dims))


def greet(neighbours):
    barrier = pltpu.get_barrier_semaphore()
    for device in neighbours:
        pl.semaphore_signal(barrier, inc=1, device_id=device, device_id_type=pl.DeviceIdType.MESH)
    pl.semaphore_wait(barrier, len(neighbours))


def remote(src, dst, send, recv, device):
    copy = pltpu.make_async_remote_copy(
        src_ref=src, dst_ref=dst, send_sem=send, recv_sem=recv,
        device_id=device, device_id_type=pl.DeviceIdType.MESH,
    )
    copy.start()
    return copy


UNITS = ((0, 0), (0, 1), (1, 0), (2, 0))
ORDERS = (0, 1, 2, 0)


def piece_of(shape, unit):
    array, piece = UNITS[unit]
    cols = shape[-1] // 2 if array == 0 else shape[-1]
    return tuple(slice(None) for _ in shape[:-1]) + (pl.ds(piece * cols, cols),), cols


def gather_kernel(dp_count, own, full, sems):
    bits, core_dim, seq_dim, orders = cube(dp_count)
    dims = bits + 2
    coords, neighbour = place(bits)
    core = coords[core_dim]
    sibling = neighbour(core_dim)
    greet([neighbour(d) for d in range(dims)])
    ici_send, ici_recv, core_send, core_recv, local = sems
    mine = region({d: coords[d] for d in range(dims)}, dims)
    everything = slice(None)
    waits = []
    ready = []
    for u, (array, _) in enumerate(UNITS):
        tail, _ = piece_of(own[array].shape[1:], u)
        here = full[array].at[(everything,) + mine + tail]
        start = pltpu.make_async_copy(own[array].at[(everything,) + tail], here, local.at[u])
        start.start()
        first = remote(own[array].at[(everything,) + tail], here, core_send.at[u, 0], core_recv.at[u, 0], sibling)
        ready.append((start, first))
        waits.append(first)
    stages = dims - 1
    last = [None] * len(UNITS)
    for t in range(stages + 1):
        for u, (array, _) in enumerate(UNITS):
            tail, _ = piece_of(own[array].shape[1:], u)
            order = orders[ORDERS[u]]
            if t == 0:
                ready[u][0].wait()
                ready[u][1].wait_recv()
            else:
                last[u].wait_recv()
                d = order[t - 1]
                fixed = {e: coords[e] for e in order[t:]}
                fixed[d] = 1 - coords[d]
                got = full[array].at[(core,) + region(fixed, dims) + tail]
                waits.append(remote(got, got, core_send.at[u, t], core_recv.at[u, t], sibling))
            if t < stages:
                fixed = {e: coords[e] for e in order[t:]}
                held = full[array].at[(core,) + region(fixed, dims) + tail]
                last[u] = remote(held, held, ici_send.at[u, t], ici_recv.at[u, t], neighbour(order[t]))
                ready.append(last[u])
    for copy in waits[: len(UNITS)]:
        copy.wait_send()
    for copy in waits[len(UNITS) :]:
        copy.wait()
    for copy in ready[len(UNITS) :]:
        copy.wait_send()


def gather_weights(own, dp_count, number):
    bits, _, _, _ = cube(dp_count)
    stages = bits + 1
    units = len(UNITS)

    def body(*refs):
        gather_kernel(dp_count, refs[:3], refs[3:6], refs[6:])

    grid = (2,) * (bits + 2)
    anywhere = pl.BlockSpec(memory_space=pl.ANY)
    return pl.pallas_call(
        body,
        out_shape=[jax.ShapeDtypeStruct(x.shape[:1] + grid + x.shape[1:], x.dtype) for x in own],
        in_specs=[anywhere] * 3,
        out_specs=[anywhere] * 3,
        scratch_shapes=[pltpu.SemaphoreType.DMA((units, stages))] * 2
        + [pltpu.SemaphoreType.DMA((units, stages + 1))] * 2
        + [pltpu.SemaphoreType.DMA((units,))],
        compiler_params=pltpu.CompilerParams(collective_id=number, has_side_effects=True),
    )(*own)


def scatter_kernel(dp_count, grads, outs, held, first, arrived, final, sems):
    bits, core_dim, seq_dim, orders = cube(dp_count)
    dims = bits + 2
    stages = dims - 1
    coords, neighbour = place(bits)
    core = coords[core_dim]
    sibling = neighbour(core_dim)
    greet([neighbour(d) for d in range(dims)])
    ici_send, ici_recv, core_send, core_recv, local = sems
    everything = region({}, dims)

    def add(u, fixed, extra, free):
        count = 2 ** len(free)

        @pl.loop(0, count)
        def _(i):
            at = {d: (i // 2 ** (len(free) - 1 - j)) % 2 for j, d in enumerate(free)}
            index = tuple(at[d] if d in at else fixed[d] for d in range(dims))
            held[u][index] += extra[tuple(at[d] for d in free)]

    starts = []
    for u, (array, _) in enumerate(UNITS):
        tail, _ = piece_of(grads[array].shape[1 + dims :], u)
        load = pltpu.make_async_copy(grads[array].at[(core,) + everything + tail], held[u], local.at[u, 0])
        load.start()
        starts.append((
            load,
            remote(grads[array].at[(1 - core,) + everything + tail], first[u], core_send.at[u, 0], core_recv.at[u, 0], sibling),
        ))
    copies = []
    last = [None] * len(UNITS)
    for t in range(stages + 1):
        for u, (array, _) in enumerate(UNITS):
            order = orders[ORDERS[u]][::-1]
            if t == 0:
                starts[u][0].wait()
                starts[u][1].wait_recv()
                add(u, {}, first[u], list(range(dims)))
            else:
                last[u].wait_recv()
                fixed = {d: coords[d] for d in order[:t]}
                add(u, fixed, arrived[u][t - 1], [d for d in range(dims) if d not in fixed])
            fixed = {d: coords[d] for d in order[:t]}
            if t < stages:
                fixed[order[t]] = 1 - coords[order[t]]
                last[u] = remote(
                    held[u].at[region(fixed, dims)], arrived[u][t], ici_send.at[u, t], ici_recv.at[u, t], neighbour(order[t])
                )
                copies.append(last[u])
            else:
                fixed[core_dim] = 1 - core
                last[u] = remote(held[u].at[region(fixed, dims)], final[u], core_send.at[u, 1], core_recv.at[u, 1], sibling)
    ends = []
    for u, (array, _) in enumerate(UNITS):
        tail, _ = piece_of(grads[array].shape[1 + dims :], u)
        mine = region({d: coords[d] for d in range(dims)}, dims)
        own = pltpu.make_async_copy(held[u].at[mine], outs[array].at[(core,) + tail], local.at[u, 1])
        own.start()
        last[u].wait_recv()
        other = pltpu.make_async_copy(final[u], outs[array].at[(1 - core,) + tail], local.at[u, 2])
        other.start()
        ends += [own, other]
    for copy in ends:
        copy.wait()
    for copy in copies + last + [s[1] for s in starts]:
        copy.wait_send()


def scatter_grads(grads, dp_count, number):
    bits, _, _, orders = cube(dp_count)
    dims = bits + 2
    stages = dims - 1
    units = len(UNITS)
    grid = (2,) * dims
    slabs = []
    for u, (array, _) in enumerate(UNITS):
        shape = grads[array].shape[1 + dims :]
        _, cols = piece_of(shape, u)
        slabs.append(shape[:-1] + (cols,))

    def body(*refs):
        grads_in, outs, refs = refs[:3], refs[3:6], refs[6:]
        held, first, final, refs = refs[:units], refs[units : 2 * units], refs[2 * units : 3 * units], refs[3 * units :]
        arrived = [refs[u * stages : (u + 1) * stages] for u in range(units)]
        scatter_kernel(dp_count, grads_in, outs, held, first, arrived, final, refs[units * stages :])

    anywhere = pl.BlockSpec(memory_space=pl.ANY)
    return pl.pallas_call(
        body,
        out_shape=[jax.ShapeDtypeStruct(x.shape[:1] + x.shape[1 + dims :], x.dtype) for x in grads],
        in_specs=[anywhere] * 3,
        out_specs=[anywhere] * 3,
        scratch_shapes=[pltpu.VMEM(grid + slab, BF) for slab in slabs] * 2
        + [pltpu.VMEM(slab, BF) for slab in slabs]
        + [pltpu.VMEM((2,) * (dims - 1 - t) + slab, BF) for slab in slabs for t in range(stages)]
        + [pltpu.SemaphoreType.DMA((units, stages))] * 2
        + [pltpu.SemaphoreType.DMA((units, 2))] * 2
        + [pltpu.SemaphoreType.DMA((units, 3))],
        compiler_params=pltpu.CompilerParams(
            collective_id=number, has_side_effects=True, vmem_limit_bytes=VMEM_LIMIT
        ),
    )(*grads)


def norm_parts(x):
    center = x - jnp.mean(x, axis=-1, keepdims=True)
    r = lax.rsqrt(jnp.mean(center * center, axis=-1, keepdims=True) + EPS)
    return center * r, r


def norm_back(x, gain, d):
    xhat, r = norm_parts(x)
    h = d * gain
    dx = r * (h - jnp.mean(h, axis=-1, keepdims=True) - xhat * jnp.mean(h * xhat, axis=-1, keepdims=True))
    return dx, jnp.sum(d * xhat, axis=0)


def gate_value(pre):
    return jax.nn.gelu(pre[0], approximate=True) * pre[1]


def shards(
    tokens, split_points, cotangent, norm_gain, in_weight, short_taps, cond_taps,
    out_weight, mlp_gain, gate_up, down_weight,
):
    rows, features = tokens.shape[1:]
    dp_count, seq_count = lax.axis_size("dp"), lax.axis_size("seq")
    devices = dp_count * seq_count
    length = rows * seq_count
    width = features // 2
    layers = in_weight.shape[0]
    share = norm_gain.shape[1]
    hidden = down_weight.shape[1] * devices
    core = lax.axis_index("dp") % 2
    seq = lax.axis_index("seq")

    swap = [(4 * k + a, 4 * k + 3 - a) for k in range(devices // 4) for a in (1, 2)]
    flip = [(i, i ^ 1) for i in range(dp_count)]

    def swap_rows(x):
        return jnp.where(core == seq, x, lax.ppermute(x, AXES, swap))

    def sibling(x):
        return lax.ppermute(x, "dp", flip)

    def beside(own, other, axis):
        return jnp.where(
            core == 0,
            jnp.concatenate([own, other], axis=axis),
            jnp.concatenate([other, own], axis=axis),
        )

    def half_of(x, which, axis):
        size = x.shape[axis] // 2
        return lax.dynamic_slice_in_dim(x, which * size, size, axis)

    def own_channels(x):
        parts = x.shape[-1] // features
        x = x.reshape(x.shape[:-1] + (parts, 2, width))
        x = lax.dynamic_index_in_dim(x, core, x.ndim - 2, keepdims=False)
        return x.reshape(x.shape[:-2] + (parts * width,))

    split = swap_rows(split_points)
    stream = swap_rows(tokens).reshape(rows, features).astype(F32)
    grad = swap_rows(cotangent).reshape(rows, features).astype(F32)
    table = transform_matrix(length)
    fwd = jnp.asarray(table, BF)
    inv = jnp.asarray(np.ascontiguousarray(table.T), BF)
    decay = own_channels(decay_table(length, features))

    def halves(x):
        parts = x.shape[-1] // features
        x = x.reshape(x.shape[:-1] + (parts, 2, width))
        x = jnp.moveaxis(x, -2, 0)
        return x.reshape(x.shape[:-2] + (parts * width,))

    lane = 128
    bits = cube(dp_count)[0]
    grid = (2,) * (bits + 2)
    small_sizes = [share, 15 * share, 5 * share, share]
    small_ends = np.cumsum([0] + small_sizes)
    small_rows = share * lane

    weights = []
    gains = []
    for layer in range(layers):
        small = jnp.concatenate(
            [x[layer].reshape(-1) for x in (norm_gain, short_taps, cond_taps, mlp_gain)]
        )
        small = jnp.pad(small, (0, 2 * small_rows - small.shape[0])).reshape(2, share, lane)
        own = [
            gate_up[layer].reshape(share, 2, hidden).transpose(1, 0, 2),
            halves(down_weight[layer]).reshape(2, hidden // features, share, width),
            jnp.concatenate([halves(in_weight[layer]), halves(out_weight[layer]), small], axis=2),
        ]
        gu_w, down_w, rest = gather_weights(own, dp_count, layer)
        gu_w = gu_w.reshape(2, features, hidden)
        down_w = down_w.reshape(2, hidden, width)
        rest = rest.reshape(2, features, 4 * width + lane)
        in_w = lax.dynamic_index_in_dim(rest, core, 0, keepdims=False)[:, : 3 * width]
        out_w = jnp.concatenate([rest[0, :, 3 * width : 4 * width], rest[1, :, 3 * width : 4 * width]], axis=1)
        weights.append((in_w, out_w, gu_w, down_w))
        small = rest[:, :, 4 * width :].reshape(2, devices, small_rows).transpose(1, 0, 2)
        small = small.reshape(devices, 2 * small_rows).astype(F32)
        ng, st, ct, mg = [small[:, small_ends[i] : small_ends[i + 1]] for i in range(4)]
        st = st.reshape(devices, 5, 3 * share).transpose(1, 0, 2).reshape(5, 3 * features)
        ct = ct.reshape(devices, 5, share).transpose(1, 0, 2).reshape(5, features)
        gains.append(
            (
                ng.reshape(features),
                jnp.pad(own_channels(st), ((0, 3), (0, 0))),
                jnp.pad(own_channels(ct), ((0, 3), (0, 0))),
                mg.reshape(features),
            )
        )

    kept = []
    for layer in range(layers):
        in_w, out_w, gu_w, down_w = weights[layer]
        ng, st, ct, mg = gains[layer]
        normed = (norm_parts(stream)[0] * ng).astype(BF)
        normed_all = beside(normed, sibling(normed), 0)
        branches = dot(normed_all, in_w).astype(BF)
        gated, q, key, conv, fh, uh = mixer_forward(
            split, branches, st, ct, decay, fwd, inv
        )
        mine = half_of(gated, core, 0)
        gated_rows = beside(mine, sibling(half_of(gated, 1 - core, 0)), 1)
        middle = stream + dot(gated_rows, out_w)
        normed_mlp = (norm_parts(middle)[0] * mg).astype(BF)
        pre = jnp.stack([dot(normed_mlp, gu_w[h]).astype(BF) for h in range(2)])
        hid = gate_value(pre.astype(F32)).astype(BF)
        kept.append((stream, normed_all, branches, gated, q, key, conv, fh, uh, middle, normed_mlp, pre, hid))
        stream = middle + jnp.concatenate([dot(hid, down_w[h]) for h in range(2)], axis=1)
    activations = swap_rows(stream.astype(BF)[None])

    scattered = []
    for layer in reversed(range(layers)):
        in_w, out_w, gu_w, down_w = weights[layer]
        ng, st, ct, mg = gains[layer]
        x, normed_all, branches, gated, q, key, conv, fh, uh, middle, normed_mlp, pre, hid = kept[layer]
        g_low = grad.astype(BF)
        g_half = [g_low[:, :width], g_low[:, width:]]
        d_down = jnp.stack([dot(hid, x, ((0,), (0,))).astype(BF) for x in g_half])
        d_hidden = sum(dot(x, w, ((1,), (1,))) for x, w in zip(g_half, down_w))
        (d_pre,) = jax.vjp(gate_value, pre.astype(F32))[1](d_hidden)
        d_pre = d_pre.astype(BF)
        d_gu = jnp.stack([dot(normed_mlp, d_pre[h], ((0,), (0,))).astype(BF) for h in range(2)])
        d_normed_mlp = sum(dot(d_pre[h], gu_w[h], ((1,), (1,))) for h in range(2))
        d_part, d_mg = norm_back(middle, mg, d_normed_mlp)
        d_middle = grad + d_part
        m_low = d_middle.astype(BF)
        m_all = beside(m_low, sibling(m_low), 0)
        d_branches, d_st, d_ct = mixer_backward(
            split, m_all, half_of(out_w, core, 0), branches, st, ct, decay, fwd, inv,
            q, key, conv, fh, uh,
        )
        d_out = dot(gated, m_all, ((0,), (0,)))
        d_in = dot(normed_all, d_branches, ((0,), (0,)))
        d_normed_all = dot(d_branches, in_w, ((1,), (1,)))
        d_normed = half_of(d_normed_all, core, 0) + sibling(half_of(d_normed_all, 1 - core, 0))
        d_part, d_ng = norm_back(x, ng, d_normed)
        grad = d_middle + d_part

        def spread(x, axis):
            return beside(x, jnp.zeros_like(x), axis)

        d_st = spread(d_st.reshape(5, 3, width), 2).reshape(5, 3 * features)
        d_ct = spread(d_ct, 1)
        d_st = d_st.reshape(5, devices, 3 * share).transpose(1, 0, 2).reshape(devices, -1)
        d_ct = d_ct.reshape(5, devices, share).transpose(1, 0, 2).reshape(devices, -1)
        small = jnp.concatenate([d_ng.reshape(devices, share), d_st, d_ct, d_mg.reshape(devices, share)], axis=1)
        small = jnp.pad(small, ((0, 0), (0, 2 * small_rows - small.shape[1]))).astype(BF)
        small = small.reshape(devices, 2, share, lane).transpose(1, 0, 2, 3).reshape(2, features, lane)
        d_in = spread(d_in.astype(BF)[None], 0)
        d_out = spread(halves(d_out.astype(BF)), 1)
        rest = jnp.concatenate([d_in, d_out, small], axis=2)
        pieces = [
            d_gu.reshape((2,) + grid + (share, hidden)),
            d_down.reshape((2,) + grid + (hidden // features, share, width)),
            rest.reshape((2,) + grid + (share, 4 * width + lane)),
        ]
        scattered.append(scatter_grads(pieces, dp_count, layers + layer))
    token_grad = swap_rows(grad[None])

    def joined(x):
        parts = x.shape[-1] // width
        x = jnp.moveaxis(x.reshape(x.shape[:-1] + (parts, width)), 0, -2)
        return x.reshape(x.shape[:-3] + (parts * features,))

    results = []
    for s_gu, s_down, s_rest in scattered[::-1]:
        small = s_rest[:, :, 4 * width :].reshape(-1)
        results.append(
            [small[small_ends[i] : small_ends[i + 1]] for i in range(4)]
            + [
                joined(s_rest[:, :, : 3 * width]),
                joined(s_rest[:, :, 3 * width : 4 * width]),
                s_gu.transpose(1, 0, 2).reshape(share, 2 * hidden),
                joined(s_down.reshape(2, -1, width)),
            ]
        )
    g_ng, g_st, g_ct, g_mg, g_in, g_out, g_gu, g_down = [jnp.stack(x).astype(F32) for x in zip(*results)]
    return (
        activations,
        token_grad,
        g_ng,
        g_in,
        g_st.reshape(layers, 5, 3 * share),
        g_ct.reshape(layers, 5, share),
        g_out,
        g_mg,
        g_gu,
        g_down,
    )


def solution(mesh):
    every = ("dp", "seq")
    rows, part = P("dp", "seq", None), P(None, every, None)
    vector, taps = P(None, every), P(None, None, every)
    return jax.shard_map(
        shards,
        mesh=mesh,
        in_specs=(rows, P("dp"), rows, vector, part, taps, taps, part, vector, part, part),
        out_specs=(rows, rows, vector, part, taps, taps, part, vector, part, part),
        check_vma=False,
    )
```

time: 2820 us -> 948 us (0.34)
  waiting for transfers between devices: 1230 us -> 11.9 us
  matrix products: 936 us -> 150 us
  Pallas kernels: 0 us -> 551 us
  blocking collectives: 321 us -> 0 us
  local copies, waits for them, and re-layouts: 151 us -> 89.1 us
    reduce_scatter x12 -> x0, waiting for transfers between devices: 1050 us -> none  [the longest x2 423 us: shards(): lax.psum_scatter(d_gate_up, ('dp', 'seq'), scatter_dimension=0, tiled=True)]
    dot_general x64 -> x34, matrix products: 936 us -> 150 us  [dot(): return lax.dot_general(a, b, (dims, ((), ())), preferred_element_type=F32)]
    pallas_call x0 -> x8, Pallas kernels: none -> 551 us  [the longest x2 222 us: gather_weights(): pl.pallas_call(body, out_shape=[jax.ShapeDtypeStruct(x.shape[:1] + grid +...]
    all_gather x4 -> x0, blocking collectives: 280 us -> none  [the longest x2 146 us: shards(): lax.all_gather(short_taps[layer_index], ('dp', 'seq'), axis=1, tiled=True)]
    unnamed x26 -> x0, waiting for transfers between devices: 132 us -> none
    slice x20 -> x26, local copies, waits for them, and re-layouts: 106 us -> 32 us  [the longest x2 18 us: shards(): pre = jnp.stack([dot(normed_mlp, gu_w[h]).astype(BF) for h in range(2)])]
    all_gather x12 -> x0, waiting for transfers between devices: 46 us -> none  [the longest x2 33.8 us: shards(): lax.all_gather(down_weight[layer_index], ('dp', 'seq'), axis=0, tiled=True)]
    unnamed x1 -> x0, blocking collectives: 41.4 us -> none
  transfers between devices with their start and end apart: 41 -> 13, of which waited for: 16 -> 1; matrix products, arithmetic and copies ran while one was open for 29% -> 17% of each run, Pallas kernels for 0% -> 30%
where the time goes in v1:
time: 948 us; the launch traced here: 937 us
  Pallas kernels  551 us (58%)
  matrix products  150 us (16%)
  other arithmetic  114 us (12%)
  local copies, waits for them, and re-layouts  89.1 us (9%)
  starting transfers between devices  17 us (2%)
  waiting for transfers between devices  11.9 us (1%)
    pallas_call x2, Pallas kernels, gather_weights(): pl.pallas_call(body, out_shape=[jax.ShapeDtypeStruct(x.shape[:1] + grid +...  222 us
    pallas_call x2, Pallas kernels, scatter_grads(): pl.pallas_call(body, out_shape=[jax.ShapeDtypeStruct(x.shape[:1] + x.shap...  212 us
    dot_general x34, matrix products, dot(): return lax.dot_general(a, b, (dims, ((), ())), preferred_element_type=F32)  150 us
    pallas_call x2, Pallas kernels, mixer_backward(): local_call(mixer_backward_kernel, [((length, 3 * width), BF), ((40, 3 * w...  70.4 us
    pallas_call x2, Pallas kernels, mixer_forward(): local_call(mixer_forward_kernel, [(tall, BF)] * 4 + [((bins, width), BF),...  47.2 us
  transfers between devices with their start and end apart: 13, of which 1 were waited for; matrix products, arithmetic and copies ran while one was open for 17% of the time, Pallas kernels for 30%

profile of v1, /device:TPU:1, one launch (start us, length us, event | category | flops | bytes accessed | tf_op | source)
XLA Modules:
  0.0 937.3 jit_solution(2613986295350492010)
XLA Ops:
  0.7 4.7 collective-permute-start.1
  21.1 110.0 %shard_map.204 = (bf16[2,2,2,2,2,2,24,3072]{7,6,5,4,3,2,1,0:T(8,128)(2,1)}, bf16[2,2,2,2,2,2,4,24,384]{8,7,6,5,4,3,2,1,0:T(8,128)(2,1)}, bf16[2,2,2,2,2,2,24,1664]{7,6,5,4,3,2,1,0:T(8,128)(2,1)}) custom-call(bf16[2,24,3072]{2,1,0:T(8,128)(2,1)} %bitcast.411, bf16[2,4,24,384]{3,2,1,0:T(8,128)(2,1)} %bitcast.419, bf16[2,24,1664]{2,1,0:T(8,128)(2,1)} %pad_maximum_fusion.10.refs_2_), custom_call_target="tpu_custom_call" | custom-call | tf_op jit(solution)/shard_map/pallas_call | solution.py:415
  138.2 111.7 %shard_map.206 = (bf16[2,2,2,2,2,2,24,3072]{7,6,5,4,3,2,1,0:T(8,128)(2,1)}, bf16[2,2,2,2,2,2,4,24,384]{8,7,6,5,4,3,2,1,0:T(8,128)(2,1)}, bf16[2,2,2,2,2,2,24,1664]{7,6,5,4,3,2,1,0:T(8,128)(2,1)}) custom-call(bf16[2,24,3072]{2,1,0:T(8,128)(2,1)} %bitcast.412, bf16[2,4,24,384]{3,2,1,0:T(8,128)(2,1)} %bitcast.420, bf16[2,24,1664]{2,1,0:T(8,128)(2,1)} %pad_maximum_fusion.11.refs_2_), custom_call_target="tpu_custom_call" | custom-call | tf_op jit(solution)/shard_map/pallas_call | solution.py:415
  270.1 9.0 fusion.147
  281.3 9.0 fusion.146
  295.7 23.5 %shard_map.205 = (bf16[1024,384]{1,0:T(8,128)(2,1)}, bf16[1024,384]{1,0:T(8,128)(2,1)}, bf16[1024,384]{1,0:T(8,128)(2,1)}, bf16[1024,384]{1,0:T(8,128)(2,1)}, bf...) custom-call(s32[1]{0:T(128)S(6)} %select_n.151.split_ref, bf16[1024,1152]{1,0:T(8,128)(2,1)} %convolution_convert_fusion.13.br_ref, ...), custom_call_target="tpu_custom_call" | custom-call | tf_op jit(solution)/shard_map/pallas_call | solution.py:274
  359.1 23.6 %shard_map.207 = (bf16[1024,384]{1,0:T(8,128)(2,1)}, bf16[1024,384]{1,0:T(8,128)(2,1)}, bf16[1024,384]{1,0:T(8,128)(2,1)}, bf16[1024,384]{1,0:T(8,128)(2,1)}, bf...) custom-call(s32[1]{0:T(128)S(6)} %select_n.151.split_ref, bf16[1024,1152]{1,0:T(8,128)(2,1)} %convolution_convert_fusion.12.br_ref, ...), custom_call_target="tpu_custom_call" | custom-call | tf_op jit(solution)/shard_map/pallas_call | solution.py:274
  384.0 6.2 fusion.118
  410.2 11.7 %multiply_bitcast_fusion.1 = (f32[1,512,3072]{2,1,0:T(8,128)}, f32[1,512,3072]{2,1,0:T(8,128)}, bf16[512,3072]{1,0:T(8,128)(2,1)}) fusion(f32[2,512,3072]{2,1,0:T(8,128)S(1)} %maximum_convert_fusion.1, f32[512,3072]{1,0:T(8,128)} %fusion.118, bf16[3072,384]{1,0:T(8,128)(2,1)} %bitcast.403, bf16[512,768]{1,0:T(8,128)(2,1)} %copy-done.15), kind=kOutput, calls=%fused_computation.59 | convolution fusion | flops 1247281152 | bytes 37355520 | tf_op jit(solution)/shard_map/dot_general | solution.py:41
  421.9 5.4 convolution_convert_fusion.8
  430.6 8.3 add_convert_fusion.1
  438.8 6.1 fusion.52
  449.3 4.6 convolution_convert_fusion.1
  458.7 4.6 fusion.144
  469.2 8.2 pad_maximum_fusion.1.refs_0_
  480.6 35.2 %shard_map.208 = (bf16[1024,1152]{1,0:T(8,128)(2,1)}, f32[40,1152]{1,0:T(8,128)}, f32[40,384]{1,0:T(8,128)}) custom-call(s32[1]{0:T(128)S(6)} %select_n.151.split_ref, bf16[1024,768]{1,0:T(8,128)(2,1)} %maximum_select_fusion.2.mid_ref, bf16[384,768]{1,0:T(8,128)(2,1)} %fusion.102.ow_ref, bf16[1024,1152]{1,0:T(8,128)(2,1)} %convolution_convert_fusion.12.br_ref, ...), custom_call_target="tpu_custom_call" | custom-call | tf_op jit(solution)/shard_map/pallas_call | solution.py:291
  515.7 4.4 fusion.73
  545.9 4.5 fusion.115
  550.4 11.5 %multiply_bitcast_fusion = (f32[1,512,3072]{2,1,0:T(8,128)}, f32[1,512,3072]{2,1,0:T(8,128)}, bf16[512,3072]{1,0:T(8,128)(2,1)}) fusion(f32[2,512,3072]{2,1,0:T(8,128)S(1)} %bitcast.356, f32[512,3072]{1,0:T(8,128)} %fusion.115, bf16[3072,384]{1,0:T(8,128)(2,1)S(1)} %bitcast.400, bf16[512,768]{1,0:T(8,128)(2,1)S(1)} %get-tuple-element.129), kind=kOutput, calls=%fused_computation.58 | convolution fusion | flops 1247281152 | bytes 37355520 | tf_op jit(solution)/shard_map/dot_general | solution.py:41
  561.9 5.3 convolution_convert_fusion.10
  570.5 5.6 add_convert_fusion
  576.1 8.4 fusion.54
  584.5 4.4 convolution_convert_fusion.2
  588.9 6.4 convolution_convert_fusion.3
  600.8 105.4 %shard_map.211 = (bf16[2,24,3072]{2,1,0:T(8,128)(2,1)}, bf16[2,4,24,384]{3,2,1,0:T(8,128)(2,1)}, bf16[2,24,1664]{2,1,0:T(8,128)(2,1)}) custom-call(bf16[2,2,2,2,2,2,24,3072]{7,6,5,4,3,2,1,0:T(8,128)(2,1)} %pad_maximum_fusion.1.refs_0_, bf16[2,2,2,2,2,2,4,24,384]{8,7,6,5,4,3,2,1,0:T(8,128)(2,1)} %pad_maximum_fusion.5.refs_1_, ...), custom_call_target="tpu_custom_call" | custom-call | tf_op jit(solution)/shard_map/pallas_call | solution.py:514
  708.7 7.8 multiply_reduce_fusion.2
  726.8 8.3 pad_maximum_fusion.refs_0_
  738.5 35.3 %shard_map.209 = (bf16[1024,1152]{1,0:T(8,128)(2,1)}, f32[40,1152]{1,0:T(8,128)}, f32[40,384]{1,0:T(8,128)}) custom-call(s32[1]{0:T(128)S(6)} %select_n.151.split_ref, bf16[1024,768]{1,0:T(8,128)(2,1)} %maximum_select_fusion.3.mid_ref, bf16[384,768]{1,0:T(8,128)(2,1)} %fusion.103.ow_ref, bf16[1024,1152]{1,0:T(8,128)(2,1)} %convolution_convert_fusion.13.br_ref, ...), custom_call_target="tpu_custom_call" | custom-call | tf_op jit(solution)/shard_map/pallas_call | solution.py:291
  783.8 5.0 fusion.50
  795.7 5.1 pad_maximum_fusion.2.refs_2_
  800.8 106.6 %shard_map.210 = (bf16[2,24,3072]{2,1,0:T(8,128)(2,1)}, bf16[2,4,24,384]{3,2,1,0:T(8,128)(2,1)}, bf16[2,24,1664]{2,1,0:T(8,128)(2,1)}) custom-call(bf16[2,2,2,2,2,2,24,3072]{7,6,5,4,3,2,1,0:T(8,128)(2,1)} %pad_maximum_fusion.refs_0_, bf16[2,2,2,2,2,2,4,24,384]{8,7,6,5,4,3,2,1,0:T(8,128)(2,1)} %pad_maximum_fusion.4.refs_1_, ...), custom_call_target="tpu_custom_call" | custom-call | tf_op jit(solution)/shard_map/pallas_call | solution.py:514
  922.3 11.8 %collective-permute-done.12 = f32[1,512,768]{2,1,0:T(8,128)} collective-permute-done((f32[1,512,768]{2,1,0:T(8,128)S(1)}, f32[1,512,768]{2,1,0:T(8,128)}, u32[]{:S(2)}, u32[]{:S(2)}) %collective-permute-start.12) | collective-permute-done | bytes 1572896 | tf_op jit(solution)/shard_map/ppermute | solution.py:567
  (470 shorter events, 215.5 us)
Async XLA Ops:
  0.6 18.7 %copy-start.49 = (bf16[2,24,6144]{2,1,0:T(8,128)(2,1)S(1)}, bf16[2,24,6144]{2,1,0:T(8,128)(2,1)}, u32[]{:S(2)}) copy-start(bf16[2,24,6144]{2,1,0:T(8,128)(2,1)} %param.22) | copy-start | bytes 1769476
  0.7 289.7 %collective-permute-start.1 = (s32[1]{0:T(128)}, s32[1]{0:T(128)}, u32[]{:S(2)}, u32[]{:S(2)}) collective-permute-start(s32[1]{0:T(128)} %param.14), channel_id=1, source_target_pairs={{1,2},{2,1},{5,6},{6,5},{9,10},{10,9},{13,14},{14,13},{17,18},{18,... | collective-permute-start | bytes 20 | tf_op jit(solution)/shard_map/ppermute | solution.py:567
  5.3 273.7 %collective-permute-start = (bf16[1,512,768]{2,1,0:T(8,128)(2,1)}, bf16[1,512,768]{2,1,0:T(8,128)(2,1)}, u32[]{:S(2)}, u32[]{:S(2)}) collective-permute-start(bf16[1,512,768]{2,1,0:T(8,128)(2,1)} %param.13), channel_id=1, source_target_pairs={{1,2},{2,1},{5,6},{6,5},{9,10},{10,9},{13,14},{14,13},{17,18},{18,... | collective-permute-start | bytes 2359304 | tf_op jit(solution)/shard_map/ppermute | solution.py:567
  7.3 346.8 %collective-permute-start.7 = (bf16[1,512,768]{2,1,0:T(8,128)(2,1)}, bf16[1,512,768]{2,1,0:T(8,128)(2,1)}, u32[]{:S(2)}, u32[]{:S(2)}) collective-permute-start(bf16[1,512,768]{2,1,0:T(8,128)(2,1)} %param.15), channel_id=1, source_target_pairs={{1,2},{2,1},{5,6},{6,5},{9,10},{10,9},{13,14},{14,13},{17,18},{18,... | collective-permute-start | bytes 2359304 | tf_op jit(solution)/shard_map/ppermute | solution.py:567
  135.5 132.7 %copy-start.37 = (bf16[768,384]{1,0:T(8,128)(2,1)}, bf16[768,384]{1,0:T(8,128)(2,1)S(1)}, u32[]{:S(2)}) copy-start(bf16[768,384]{1,0:T(8,128)(2,1)S(1)} %get-tuple-element.150) | copy-start | bytes 1769476
  258.3 32.7 %copy-start.24 = (bf16[768,1664]{1,0:T(8,128)(2,1)}, bf16[768,1664]{1,0:T(8,128)(2,1)S(1)}, u32[]{:S(2)}) copy-start(bf16[768,1664]{1,0:T(8,128)(2,1)S(1)} %dynamic-slice_bitcast_fusion.1) | copy-start | bytes 7667716
  261.3 64.0 %copy-start.61 = (f32[768]{0:T(1024)}, f32[768]{0:T(1024)S(1)}, u32[]{:S(2)}) copy-start(f32[768]{0:T(1024)S(1)} %mul.469) | copy-start | bytes 9220
  261.4 19.5 %copy-start.56 = (f32[768]{0:T(1024)}, f32[768]{0:T(1024)S(1)}, u32[]{:S(2)}) copy-start(f32[768]{0:T(1024)S(1)} %mul.447) | copy-start | bytes 9220
  280.5 43.5 %copy-start.3 = (bf16[1,512,768]{2,1,0:T(8,128)(2,1)}, bf16[1,512,768]{2,1,0:T(8,128)(2,1)S(1)}, u32[]{:S(2)}) copy-start(bf16[1,512,768]{2,1,0:T(8,128)(2,1)S(1)} %get-tuple-element.137) | copy-start | bytes 2359300
  280.5 9.8 %copy-start.59 = (f32[512]{0:T(512)}, f32[512]{0:T(512)S(1)}, u32[]{:S(2)}) copy-start(f32[512]{0:T(512)S(1)} %broadcast_multiply_fusion.11) | copy-start | bytes 6148
  281.2 9.8 %copy-start.41 = (bf16[512,768]{1,0:T(8,128)(2,1)}, bf16[512,768]{1,0:T(8,128)(2,1)S(1)}, u32[]{:S(2)}) copy-start(bf16[512,768]{1,0:T(8,128)(2,1)S(1)} %fusion.64) | copy-start | bytes 2359300
  281.2 9.8 %collective-permute-start.2 = (bf16[512,768]{1,0:T(8,128)(2,1)S(1)}, bf16[512,768]{1,0:T(8,128)(2,1)S(1)}, u32[]{:S(2)}, u32[]{:S(2)}) collective-permute-start(bf16[512,768]{1,0:T(8,128)(2,1)S(1)} %fusion.64), channel_id=1, source_target_pairs={{0,2},{2,0},{4,6},{6,4},{8,10},{10,8},{12,14},{14,12},{16,18},{18,... | collective-permute-start | bytes 2359304 | tf_op jit(solution)/shard_map/ppermute | solution.py:570
  320.5 3.5 collective-permute-start.3
  324.0 21.2 %copy-start.27 = (bf16[1,2,2,2,2,2,4,24,384]{8,7,6,5,4,3,2,1,0:T(8,128)(2,1)}, bf16[1,2,2,2,2,2,4,24,384]{8,7,6,5,4,3,2,1,0:T(8,128)(2,1)S(1)}, u32[]{:S(2)}) copy-start(bf16[1,2,2,2,2,2,4,24,384]{8,7,6,5,4,3,2,1,0:T(8,128)(2,1)S(1)} %get-tuple-element.155) | copy-start | bytes 7077892
  324.0 23.0 %copy-start.8 = (bf16[1,2,2,2,2,2,4,24,384]{8,7,6,5,4,3,2,1,0:T(8,128)(2,1)}, bf16[1,2,2,2,2,2,4,24,384]{8,7,6,5,4,3,2,1,0:T(8,128)(2,1)S(1)}, u32[]{:S(2)}) copy-start(bf16[1,2,2,2,2,2,4,24,384]{8,7,6,5,4,3,2,1,0:T(8,128)(2,1)S(1)} %get-tuple-element.154) | copy-start | bytes 7077892
  325.0 23.9 %copy-start.1 = (f32[512,768]{1,0:T(8,128)}, f32[512,768]{1,0:T(8,128)S(1)}, u32[]{:S(2)}) copy-start(f32[512,768]{1,0:T(8,128)S(1)} %get-tuple-element.182) | copy-start | bytes 4718596
  349.8 5.6 collective-permute-start.4
  355.4 28.6 %copy-start.15 = (bf16[512,768]{1,0:T(8,128)(2,1)}, bf16[512,768]{1,0:T(8,128)(2,1)S(1)}, u32[]{:S(2)}) copy-start(bf16[512,768]{1,0:T(8,128)(2,1)S(1)} %select_bitcast_fusion) | copy-start | bytes 2359300
  383.9 6.3 collective-permute-start.5
  463.3 14.1 %collective-permute-start.8 = (bf16[512,768]{1,0:T(8,128)(2,1)}, bf16[512,768]{1,0:T(8,128)(2,1)S(1)}, u32[]{:S(2)}, u32[]{:S(2)}) collective-permute-start(bf16[512,768]{1,0:T(8,128)(2,1)} %get-tuple-element.132), channel_id=1, source_target_pairs={{0,2},{2,0},{4,6},{6,4},{8,10},{10,8},{12,14},{14,12},{16,18},{18,... | collective-permute-start | bytes 2359304 | tf_op jit(solution)/shard_map/ppermute | solution.py:570
  463.8 70.1 %collective-permute-start.6 = (bf16[1,512,768]{2,1,0:T(8,128)(2,1)}, bf16[1,512,768]{2,1,0:T(8,128)(2,1)}, u32[]{:S(2)}, u32[]{:S(2)}) collective-permute-start(bf16[1,512,768]{2,1,0:T(8,128)(2,1)} %get-tuple-element.156), channel_id=1, source_target_pairs={{1,2},{2,1},{5,6},{6,5},{9,10},{10,9},{13,14},{14,13},{17,18},{18,... | collective-permute-start | bytes 2359304 | tf_op jit(solution)/shard_map/ppermute | solution.py:567
  523.2 17.3 %collective-permute-start.9 = (f32[512,768]{1,0:T(8,128)}, f32[512,768]{1,0:T(8,128)}, u32[]{:S(2)}, u32[]{:S(2)}) collective-permute-start(f32[512,768]{1,0:T(8,128)} %constant_dynamic-slice_fusion.2), channel_id=1, source_target_pairs={{0,2},{2,0},{4,6},{6,4},{8,10},{10,8},{12,14},{14,12},{16,18},{18,... | collective-permute-start | bytes 4718600 | tf_op jit(solution)/shard_map/ppermute | solution.py:570
  538.4 12.0 %slice-start = ((s8[12582912]{0:T(1024)(128)(4,1)}), s8[4194304]{0:T(1024)(128)(4,1)S(1)}, s32[]{:S(2)}) async-start(s8[12582912]{0:T(1024)(128)(4,1)} %bitcast.355), calls=%async_computation | async-start | bytes 8388608
  540.5 9.9 %slice-start.1 = ((s8[12582912]{0:T(1024)(128)(4,1)}), s8[4194304]{0:T(1024)(128)(4,1)S(1)}, s32[]{:S(2)}) async-start(s8[12582912]{0:T(1024)(128)(4,1)} %bitcast.355), calls=%async_computation.1 | async-start | bytes 8388608
  600.7 107.9 %copy-start.2 = (f32[512,768]{1,0:T(8,128)S(1)}, f32[512,768]{1,0:T(8,128)}, u32[]{:S(2)}) copy-start(f32[512,768]{1,0:T(8,128)} %copy-done.1) | copy-start | bytes 4718596
  600.7 107.9 %copy-start.62 = (f32[768]{0:T(1024)S(1)}, f32[768]{0:T(1024)}, u32[]{:S(2)}) copy-start(f32[768]{0:T(1024)} %copy-done.61) | copy-start | bytes 9220
  600.7 108.0 %copy-start.67 = (f32[512]{0:T(512)S(1)}, f32[512]{0:T(512)}, u32[]{:S(2)}) copy-start(f32[512]{0:T(512)} %copy-done.66) | copy-start | bytes 6148
  600.7 108.0 %copy-start.71 = (f32[512]{0:T(512)S(1)}, f32[512]{0:T(512)}, u32[]{:S(2)}) copy-start(f32[512]{0:T(512)} %copy-done.70) | copy-start | bytes 6148
  720.1 15.0 %collective-permute-start.10 = (bf16[512,768]{1,0:T(8,128)(2,1)}, bf16[512,768]{1,0:T(8,128)(2,1)}, u32[]{:S(2)}, u32[]{:S(2)}) collective-permute-start(bf16[512,768]{1,0:T(8,128)(2,1)} %get-tuple-element.127), channel_id=1, source_target_pairs={{0,2},{2,0},{4,6},{6,4},{8,10},{10,8},{12,14},{14,12},{16,18},{18,... | collective-permute-start | bytes 2359304 | tf_op jit(solution)/shard_map/ppermute | solution.py:570
  738.5 35.3 %copy-start.25 = (bf16[768,1664]{1,0:T(8,128)(2,1)S(1)}, bf16[768,1664]{1,0:T(8,128)(2,1)}, u32[]{:S(2)}) copy-start(bf16[768,1664]{1,0:T(8,128)(2,1)} %copy-done.24) | copy-start | bytes 7667716
  780.8 10.2 %collective-permute-start.11 = (f32[512,768]{1,0:T(8,128)}, f32[512,768]{1,0:T(8,128)}, u32[]{:S(2)}, u32[]{:S(2)}) collective-permute-start(f32[512,768]{1,0:T(8,128)} %constant_dynamic-slice_fusion.1), channel_id=1, source_target_pairs={{0,2},{2,0},{4,6},{6,4},{8,10},{10,8},{12,14},{14,12},{16,18},{18,... | collective-permute-start | bytes 4718600 | tf_op jit(solution)/shard_map/ppermute | solution.py:570
  912.2 22.0 %collective-permute-start.12 = (f32[1,512,768]{2,1,0:T(8,128)S(1)}, f32[1,512,768]{2,1,0:T(8,128)}, u32[]{:S(2)}, u32[]{:S(2)}) collective-permute-start(f32[1,512,768]{2,1,0:T(8,128)S(1)} %fusion.69), channel_id=1, source_target_pairs={{1,2},{2,1},{5,6},{6,5},{9,10},{10,9},{13,14},{14,13},{17,18},{18,... | collective-permute-start | bytes 4718600 | tf_op jit(solution)/shard_map/ppermute | solution.py:567
  (79 other events, 355.6 us)

commit v2 on v1

v2 whole, which is shorter than its diff:
```python
import functools
import math

import numpy as np
import jax
import jax.numpy as jnp
from jax import lax
from jax.experimental import pallas as pl
from jax.experimental.pallas import tpu as pltpu
from jax.sharding import PartitionSpec as P

BF = jnp.bfloat16
F32 = jnp.float32
EPS = 1e-05
AXES = ("dp", "seq")
GAP = 128
VMEM_LIMIT = 60 * 2**20
STRIP = 128
LANES = 128
BINS = 448
ROWS = 256
CHUNK = 64


def transform_matrix(length):
    half = length - GAP
    freq = np.arange(half)[:, None]
    place = np.arange(length)[None, :]
    angle = ((2 * freq + 1) * place % (4 * half)).astype(np.float64) * (math.pi / (2 * half))
    both = np.stack([np.cos(angle), -np.sin(angle)])
    both = both.reshape(2, half // BINS, BINS, length).transpose(1, 0, 2, 3)
    return both.reshape(2 * half, length).astype(np.float32)


def decay_table(length, features):
    channels = jnp.arange(features).astype(F32)
    positions = jnp.arange(length).astype(F32)
    rates = jnp.exp(math.log(1.0 / length) + channels / (features - 1) * math.log(4.0))
    scales = lax.rsqrt(jnp.sum(jnp.exp(-2.0 * positions[:, None] * rates[None, :]), axis=0))
    return jnp.exp(-positions[:, None] * rates[None, :]) * scales[None, :]


def dot(a, b, dims=((1,), (0,))):
    return lax.dot_general(a, b, (dims, ((), ())), preferred_element_type=F32)


def tap_same(row0, split):
    t = row0 + lax.broadcasted_iota(jnp.int32, (CHUNK, STRIP), 0)
    here = t >= split
    return [
        None if off == 2 else jnp.where(((t + (off - 2)) >= split) == here, 1.0, 0.0)
        for off in range(5)
    ]


def shifted(ref, row0, cols, same):
    block = ref[pl.ds(row0, CHUNK + 16), cols]
    out = []
    for off in range(5):
        turned = pltpu.roll(block, (2 - off) % (CHUNK + 16), 0) if off != 2 else block
        rows = turned[8 : 8 + CHUNK]
        out.append(rows if same[off] is None else rows * same[off])
    return out


def over_chunks(length, split, body):
    @pl.loop(0, length // CHUNK)
    def _(i):
        row0 = pl.multiple_of(i * CHUNK, CHUNK)
        touched = (split > row0 - 2) & (split < row0 + CHUNK + 2)

        @pl.when(touched)
        def _():
            body(row0, tap_same(row0, split))

        @pl.when(jnp.logical_not(touched))
        def _():
            body(row0, [None] * 5)


def weigh(rows, w_ref, cols, flip):
    total = None
    for off, x in enumerate(rows):
        tap = 4 - off if flip else off
        term = x * w_ref[tap : tap + 1, cols]
        total = term if total is None else total + term
    return total


def clear_ends(ref, length):
    ref[0:8, :] = jnp.zeros((8, ref.shape[1]), F32)
    ref[8 + length : 16 + length, :] = jnp.zeros((8, ref.shape[1]), F32)


def fetch(pairs, sems):
    copies = [pltpu.make_async_copy(src, dst, sems.at[i]) for i, (src, dst) in enumerate(pairs)]
    for copy in copies:
        copy.start()
    return copies


def mixer_forward_kernel(
    scalar_ref, own_ref, other_ref, sw_ref, cw_ref, iw_hbm, decay_hbm, fwd_hbm, inv_hbm,
    gated_ref, mine_ref, send_ref, br_hbm, q_hbm, key_hbm, conv_hbm, fh_hbm, uh_hbm,
    iw_ref, decay_ref, fwd_ref, inv_ref, br_ref, q_ref, key_ref, conv_ref, fh_ref, uh_ref,
    pad, kpad, filt, u, prod, in_sems, out_sems,
):
    length, width = q_ref.shape
    rows_own = own_ref.shape[0]
    half = length - GAP
    split, core = scalar_ref[0], scalar_ref[1]
    strips = width // STRIP
    loads = fetch(
        [
            (iw_hbm.at[core, :, pl.ds(0, 3 * width)], iw_ref),
            (decay_hbm, decay_ref),
            (fwd_hbm, fwd_ref),
            (inv_hbm, inv_ref),
        ],
        in_sems,
    )
    outs = [(br_ref, br_hbm), (q_ref, q_hbm), (key_ref, key_hbm), (fh_ref, fh_hbm), (uh_ref, uh_hbm), (conv_ref, conv_hbm)]
    stores = [pltpu.make_async_copy(src, dst, out_sems.at[i]) for i, (src, dst) in enumerate(outs)]
    clear_ends(pad, length)
    clear_ends(kpad, length)
    loads[0].wait()
    for ref, side in ((own_ref, core), (other_ref, 1 - core)):

        @pl.loop(0, rows_own // ROWS)
        def _(i):
            row0 = pl.multiple_of(side * rows_own + i * ROWS, ROWS)
            low = dot(ref[pl.ds(pl.multiple_of(i * ROWS, ROWS), ROWS), :], iw_ref[...]).astype(BF)
            br_ref[pl.ds(row0, ROWS), :] = low
            pad[pl.ds(row0 + 8, ROWS), :] = low.astype(F32)

    stores[0].start()

    def mix(row0, same):
        rows = pl.ds(row0, CHUNK)
        first = row0 + lax.broadcasted_iota(jnp.int32, (CHUNK, STRIP), 0) < split
        for part in range(3):
            for strip in range(strips):
                cols = pl.ds(part * width + strip * STRIP, STRIP)
                own = pl.ds(strip * STRIP, STRIP)
                low = weigh(shifted(pad, row0, cols, same), sw_ref, cols, False).astype(BF)
                if part == 0:
                    q_ref[rows, own] = low
                elif part == 1:
                    key_ref[rows, own] = low
                    kpad[pl.ds(row0 + 8, CHUNK), own] = low.astype(F32)
                else:
                    low = low.astype(F32)
                    u[0, rows, own] = jnp.where(first, low, 0.0).astype(BF)
                    u[1, rows, own] = jnp.where(first, 0.0, low).astype(BF)

    over_chunks(length, split, mix)
    stores[1].start()
    stores[2].start()
    loads[1].wait()

    def make_filter(row0, same):
        rows = pl.ds(row0, CHUNK)
        for strip in range(strips):
            cols = pl.ds(strip * STRIP, STRIP)
            total = weigh(shifted(kpad, row0, cols, same), cw_ref, cols, False)
            filt[rows, cols] = (total * decay_ref[rows, cols]).astype(BF)

    over_chunks(length, split, make_filter)
    scale = 1.0 / half
    loads[2].wait()

    @pl.loop(0, half // BINS)
    def _(i):
        rows = pl.ds(pl.multiple_of(i * 2 * BINS, 2 * BINS), 2 * BINS)
        f = dot(fwd_ref[rows, pl.ds(0, half)], filt[pl.ds(0, half), :])
        fr, fi = f[:BINS], f[BINS:]
        fh_ref[rows, :] = f.astype(BF)
        for m in range(2):
            s = dot(fwd_ref[rows, :], u[m])
            uh_ref[m, rows, :] = s.astype(BF)
            sr, si = s[:BINS], s[BINS:]
            prod[m, rows, :] = jnp.concatenate(
                [(fr * sr - fi * si) * scale, (fr * si + fi * sr) * scale], axis=0
            ).astype(BF)

    stores[3].start()
    stores[4].start()
    corner = split // ROWS
    loads[3].wait()

    @pl.loop(0, length // ROWS)
    def _(i):
        rows = pl.ds(pl.multiple_of(i * ROWS, ROWS), ROWS)
        pick = (i > corner).astype(jnp.int32)
        conv_ref[rows, :] = dot(inv_ref[rows, :], prod[pick]).astype(BF)

        @pl.when(i == corner)
        def _():
            later = i * ROWS + lax.broadcasted_iota(jnp.int32, (ROWS, width), 0) >= split
            other = dot(inv_ref[rows, :], prod[1])
            conv_ref[rows, :] = jnp.where(later, other, conv_ref[rows, :].astype(F32)).astype(BF)

        gated_ref[rows, :] = (q_ref[rows, :].astype(F32) * conv_ref[rows, :].astype(F32)).astype(BF)

    stores[5].start()
    mine_ref[...] = gated_ref[pl.ds(pl.multiple_of(core * rows_own, ROWS), rows_own), :]
    send_ref[...] = gated_ref[pl.ds(pl.multiple_of((1 - core) * rows_own, ROWS), rows_own), :]
    for copy in stores:
        copy.wait()


def mixer_backward_kernel(
    scalar_ref, mid_own_ref, mid_other_ref, sw_ref, cw_ref,
    w_hbm, own_hbm, other_hbm, gated_hbm, br_hbm, decay_hbm, fwd_hbm, inv_hbm, q_hbm, key_hbm, conv_hbm, fh_hbm, uh_hbm,
    rest_ref, dn_ref, dn_send_ref, dsw_ref, dcw_ref,
    ow_ref, iw_ref, own_ref, other_ref, gated_ref, br_ref, decay_ref, fwd_ref, inv_ref, q_ref, key_ref, conv_ref, fh_ref,
    uh_ref, pad, epad, kpad, g, prod, mid_ref, dbr_ref, dsw_sum, dcw_sum, in_sems,
):
    length, width = q_ref.shape
    rows_own, features = own_ref.shape
    half = length - GAP
    split, core = scalar_ref[0], scalar_ref[1]
    strips = width // STRIP
    part = pl.ds(pl.multiple_of(core * width, STRIP), width)
    apart = pl.ds(pl.multiple_of((1 - core) * width, STRIP), width)
    near = pl.ds(pl.multiple_of(core * rows_own, ROWS), rows_own)
    far = pl.ds(pl.multiple_of((1 - core) * rows_own, ROWS), rows_own)
    out_cols = pl.ds(3 * width, width)
    loads = fetch(
        [
            (w_hbm.at[0, part, out_cols], ow_ref.at[0]),
            (w_hbm.at[1, part, out_cols], ow_ref.at[1]),
            (conv_hbm, conv_ref),
            (q_hbm, q_ref),
            (fwd_hbm, fwd_ref),
            (fh_hbm, fh_ref),
            (uh_hbm, uh_ref),
            (inv_hbm, inv_ref),
            (decay_hbm, decay_ref),
            (key_hbm, key_ref),
            (br_hbm, br_ref),
            (gated_hbm, gated_ref),
            (own_hbm, own_ref),
            (other_hbm, other_ref),
            (w_hbm.at[core, :, pl.ds(0, 3 * width)], iw_ref),
        ],
        in_sems,
    )
    mid_ref[near, :] = mid_own_ref[...]
    mid_ref[far, :] = mid_other_ref[...]
    clear_ends(pad, length)
    clear_ends(epad, length)
    clear_ends(kpad, length)
    dsw_sum[...] = jnp.zeros(dsw_sum.shape, F32)
    dcw_sum[...] = jnp.zeros(dcw_sum.shape, F32)
    rest_ref[1 - core, :, pl.ds(0, 3 * width)] = jnp.zeros((features, 3 * width), BF)
    for h in range(2):
        rest_ref[h, apart, out_cols] = jnp.zeros((width, width), BF)
    for copy in loads[:4]:
        copy.wait()
    out_w = jnp.concatenate([ow_ref[0], ow_ref[1]], axis=1)

    @pl.loop(0, length // ROWS)
    def _(i):
        row0 = pl.multiple_of(i * ROWS, ROWS)
        rows = pl.ds(row0, ROWS)
        dg = dot(mid_ref[rows, :], out_w, ((1,), (1,)))
        first = row0 + lax.broadcasted_iota(jnp.int32, (ROWS, width), 0) < split
        pad[pl.ds(row0 + 8, ROWS), pl.ds(0, width)] = dg * conv_ref[rows, :].astype(F32)
        dc = dg * q_ref[rows, :].astype(F32)
        g[0, rows, :] = jnp.where(first, dc, 0.0).astype(BF)
        g[1, rows, :] = jnp.where(first, 0.0, dc).astype(BF)

    scale = 1.0 / half
    for copy in loads[4:7]:
        copy.wait()

    @pl.loop(0, half // BINS)
    def _(i):
        rows = pl.ds(pl.multiple_of(i * 2 * BINS, 2 * BINS), 2 * BINS)
        f = fh_ref[rows, :].astype(F32)
        fr, fi = f[:BINS], f[BINS:]
        er = None
        for m in range(2):
            s = dot(fwd_ref[rows, :], g[m])
            sr, si = s[:BINS], s[BINS:]
            prod[m, rows, :] = jnp.concatenate(
                [(fr * sr + fi * si) * scale, (fr * si - fi * sr) * scale], axis=0
            ).astype(BF)
            w = uh_ref[m, rows, :].astype(F32)
            wr, wi = w[:BINS], w[BINS:]
            tr = wr * sr + wi * si
            ti = wr * si - wi * sr
            er, ei = (tr, ti) if er is None else (er + tr, ei + ti)
        prod[2, rows, :] = jnp.concatenate([er * scale, ei * scale], axis=0).astype(BF)

    corner = split // ROWS
    value_cols = pl.ds(2 * width, width)
    for copy in loads[7:10]:
        copy.wait()
    kpad[pl.ds(8, length), :] = key_ref[...].astype(F32)

    @pl.loop(0, length // ROWS)
    def _(i):
        row0 = pl.multiple_of(i * ROWS, ROWS)
        rows = pl.ds(row0, ROWS)
        spot = pl.ds(row0 + 8, ROWS)
        pick = (i > corner).astype(jnp.int32)
        pad[spot, value_cols] = dot(inv_ref[rows, :], prod[pick])

        @pl.when(i == corner)
        def _():
            later = i * ROWS + lax.broadcasted_iota(jnp.int32, (ROWS, width), 0) >= split
            other = dot(inv_ref[rows, :], prod[1])
            pad[spot, value_cols] = jnp.where(later, other, pad[spot, value_cols])

        inside = row0 + lax.broadcasted_iota(jnp.int32, (ROWS, width), 0) < half
        d_filt = dot(inv_ref[rows, :], prod[2])
        epad[spot, :] = jnp.where(inside, d_filt, 0.0) * decay_ref[rows, :]

    def key_taps(row0, same):
        spot = pl.ds(row0 + 8, CHUNK)
        for strip in range(strips):
            cols = pl.ds(strip * STRIP, STRIP)
            e = epad[spot, cols]
            pad[spot, pl.ds(width + strip * STRIP, STRIP)] = weigh(shifted(epad, row0, cols, same), cw_ref, cols, True)
            for off, x in enumerate(shifted(kpad, row0, cols, same)):
                dcw_sum[off, :, cols] += (x * e).reshape(CHUNK // 8, 8, STRIP).sum(0)

    over_chunks(length, split, key_taps)
    loads[10].wait()

    @pl.loop(0, 3 * strips)
    def _(strip):
        cols = pl.ds(pl.multiple_of(strip * STRIP, STRIP), STRIP)
        kpad[pl.ds(8, length), pl.ds(0, STRIP)] = br_ref[:, cols].astype(F32)

        def branch_taps(row0, same):
            e = pad[pl.ds(row0 + 8, CHUNK), cols]
            total = weigh(shifted(pad, row0, cols, same), sw_ref, cols, True)
            dbr_ref[pl.ds(row0, CHUNK), cols] = total.astype(BF)
            for off, x in enumerate(shifted(kpad, row0, pl.ds(0, STRIP), same)):
                dsw_sum[off, :, cols] += (x * e).reshape(CHUNK // 8, 8, STRIP).sum(0)

        over_chunks(length, split, branch_taps)

    dsw_ref[...] = jnp.sum(dsw_sum[...], axis=1)
    dcw_ref[...] = jnp.sum(dcw_sum[...], axis=1)
    for copy in loads[11:]:
        copy.wait()
    d_out = dot(gated_ref[...], mid_ref[...], ((0,), (0,))).astype(BF)
    for h in range(2):
        rest_ref[h, part, out_cols] = d_out[:, h * width : (h + 1) * width]
    for p in range(3):
        cols = pl.ds(p * width, width)
        d_in = dot(own_ref[...], dbr_ref[near, cols], ((0,), (0,)))
        d_in += dot(other_ref[...], dbr_ref[far, cols], ((0,), (0,)))
        rest_ref[core, :, cols] = d_in.astype(BF)
    dn_ref[...] = dot(dbr_ref[near, :], iw_ref[...], ((1,), (1,)))
    dn_send_ref[...] = dot(dbr_ref[far, :], iw_ref[...], ((1,), (1,))).astype(BF)


def local_call(kernel, args, direct, outs, direct_outs, scratch):
    vmem, anywhere = pl.BlockSpec(memory_space=pltpu.VMEM), pl.BlockSpec(memory_space=pl.ANY)
    return pl.pallas_call(
        kernel,
        out_shape=[jax.ShapeDtypeStruct(shape, dtype) for shape, dtype in outs],
        in_specs=[pl.BlockSpec(memory_space=pltpu.SMEM)]
        + [vmem] * (direct - 1)
        + [anywhere] * (len(args) - direct),
        out_specs=[vmem] * direct_outs + [anywhere] * (len(outs) - direct_outs),
        scratch_shapes=scratch,
        compiler_params=pltpu.CompilerParams(vmem_limit_bytes=VMEM_LIMIT),
    )(*args)


def mixer_forward(scalars, own, other, sw, cw, weight, decay, fwd, inv):
    length, width = decay.shape
    features = own.shape[1]
    bins = fwd.shape[0]
    tall, short, wide = (length, width), (own.shape[0], width), (length, 3 * width)
    kept = [(wide, BF), (tall, BF), (tall, BF), (tall, BF), ((bins, width), BF), ((2, bins, width), BF)]
    scratch = [((features, 3 * width), BF), (tall, F32), (fwd.shape, BF), (inv.shape, BF)] + kept
    scratch += [
        ((length + 16, 3 * width), F32),
        ((length + 16, width), F32),
        (tall, BF),
        ((2,) + tall, BF),
        ((2, bins, width), BF),
    ]
    return local_call(
        mixer_forward_kernel,
        (scalars, own, other, sw, cw, weight, decay, fwd, inv),
        5,
        [(tall, BF), (short, BF), (short, BF)] + kept,
        3,
        [pltpu.VMEM(*x) for x in scratch] + [pltpu.SemaphoreType.DMA((4,)), pltpu.SemaphoreType.DMA((6,))],
    )


def mixer_backward(scalars, mid_own, mid_other, sw, cw, weight, own, other, gated, br, decay, fwd, inv, q, key, conv, fh, uh):
    length, width = decay.shape
    bins = fwd.shape[0]
    rows, features = mid_own.shape
    held = (own, other, gated, br, decay, fwd, inv, q, key, conv, fh, uh)
    scratch = [((2, width, width), BF), ((features, 3 * width), BF)] + [(x.shape, x.dtype) for x in held]
    scratch += [
        ((length + 16, 3 * width), F32),
        ((length + 16, width), F32),
        ((length + 16, width), F32),
        ((2, length, width), BF),
        ((3, bins, width), BF),
        ((length, features), BF),
        ((length, 3 * width), BF),
        ((5, 8, 3 * width), F32),
        ((5, 8, width), F32),
    ]
    return local_call(
        mixer_backward_kernel,
        (scalars, mid_own, mid_other, sw, cw, weight) + held,
        5,
        [
            ((2, features, 4 * width), BF),
            ((rows, features), F32),
            ((rows, features), BF),
            ((5, 3 * width), F32),
            ((5, width), F32),
        ],
        5,
        [pltpu.VMEM(*x) for x in scratch] + [pltpu.SemaphoreType.DMA((15,))],
    )


def cube(dp_count):
    bits = (dp_count // 2).bit_length() - 1
    core, seq = bits, bits + 1
    low, rest = [bits - 1], list(range(bits - 1))
    orders = (
        rest + [seq] + low, rest + low + [seq], low + [seq] + rest,
        low + rest + [seq], [seq] + rest + low, [seq] + low + rest,
    )
    return bits, core, seq, orders


def place(bits):
    dp, seq = lax.axis_index("dp"), lax.axis_index("seq")
    coords = [(dp // (2 << (bits - 1 - d))) % 2 for d in range(bits)] + [dp % 2, seq]

    def neighbour(d):
        if d == bits + 1:
            return dp, 1 - seq
        step = 1 if d == bits else 2 << (bits - 1 - d)
        return dp + step * (1 - 2 * coords[d]), seq

    return coords, neighbour


def region(fixed, dims):
    return tuple(fixed[d] if d in fixed else slice(None) for d in range(dims))


def greet(neighbours):
    barrier = pltpu.get_barrier_semaphore()
    for device in neighbours:
        pl.semaphore_signal(barrier, inc=1, device_id=device, device_id_type=pl.DeviceIdType.MESH)
    pl.semaphore_wait(barrier, len(neighbours))


def remote(src, dst, send, recv, device):
    copy = pltpu.make_async_remote_copy(
        src_ref=src, dst_ref=dst, send_sem=send, recv_sem=recv,
        device_id=device, device_id_type=pl.DeviceIdType.MESH,
    )
    copy.start()
    return copy


GATHER_UNITS = (
    (3, 0, 640, 0, 0), (3, 640, 640, 1, 0), (3, 1280, 384, 2, 0),
    (0, 0, 768, 0, 1), (0, 768, 768, 1, 1), (2, 2, 2, 2, 1),
    (0, 1536, 768, 0, 2), (0, 2304, 768, 1, 2),
    (1, 0, 2, 0, 3), (1, 2, 2, 1, 3), (4, 1280, 384, 2, 3),
    (4, 0, 640, 0, 4), (4, 640, 640, 1, 4),
    (2, 0, 1, 0, 5), (2, 1, 1, 1, 5),
)
SCATTER_UNITS = (
    (0, 0, 768, 0, 0), (0, 768, 768, 1, 0), (2, 2, 2, 2, 0),
    (0, 1536, 768, 0, 1), (0, 2304, 768, 1, 1), (3, 1280, 256, 2, 1),
    (1, 0, 2, 0, 2), (1, 2, 2, 1, 2), (4, 1280, 256, 2, 2),
    (3, 0, 640, 0, 3), (3, 640, 640, 1, 3), (5, 0, 128, 2, 3),
    (4, 0, 640, 0, 4), (4, 640, 640, 1, 4),
    (2, 0, 1, 0, 5), (2, 1, 1, 1, 5),
)


def piece_of(unit, slabs):
    span = pl.ds(unit[1], unit[2])
    return (span, slice(None), slice(None)) if slabs else (slice(None), span)


def ticks(units, stages, shrinking):
    steps = [max(2**t, 2 ** (stages - 2)) for t in range(stages)]
    if shrinking:
        steps = steps[::-1]
    spacing = 2**stages // 4
    due = []
    for i, unit in enumerate(units):
        if shrinking:
            due.append((spacing * (unit[4] - 1) - 1, i, -1))
        due += [(spacing * unit[4] + sum(steps[:t]), i, t) for t in range(stages + 1)]
    return [(i, t) for _, i, t in sorted(due)]


def gather_kernel(dp_count, units, own, full, sems):
    bits, core_dim, _, orders = cube(dp_count)
    dims = bits + 2
    stages = dims - 1
    coords, neighbour = place(bits)
    core = coords[core_dim]
    sibling = neighbour(core_dim)
    greet([neighbour(d) for d in range(dims)])
    ici_send, ici_recv, core_send, core_recv, local = sems
    mine = region(dict(enumerate(coords)), dims)
    firsts, forwards, sends = [], [], []
    last = [None] * len(units)
    for u, unit in enumerate(units):
        array, tail = unit[0], piece_of(unit, len(own[unit[0]].shape) == 4)
        piece = own[array].at[(slice(None),) + tail]
        here = full[array].at[(slice(None),) + mine + tail]
        keep = pltpu.make_async_copy(piece, here, local.at[u])
        keep.start()
        firsts.append((keep, remote(piece, here, core_send.at[u, 0], core_recv.at[u, 0], sibling)))
    for u, t in ticks(units, stages, False):
        unit = units[u]
        array, tail, order = unit[0], piece_of(unit, len(own[unit[0]].shape) == 4), orders[unit[3]]
        fixed = {e: coords[e] for e in order[t:]}
        if t == 0:
            firsts[u][0].wait()
            firsts[u][1].wait_recv()
        else:
            last[u].wait_recv()
            got = full[array].at[(core,) + region(fixed | {order[t - 1]: 1 - coords[order[t - 1]]}, dims) + tail]
        if t < stages:
            held = full[array].at[(core,) + region(fixed, dims) + tail]
            last[u] = remote(held, held, ici_send.at[u, t], ici_recv.at[u, t], neighbour(order[t]))
            sends.append(last[u])
        if t > 0:
            forwards.append(remote(got, got, core_send.at[u, t], core_recv.at[u, t], sibling))
    for keep, copy in firsts:
        copy.wait_send()
    for copy in forwards:
        copy.wait()
    for copy in sends:
        copy.wait_send()


def gather_weights(own, dp_count, number):
    bits = cube(dp_count)[0]
    stages = bits + 1
    units = GATHER_UNITS
    arrays = len(own)
    count = len(units)

    def body(*refs):
        gather_kernel(dp_count, units, refs[:arrays], refs[arrays : 2 * arrays], refs[2 * arrays :])

    grid = (2,) * (bits + 2)
    anywhere = pl.BlockSpec(memory_space=pl.ANY)
    return pl.pallas_call(
        body,
        out_shape=[jax.ShapeDtypeStruct(x.shape[:1] + grid + x.shape[1:], x.dtype) for x in own],
        in_specs=[anywhere] * arrays,
        out_specs=[anywhere] * arrays,
        scratch_shapes=[pltpu.SemaphoreType.DMA((count, stages))] * 2
        + [pltpu.SemaphoreType.DMA((count, stages + 1))] * 2
        + [pltpu.SemaphoreType.DMA((count,))],
        compiler_params=pltpu.CompilerParams(collective_id=number, has_side_effects=True),
    )(*own)


def scatter_kernel(dp_count, units, grads, outs, held, first, arrived, final, sems):
    bits, core_dim, _, orders = cube(dp_count)
    dims = bits + 2
    stages = dims - 1
    coords, neighbour = place(bits)
    core = coords[core_dim]
    sibling = neighbour(core_dim)
    greet([neighbour(d) for d in range(dims)])
    ici_send, ici_recv, core_send, core_recv, local = sems
    everything = region({}, dims)

    def add(u, fixed, extra):
        free = [d for d in range(dims) if d not in fixed]

        @pl.loop(0, 2 ** len(free))
        def _(i):
            at = {d: (i // 2 ** (len(free) - 1 - j)) % 2 for j, d in enumerate(free)}
            index = tuple(at[d] if d in at else fixed[d] for d in range(dims))
            held[u][index] += extra[tuple(at[d] for d in free)]

    starts, sends = [None] * len(units), []
    last = [None] * len(units)
    for u, t in ticks(units, stages, True):
        if t < 0:
            array, tail = units[u][0], piece_of(units[u], len(outs[units[u][0]].shape) == 4)
            load = pltpu.make_async_copy(grads[array].at[(core,) + everything + tail], held[u], local.at[u, 0])
            load.start()
            other = grads[array].at[(1 - core,) + everything + tail]
            starts[u] = (load, remote(other, first[u], core_send.at[u, 0], core_recv.at[u, 0], sibling))
            continue
        order = orders[units[u][3]][::-1]
        fixed = {d: coords[d] for d in order[:t]}
        if t == 0:
            starts[u][0].wait()
            starts[u][1].wait_recv()
            add(u, fixed, first[u])
        else:
            last[u].wait_recv()
            add(u, fixed, arrived[u][t - 1])
        if t < stages:
            away = held[u].at[region(fixed | {order[t]: 1 - coords[order[t]]}, dims)]
            last[u] = remote(away, arrived[u][t], ici_send.at[u, t], ici_recv.at[u, t], neighbour(order[t]))
            sends.append(last[u])
        else:
            away = held[u].at[region(fixed | {core_dim: 1 - core}, dims)]
            last[u] = remote(away, final[u], core_send.at[u, 1], core_recv.at[u, 1], sibling)
    ends = []
    mine = region(dict(enumerate(coords)), dims)
    for u, unit in enumerate(units):
        array, tail = unit[0], piece_of(unit, len(outs[unit[0]].shape) == 4)
        own = pltpu.make_async_copy(held[u].at[mine], outs[array].at[(core,) + tail], local.at[u, 1])
        own.start()
        last[u].wait_recv()
        other = pltpu.make_async_copy(final[u], outs[array].at[(1 - core,) + tail], local.at[u, 2])
        other.start()
        ends += [own, other]
    for copy in ends:
        copy.wait()
    for copy in sends + last + [s[1] for s in starts]:
        copy.wait_send()


def scatter_grads(grads, dp_count, number):
    bits = cube(dp_count)[0]
    dims = bits + 2
    stages = dims - 1
    units = SCATTER_UNITS
    arrays = len(grads)
    count = len(units)
    grid = (2,) * dims
    slabs = []
    for array, _, size, _, _ in units:
        shape = grads[array].shape[1 + dims :]
        slabs.append((size,) + shape[1:] if len(shape) == 3 else shape[:-1] + (size,))

    def body(*refs):
        grads_in, outs, refs = refs[:arrays], refs[arrays : 2 * arrays], refs[2 * arrays :]
        held, first, final = refs[:count], refs[count : 2 * count], refs[2 * count : 3 * count]
        refs = refs[3 * count :]
        arrived = [refs[u * stages : (u + 1) * stages] for u in range(count)]
        scatter_kernel(dp_count, units, grads_in, outs, held, first, arrived, final, refs[count * stages :])

    anywhere = pl.BlockSpec(memory_space=pl.ANY)
    return pl.pallas_call(
        body,
        out_shape=[jax.ShapeDtypeStruct(x.shape[:1] + x.shape[1 + dims :], x.dtype) for x in grads],
        in_specs=[anywhere] * arrays,
        out_specs=[anywhere] * arrays,
        scratch_shapes=[pltpu.VMEM(grid + slab, BF) for slab in slabs] * 2
        + [pltpu.VMEM(slab, BF) for slab in slabs]
        + [pltpu.VMEM((2,) * (dims - 1 - t) + slab, BF) for slab in slabs for t in range(stages)]
        + [pltpu.SemaphoreType.DMA((count, stages))] * 2
        + [pltpu.SemaphoreType.DMA((count, 2))] * 2
        + [pltpu.SemaphoreType.DMA((count, 3))],
        compiler_params=pltpu.CompilerParams(
            collective_id=number, has_side_effects=True, vmem_limit_bytes=VMEM_LIMIT
        ),
    )(*grads)


def norm_parts(x):
    center = x - jnp.mean(x, axis=-1, keepdims=True)
    r = lax.rsqrt(jnp.mean(center * center, axis=-1, keepdims=True) + EPS)
    return center * r, r


def norm_back(x, gain, d):
    xhat, r = norm_parts(x)
    h = d * gain
    dx = r * (h - jnp.mean(h, axis=-1, keepdims=True) - xhat * jnp.mean(h * xhat, axis=-1, keepdims=True))
    return dx, jnp.sum(d * xhat, axis=0, keepdims=True)


SLOPE = math.sqrt(2.0 / math.pi)
CUBE = 0.044715


def gelu_parts(x):
    square = x * x
    t = jnp.tanh(SLOPE * (x + CUBE * square * x))
    flat = 0.5 + 0.5 * t
    return x * flat, flat + 0.5 * x * (1.0 - t * t) * (SLOPE + 3.0 * SLOPE * CUBE * square)


def mlp_forward_kernel(
    scalar_ref, x_ref, g0_ref, g1_ref, o0_ref, o1_ref, mg_ref, ng_ref, wg_ref, wu_ref, d0_ref, d1_ref,
    mid_ref, hm_ref, pre_ref, out_ref, next_ref,
):
    j = pl.program_id(0)

    @pl.when(j == 0)
    def _():
        width = g0_ref.shape[1]
        mid = x_ref[...]
        for ref, side in ((g0_ref, scalar_ref[1]), (g1_ref, 1 - scalar_ref[1])):
            rows = pl.ds(pl.multiple_of(side * width, STRIP), width)
            mid += dot(ref[...], jnp.concatenate([o0_ref[rows, :], o1_ref[rows, :]], axis=1))
        mid_ref[...] = mid
        out_ref[...] = mid
        hm_ref[...] = (norm_parts(mid)[0] * mg_ref[...]).astype(BF)

    gate = dot(hm_ref[...], wg_ref[...])
    up = dot(hm_ref[...], wu_ref[...])
    pre_ref[0] = gate.astype(BF)
    pre_ref[1] = up.astype(BF)
    hid = (gelu_parts(gate)[0] * up).astype(BF)
    down = jnp.concatenate([d0_ref[...], d1_ref[...]], axis=1)
    out_ref[...] += dot(hid, down)

    @pl.when(j == pl.num_programs(0) - 1)
    def _():
        next_ref[...] = (norm_parts(out_ref[...])[0] * ng_ref[...]).astype(BF)


def mlp_backward_kernel(
    g_ref, hm_ref, mid_ref, mg_ref, pre_ref, wg_ref, wu_ref, d0_ref, d1_ref,
    dgu_ref, ddn_ref, dmid_ref, mlow_ref, dmg_ref,
    glow, hm_t, acc,
):
    j = pl.program_id(0)
    width = d0_ref.shape[1]

    @pl.when(j == 0)
    def _():
        glow[...] = g_ref[...].astype(BF)
        hm_t[...] = hm_ref[...].T
        acc[...] = jnp.zeros(acc.shape, F32)

    down = jnp.concatenate([d0_ref[...], d1_ref[...]], axis=1)
    dh = dot(glow[...], down, ((1,), (1,)))
    value, slope = gelu_parts(pre_ref[0].astype(F32))
    up = pre_ref[1].astype(F32)
    hid = (value * up).astype(BF)
    d_gate = (dh * up * slope).astype(BF)
    d_up = (dh * value).astype(BF)
    d_down = dot(hid, glow[...], ((0,), (0,))).astype(BF)
    ddn_ref[0] = d_down[:, :width]
    ddn_ref[1] = d_down[:, width:]
    for h, d in enumerate((d_gate, d_up)):
        grad = dot(hm_t[...], d).astype(BF)
        if len(dgu_ref.shape) == 3:
            dgu_ref[h] = grad
        else:
            dgu_ref[:, h * TILE : (h + 1) * TILE] = grad
    acc[...] += dot(d_gate, wg_ref[...], ((1,), (1,))) + dot(d_up, wu_ref[...], ((1,), (1,)))

    @pl.when(j == pl.num_programs(0) - 1)
    def _():
        dx, dg = norm_back(mid_ref[...], mg_ref[...], acc[...])
        dmid = g_ref[...] + dx
        dmid_ref[...] = dmid
        mlow_ref[...] = dmid.astype(BF)
        dmg_ref[...] = dg


TILE = 512


def whole(shape):
    return pl.BlockSpec(shape, lambda j: (0,) * len(shape))


def weight_specs(layout, hidden, features):
    steps = hidden // TILE
    gate_up = pl.BlockSpec((features, TILE), lambda j: (0, j))
    up = pl.BlockSpec((features, TILE), lambda j: (1, j) if layout == "halves" else (0, steps + j))
    down = [
        pl.BlockSpec((TILE, features // 2), lambda j: (j, 0)),
        pl.BlockSpec((TILE, features // 2), lambda j: (steps + j, 0)),
    ]
    return [gate_up, up] + down


def mlp_forward(scalars, x, g0, g1, weight, mg, ng, weights):
    layout, gu, dn = weights
    rows, features = x.shape
    hidden = dn.shape[0] // 2
    square, vector = whole((rows, features)), whole((1, features))
    narrow = [whole(a.shape) for a in (g0, g1)]
    narrow += [pl.BlockSpec((features, features // 2), lambda j, h=h: (h, 3)) for h in range(2)]
    shapes = [((rows, features), F32), ((rows, features), BF), ((2, rows, hidden), BF), ((rows, features), F32), ((rows, features), BF)]
    return pl.pallas_call(
        mlp_forward_kernel,
        grid=(hidden // TILE,),
        out_shape=[jax.ShapeDtypeStruct(*s) for s in shapes],
        in_specs=[pl.BlockSpec(memory_space=pltpu.SMEM), square] + narrow + [vector] * 2 + weight_specs(layout, hidden, features),
        out_specs=[square, square, pl.BlockSpec((2, rows, TILE), lambda j: (0, 0, j)), square, square],
        compiler_params=pltpu.CompilerParams(vmem_limit_bytes=VMEM_LIMIT),
    )(scalars, x, g0, g1, weight, weight, mg, ng, gu, gu, dn, dn)


def mlp_backward(g, hm, mid, mg, pre, weights, side_by_side):
    layout, gu, dn = weights
    rows, features = g.shape
    hidden = pre.shape[2]
    width = features // 2
    square, vector = whole((rows, features)), whole((1, features))
    both = (features, 2 * hidden) if side_by_side else (2, features, hidden)
    shapes = [(both, BF), ((2, hidden, width), BF), ((rows, features), F32), ((rows, features), BF), ((1, features), F32)]
    return pl.pallas_call(
        mlp_backward_kernel,
        grid=(hidden // TILE,),
        out_shape=[jax.ShapeDtypeStruct(*s) for s in shapes],
        in_specs=[square] * 3
        + [vector, pl.BlockSpec((2, rows, TILE), lambda j: (0, 0, j))]
        + weight_specs(layout, hidden, features),
        out_specs=[
            pl.BlockSpec((features, 2 * TILE), lambda j: (0, j))
            if side_by_side
            else pl.BlockSpec((2, features, TILE), lambda j: (0, 0, j)),
            pl.BlockSpec((2, TILE, width), lambda j: (0, j, 0)),
            square, square, vector,
        ],
        scratch_shapes=[pltpu.VMEM((rows, features), BF), pltpu.VMEM((features, rows), BF), pltpu.VMEM((rows, features), F32)],
        compiler_params=pltpu.CompilerParams(vmem_limit_bytes=VMEM_LIMIT),
    )(g, hm, mid, mg, pre, gu, gu, dn, dn)


def shards(
    tokens, split_points, cotangent, norm_gain, in_weight, short_taps, cond_taps,
    out_weight, mlp_gain, gate_up, down_weight,
):
    rows, features = tokens.shape[1:]
    dp_count, seq_count = lax.axis_size("dp"), lax.axis_size("seq")
    devices = dp_count * seq_count
    length = rows * seq_count
    width = features // 2
    layers = in_weight.shape[0]
    share = norm_gain.shape[1]
    hidden = down_weight.shape[1] * devices
    core = lax.axis_index("dp") % 2
    seq = lax.axis_index("seq")

    swap = [(4 * k + a, 4 * k + 3 - a) for k in range(devices // 4) for a in (1, 2)]
    flip = [(i, i ^ 1) for i in range(dp_count)]

    def swap_rows(x):
        return jnp.where(core == seq, x, lax.ppermute(x, AXES, swap))

    def sibling(x):
        return lax.ppermute(x, "dp", flip)

    def beside(own, other, axis):
        return jnp.where(
            core == 0,
            jnp.concatenate([own, other], axis=axis),
            jnp.concatenate([other, own], axis=axis),
        )

    def half_of(x, which, axis):
        size = x.shape[axis] // 2
        return lax.dynamic_slice_in_dim(x, which * size, size, axis)

    def own_channels(x):
        parts = x.shape[-1] // features
        x = x.reshape(x.shape[:-1] + (parts, 2, width))
        x = lax.dynamic_index_in_dim(x, core, x.ndim - 2, keepdims=False)
        return x.reshape(x.shape[:-2] + (parts * width,))

    split = swap_rows(split_points)
    stream = swap_rows(tokens).reshape(rows, features).astype(F32)
    grad = swap_rows(cotangent).reshape(rows, features).astype(F32)
    table = transform_matrix(length)
    fwd = jnp.asarray(table, BF)
    inv = jnp.asarray(np.ascontiguousarray(table.T), BF)
    decay = own_channels(decay_table(length, features))

    def halves(x):
        parts = x.shape[-1] // features
        x = x.reshape(x.shape[:-1] + (parts, 2, width))
        x = jnp.moveaxis(x, -2, 0)
        return x.reshape(x.shape[:-2] + (parts * width,))

    grid = (2,) * (cube(dp_count)[0] + 2)

    small = jnp.concatenate(
        [
            norm_gain[:, :, None],
            mlp_gain[:, :, None],
            cond_taps.transpose(0, 2, 1),
            short_taps.reshape(layers, 5, share, 3).transpose(0, 2, 3, 1).reshape(layers, share, 15),
        ],
        axis=2,
    )
    small = jnp.pad(small, ((0, 0), (0, 0), (0, LANES - 22)))
    own = [gate_up[0].reshape(share, 2, hidden).transpose(1, 0, 2)]
    own += [halves(down_weight[layer]).reshape(2, hidden // features, share, width) for layer in range(layers)]
    for layer in range(layers):
        pair = jnp.stack([small[layer], jnp.zeros_like(small[layer])])
        own.append(jnp.concatenate([halves(in_weight[layer]), halves(out_weight[layer]), pair], axis=2))
    full = gather_weights(own, dp_count, 0)
    downs = [x.reshape(2 * hidden, width) for x in full[1 : 1 + layers]]
    mixer_w = [x.reshape(2, features, 4 * width + LANES) for x in full[1 + layers :]]
    late, _ = lax.optimization_barrier((gate_up[1:], full[0]))
    gate_ups = [("halves", full[0].reshape(2 * features, hidden))]
    gate_ups += [("plain", lax.all_gather(x, AXES, axis=0, tiled=True)) for x in late]
    ng, mg, ct, st = [], [], [], []
    for layer in range(layers):
        small = mixer_w[layer][0, :, 4 * width :].astype(F32).T
        ng.append(small[0:1])
        mg.append(small[1:2])
        ct.append(own_channels(small[2:7]))
        taps = small[7:22].reshape(3, 5, features).transpose(1, 2, 0).reshape(5, 3 * features)
        st.append(own_channels(taps))

    scalars = jnp.concatenate([split, core[None].astype(jnp.int32)])
    normed = (norm_parts(stream)[0] * ng[0]).astype(BF)
    kept = []
    for layer in range(layers):
        normed_far = sibling(normed)
        gated, mine, away, branches, q, key, conv, fh, uh = mixer_forward(
            scalars, normed, normed_far, st[layer], ct[layer], mixer_w[layer], decay, fwd, inv
        )
        middle, normed_mlp, pre, out, normed_next = mlp_forward(
            scalars, stream, mine, sibling(away), mixer_w[layer].reshape(2 * features, -1), mg[layer],
            ng[(layer + 1) % layers], gate_ups[layer] + (downs[layer],),
        )
        kept.append((stream, normed, normed_far, gated, branches, q, key, conv, fh, uh, middle, normed_mlp, pre))
        stream, normed = out, normed_next
    activations = swap_rows(stream.astype(BF)[None])

    summed = []
    early = [None] * layers
    for layer in reversed(range(layers)):
        x, normed, normed_far, gated, branches, q, key, conv, fh, uh, middle, normed_mlp, pre = kept[layer]
        d_gu, d_down, d_middle, m_low, d_mg = mlp_backward(
            grad, normed_mlp, middle, mg[layer], pre, gate_ups[layer] + (downs[layer],), layer > 0
        )
        rest, d_normed, d_away, d_st, d_ct = mixer_backward(
            scalars, m_low, sibling(m_low), st[layer], ct[layer], mixer_w[layer], normed, normed_far, gated, branches,
            decay, fwd, inv, q, key, conv, fh, uh,
        )
        d_part, d_ng = norm_back(x, ng[layer], d_normed + sibling(d_away).astype(F32))
        grad = d_middle + d_part

        if layer > 0:
            early[layer] = lax.psum_scatter(d_gu, AXES, scatter_dimension=0, tiled=True)
        summed.append((d_gu, d_down, rest, d_ng, d_mg, d_ct, d_st))
    token_grad = swap_rows(grad[None])
    d_gus, d_downs, rests, *smalls = zip(*summed[::-1])
    d_ng, d_mg, d_ct, d_st = [jnp.stack(x) for x in smalls]
    other = jnp.zeros_like(d_ct)
    d_ct = beside(d_ct, other, 2)
    d_st = d_st.reshape(layers, 5, 3, width)
    d_st = beside(d_st, jnp.zeros_like(d_st), 3).reshape(layers, 5, features, 3)
    d_st = d_st.transpose(0, 3, 1, 2).reshape(layers, 15, features)
    small = jnp.concatenate([d_ng, d_mg, d_ct, d_st, jnp.zeros((layers, LANES - 22, features), F32)], axis=1)
    small = small.astype(BF).transpose(0, 2, 1)
    pieces = [d_gus[0].reshape((2,) + grid + (share, hidden))]
    pieces += [x.reshape((2,) + grid + (hidden // features, share, width)) for x in d_downs]
    pieces += [x.reshape((2,) + grid + (share, 4 * width)) for x in rests]
    pieces.append(small.reshape((2,) + grid + (share, LANES)))
    outs = scatter_grads(pieces, dp_count, 1)

    def joined(x):
        parts = x.shape[-1] // width
        x = jnp.moveaxis(x.reshape(x.shape[:-1] + (parts, width)), 0, -2)
        return x.reshape(x.shape[:-3] + (parts * features,))

    early[0] = outs[0].transpose(1, 0, 2)
    for layer in range(1, layers):
        early[layer] = early[layer].reshape(share, hidden // TILE, 2, TILE).transpose(0, 2, 1, 3)
    g_gu = jnp.stack([x.reshape(share, 2 * hidden) for x in early]).astype(F32)
    g_down = jnp.stack([joined(x.reshape(2, -1, width)) for x in outs[1 : 1 + layers]]).astype(F32)
    rest = outs[1 + layers : 1 + 2 * layers]
    g_in = jnp.stack([joined(x[:, :, : 3 * width]) for x in rest]).astype(F32)
    g_out = jnp.stack([joined(x[:, :, 3 * width :]) for x in rest]).astype(F32)
    small = outs[-1].astype(F32)
    g_ng, g_mg, g_ct = small[:, :, 0], small[:, :, 1], small[:, :, 2:7].transpose(0, 2, 1)
    g_st = small[:, :, 7:22].reshape(layers, share, 3, 5).transpose(0, 3, 1, 2)
    return (
        activations,
        token_grad,
        g_ng,
        g_in,
        g_st.reshape(layers, 5, 3 * share),
        g_ct,
        g_out,
        g_mg,
        g_gu,
        g_down,
    )


def solution(mesh):
    every = ("dp", "seq")
    rows, part = P("dp", "seq", None), P(None, every, None)
    vector, taps = P(None, every), P(None, None, every)
    return jax.shard_map(
        shards,
        mesh=mesh,
        in_specs=(rows, P("dp"), rows, vector, part, taps, taps, part, vector, part, part),
        out_specs=(rows, rows, vector, part, taps, taps, part, vector, part, part),
        check_vma=False,
    )
```

time: 948 us -> 601 us (0.63)
  matrix products: 150 us -> 0 us
  other arithmetic: 114 us -> 29.3 us
  Pallas kernels: 551 us -> 472 us
  local copies, waits for them, and re-layouts: 89.1 us -> 52.3 us
  between operations: 4.24 us -> 16.6 us
    dot_general x34 -> x0, matrix products: 150 us -> none  [dot(): return lax.dot_general(a, b, (dims, ((), ())), preferred_element_type=F32)]
    pallas_call x4 -> x8, Pallas kernels: 118 us -> 205 us  [the longest x4 116 us: local_call(): pl.pallas_call(kernel, out_shape=[jax.ShapeDtypeStruct(shape, dtype) for...]
    pallas_call x2 -> x1, Pallas kernels: 222 us -> 137 us  [gather_weights(): pl.pallas_call(body, out_shape=[jax.ShapeDtypeStruct(x.shape[:1] + grid +...]
    pallas_call x2 -> x1, Pallas kernels: 212 us -> 131 us  [scatter_grads(): pl.pallas_call(body, out_shape=[jax.ShapeDtypeStruct(x.shape[:1] + x.shap...]
    convert_element_type x23 -> x8, other arithmetic: 42.2 us -> 8.12 us  [the longest x1 2.39 us: shards(): grad = swap_rows(cotangent).reshape(rows, features).astype(F32)]
    another operation x8, other arithmetic: 24.1 us -> 1.51 us  [the longest x5 0.75 us: shards(): d_ng, d_mg, d_ct, d_st = [jnp.stack(x) for x in smalls]]
    slice x23 -> x19, local copies, waits for them, and re-layouts: 29.2 us -> 11.7 us  [the longest x4 3.32 us: shards(): ng.append(small[0:1])]
    select_n x6 -> x0, other arithmetic: 12.5 us -> none  [beside(): jnp.where(core == 0, jnp.concatenate([own, other], axis=axis), jnp.concat...]
  transfers between devices with their start and end apart: 13 -> 15, of which waited for: 1 -> 3; matrix products, arithmetic and copies ran while one was open for 17% -> 11% of each run, Pallas kernels for 30% -> 49%
where the time goes in v2:
time: 601 us; the launch traced here: 594 us
  Pallas kernels  472 us (79%)
  local copies, waits for them, and re-layouts  52.3 us (9%)
  other arithmetic  29.3 us (5%)
  between operations  16.6 us (3%)
  starting transfers between devices  16 us (3%)
  waiting for transfers between devices  7.62 us (1%)
    pallas_call x1, Pallas kernels, gather_weights(): pl.pallas_call(body, out_shape=[jax.ShapeDtypeStruct(x.shape[:1] + grid +...  137 us
    pallas_call x1, Pallas kernels, scatter_grads(): pl.pallas_call(body, out_shape=[jax.ShapeDtypeStruct(x.shape[:1] + x.shap...  131 us
    pallas_call x4, Pallas kernels, local_call(): pl.pallas_call(kernel, out_shape=[jax.ShapeDtypeStruct(shape, dtype) for...  116 us
    pallas_call x2, Pallas kernels, mlp_backward(): pl.pallas_call(mlp_backward_kernel, grid=(hidden // TILE,), out_shape=[ja...  53.1 us
    pallas_call x2, Pallas kernels, mlp_forward(): pl.pallas_call(mlp_forward_kernel, grid=(hidden // TILE,), out_shape=[jax...  35.5 us
    ppermute x5, starting transfers between devices, swap_rows(): return jnp.where(core == seq, x, lax.ppermute(x, AXES, swap))  14.2 us
  transfers between devices with their start and end apart: 15, of which 3 were waited for; matrix products, arithmetic and copies ran while one was open for 11% of the time, Pallas kernels for 49%

profile of v2, /device:TPU:1, one launch (start us, length us, event | category | flops | bytes accessed | tf_op | source)
XLA Modules:
  0.0 593.7 jit_solution(2609829915352089692)
XLA Ops:
  7.2 1.8 fusion.10
  13.7 136.6 %shard_map.204 = (bf16[2,2,2,2,2,2,24,3072]{7,6,5,4,3,2,1,0:T(8,128)(2,1)}, bf16[2,2,2,2,2,2,4,24,384]{8,7,6,5,4,3,2,1,0:T(8,128)(2,1)}, bf16[2,2,2,2,2,2,4,24,3...) custom-call(bf16[2,24,3072]{2,1,0:T(8,128)(2,1)} %bitcast.176, ...), custom_call_target="tpu_custom_call" | custom-call | tf_op jit(solution)/shard_map/pallas_call | solution.py:569
  150.4 1.9 collective-permute-start
  152.3 3.6 collective-permute-start.1
  162.7 5.4 collective-permute-done.1
  168.2 1.4 convert_reduce_fusion
  171.6 1.5 multiply_bitcast_fusion.decay_hbm
  175.2 22.8 %shard_map.205 = (bf16[1024,384]{1,0:T(8,128)(2,1)}, bf16[512,384]{1,0:T(8,128)(2,1)}, bf16[512,384]{1,0:T(8,128)(2,1)}, bf16[1024,1152]{1,0:T(8,128)(2,1)}, bf1...) custom-call(s32[2]{0:T(128)} %pad_add_fusion.scalar_ref, ...), custom_call_target="tpu_custom_call" | custom-call | tf_op jit(solution)/shard_map/pallas_call | solution.py:365
  200.9 1.3 convert_bitcast_fusion.x_ref
  203.0 17.8 %shard_map.206 = (f32[512,768]{1,0:T(8,128)}, bf16[512,768]{1,0:T(8,128)(2,1)}, bf16[2,512,3072]{2,1,0:T(8,128)(2,1)}, f32[512,768]{1,0:T(8,128)}, bf16[512,768]{1,0:T(8,128)(2,1)}) custom-call(s32[2]{0:T(128)} %pad_add_fusion.scalar_ref, f32[512,768]{1,0:T(8,128)} %convert_bitcast_fusion.x_ref, bf16[512,384]{1,0:T(8,128)(2,1)} %get-tuple-element.70.g0_ref, ...), custom_call_target="tpu_custom_call" | custom-call | tf_op jit(solution)/shard_map/pallas_call | solution.py:802
  220.9 3.3 collective-permute-start.7
  226.1 1.5 copy.186
  227.5 1.7 reshape_reshape.28
  233.5 22.5 %shard_map.207 = (bf16[1024,384]{1,0:T(8,128)(2,1)}, bf16[512,384]{1,0:T(8,128)(2,1)}, bf16[512,384]{1,0:T(8,128)(2,1)}, bf16[1024,1152]{1,0:T(8,128)(2,1)}, bf1...) custom-call(s32[2]{0:T(128)} %pad_add_fusion.scalar_ref, ...), custom_call_target="tpu_custom_call" | custom-call | tf_op jit(solution)/shard_map/pallas_call | solution.py:365
  257.6 2.4 bitcast_convert_fusion.g_ref
  260.7 17.7 %shard_map.208 = (f32[512,768]{1,0:T(8,128)}, bf16[512,768]{1,0:T(8,128)(2,1)}, bf16[2,512,3072]{2,1,0:T(8,128)(2,1)}, f32[512,768]{1,0:T(8,128)}, bf16[512,768]{1,0:T(8,128)(2,1)}) custom-call(s32[2]{0:T(128)} %pad_add_fusion.scalar_ref, f32[512,768]{1,0:T(8,128)} %get-tuple-element.75.x_ref, bf16[512,384]{1,0:T(8,128)(2,1)} %get-tuple-element.77.g0_ref, ...), custom_call_target="tpu_custom_call" | custom-call | tf_op jit(solution)/shard_map/pallas_call | solution.py:802
  278.4 26.4 %shard_map.209 = (bf16[768,6144]{1,0:T(8,128)(2,1)}, bf16[2,3072,384]{2,1,0:T(8,128)(2,1)}, f32[512,768]{1,0:T(8,128)}, bf16[512,768]{1,0:T(8,128)(2,1)}, f32[1,768]{1,0:T(1,128)}) custom-call(f32[512,768]{1,0:T(8,128)} %bitcast_convert_fusion.g_ref, bf16[512,768]{1,0:T(8,128)(2,1)} %get-tuple-element.82.hm_ref, f32[512,768]{1,0:T(8,128)} %get-tuple-element.83.mid_ref, ...), custom_call_target="tpu_custom_call" | custom-call | tf_op jit(solution)/shard_map/pallas_call | solution.py:820
  306.7 1.9 collective-permute-done.8.mid_other_ref
  308.5 35.4 %shard_map.210 = (bf16[2,768,1536]{2,1,0:T(8,128)(2,1)}, f32[512,768]{1,0:T(8,128)}, bf16[512,768]{1,0:T(8,128)(2,1)}, f32[5,1152]{1,0:T(8,128)}, f32[5,384]{1,0:T(8,128)}) custom-call(s32[2]{0:T(128)} %pad_add_fusion.scalar_ref, bf16[512,768]{1,0:T(8,128)(2,1)} %get-tuple-element.86.mid_own_ref, bf16[512,768]{1,0:T(8,128)(2,1)} %collective-permute-done.8.mid_other_ref, ...), custom_call_target="tpu_custom_call" | custom-call | tf_op jit(solution)/shard_map/pallas_call | solution.py:365
  346.3 1.9 collective-permute-start.6
  349.7 1.7 multiply_add_fusion.g_ref
  351.4 26.7 %shard_map.211 = (bf16[2,768,3072]{2,1,0:T(8,128)(2,1)}, bf16[2,3072,384]{2,1,0:T(8,128)(2,1)}, f32[512,768]{1,0:T(8,128)}, bf16[512,768]{1,0:T(8,128)(2,1)}, f32[1,768]{1,0:T(1,128)}) custom-call(f32[512,768]{1,0:T(8,128)} %multiply_add_fusion.g_ref, bf16[512,768]{1,0:T(8,128)(2,1)} %get-tuple-element.96.hm_ref, f32[512,768]{1,0:T(8,128)} %get-tuple-element.97.mid_ref, ...), custom_call_target="tpu_custom_call" | custom-call | tf_op jit(solution)/shard_map/pallas_call | solution.py:820
  378.3 2.1 broadcast_select_fusion.1
  381.6 35.3 %shard_map.212 = (bf16[2,768,1536]{2,1,0:T(8,128)(2,1)}, f32[512,768]{1,0:T(8,128)}, bf16[512,768]{1,0:T(8,128)(2,1)}, f32[5,1152]{1,0:T(8,128)}, f32[5,384]{1,0:T(8,128)}) custom-call(s32[2]{0:T(128)} %pad_add_fusion.scalar_ref, bf16[512,768]{1,0:T(8,128)(2,1)} %get-tuple-element.100.mid_own_ref, bf16[512,768]{1,0:T(8,128)(2,1)} %copy-done.13, ...), custom_call_target="tpu_custom_call" | custom-call | tf_op jit(solution)/shard_map/pallas_call | solution.py:365
  420.5 2.9 multiply_reduce_fusion.1
  424.1 3.4 collective-permute-start.12
  428.2 4.9 reshape.265
  433.1 1.5 copy.192
  436.1 3.2 concatenate.37
  439.2 130.7 %shard_map.213 = (bf16[2,24,3072]{2,1,0:T(8,128)(2,1)}, bf16[2,4,24,384]{3,2,1,0:T(8,128)(2,1)}, bf16[2,4,24,384]{3,2,1,0:T(8,128)(2,1)}, bf16[2,24,1536]{2,1,0:...) custom-call(bf16[2,2,2,2,2,2,24,3072]{7,6,5,4,3,2,1,0:T(8,128)(2,1)} %bitcast.168, ...), custom_call_target="tpu_custom_call" | custom-call | tf_op jit(solution)/shard_map/pallas_call | solution.py:664
  581.2 2.7 broadcast_select_fusion
  584.0 1.2 reshape.274
  (221 shorter events, 51.9 us)
Async XLA Ops:
  7.2 252.8 %all-gather.3.cloned.1.call-start = ((), (), s32[]{:S(2)}) async-start(), calls=%async_computation.2 | async-start | bytes 9732096 | tf_op jit(solution)/shard_map/all_gather | solution.py:916
  9.1 3.1 copy-start.32
  9.1 3.2 copy-start.30
  9.1 3.3 copy-start.22
  9.3 3.1 copy-start.19
  12.5 139.8 %copy-start.14 = (bf16[1,512,768]{2,1,0:T(8,128)(2,1)S(1)}, bf16[1,512,768]{2,1,0:T(8,128)(2,1)}, u32[]{:S(2)}) copy-start(bf16[1,512,768]{2,1,0:T(8,128)(2,1)} %param.13) | copy-start | bytes 2359300
  150.4 433.6 %reduce-scatter.2.cloned.1.call-start = ((), (), s32[]{:S(2)}) async-start(), calls=%async_computation.1 | async-start | bytes 9732096 | tf_op jit(solution)/shard_map/reduce_scatter | solution.py:957
  150.4 22.6 %collective-permute-start = (s32[1]{0:T(128)}, s32[1]{0:T(128)}, u32[]{:S(2)}, u32[]{:S(2)}) collective-permute-start(s32[1]{0:T(128)} %param.14), channel_id=1, source_target_pairs={{1,2},{2,1},{5,6},{6,5},{9,10},{10,9},{13,14},{14,13},{17,18},{18,... | collective-permute-start | bytes 20 | tf_op jit(solution)/shard_map/ppermute | solution.py:858
  152.3 15.8 %collective-permute-start.1 = (bf16[1,512,768]{2,1,0:T(8,128)(2,1)S(1)}, bf16[1,512,768]{2,1,0:T(8,128)(2,1)}, u32[]{:S(2)}, u32[]{:S(2)}) collective-permute-start(bf16[1,512,768]{2,1,0:T(8,128)(2,1)S(1)} %copy-done.14), channel_id=1, source_target_pairs={{1,2},{2,1},{5,6},{6,5},{9,10},{10,9},{13,14},{14,13},{17,18},{18,... | collective-permute-start | bytes 2359304 | tf_op jit(solution)/shard_map/ppermute | solution.py:858
  170.3 4.0 copy-start.1
  170.3 4.0 collective-permute-start.2
  198.0 4.2 collective-permute-start.3
  220.8 11.7 %collective-permute-start.4 = (bf16[512,768]{1,0:T(8,128)(2,1)}, bf16[512,768]{1,0:T(8,128)(2,1)S(1)}, u32[]{:S(2)}, u32[]{:S(2)}) collective-permute-start(bf16[512,768]{1,0:T(8,128)(2,1)} %get-tuple-element.76.own_ref.own_hbm), channel_id=1, source_target_pairs={{0,2},{2,0},{4,6},{6,4},{8,10},{10,8},{12,14},{14,12},{16,18},{18,... | collective-permute-start | bytes 2359304 | tf_op jit(solution)/shard_map/ppermute | solution.py:861
  220.9 36.7 %collective-permute-start.7 = (bf16[1,512,768]{2,1,0:T(8,128)(2,1)}, bf16[1,512,768]{2,1,0:T(8,128)(2,1)}, u32[]{:S(2)}, u32[]{:S(2)}) collective-permute-start(bf16[1,512,768]{2,1,0:T(8,128)(2,1)} %param.15), channel_id=1, source_target_pairs={{1,2},{2,1},{5,6},{6,5},{9,10},{10,9},{13,14},{14,13},{17,18},{18,... | collective-permute-start | bytes 2359304 | tf_op jit(solution)/shard_map/ppermute | solution.py:858
  233.5 22.6 %copy-start.9 = (f32[1,768]{0,1:T(8,128)S(1)}, f32[1,768]{0,1:T(8,128)}, u32[]{:S(2)}) copy-start(f32[1,768]{0,1:T(8,128)} %get-tuple-element.193) | copy-start | bytes 9220
  233.5 23.4 %copy-start.8 = (f32[1,768]{0,1:T(8,128)S(1)}, f32[1,768]{0,1:T(8,128)}, u32[]{:S(2)}) copy-start(f32[1,768]{0,1:T(8,128)} %get-tuple-element.195) | copy-start | bytes 9220
  256.0 3.9 collective-permute-start.5
  306.0 2.5 collective-permute-start.8
  343.9 4.4 collective-permute-start.9
  344.6 3.7 copy-start.5
  346.3 31.9 %collective-permute-start.6 = (bf16[1,512,768]{2,1,0:T(8,128)(2,1)}, bf16[1,512,768]{2,1,0:T(8,128)(2,1)}, u32[]{:S(2)}, u32[]{:S(2)}) collective-permute-start(bf16[1,512,768]{2,1,0:T(8,128)(2,1)} %convert_bitcast_fusion.1), channel_id=1, source_target_pairs={{1,2},{2,1},{5,6},{6,5},{9,10},{10,9},{13,14},{14,13},{17,18},{18,... | collective-permute-start | bytes 2359304 | tf_op jit(solution)/shard_map/ppermute | solution.py:858
  351.4 26.8 %copy-start.26 = (f32[1,768]{1,0:T(1,128)S(1)}, f32[1,768]{1,0:T(1,128)}, u32[]{:S(2)}) copy-start(f32[1,768]{1,0:T(1,128)} %get-tuple-element.116) | copy-start | bytes 9220
  351.4 26.8 %copy-start.23 = (f32[5,1152]{1,0:T(8,128)S(1)}, f32[5,1152]{1,0:T(8,128)}, u32[]{:S(2)}) copy-start(f32[5,1152]{1,0:T(8,128)} %get-tuple-element.120) | copy-start | bytes 69124
  351.4 26.8 %copy-start.3 = (f32[512,768]{1,0:T(8,128)S(1)}, f32[512,768]{1,0:T(8,128)}, u32[]{:S(2)}) copy-start(f32[512,768]{1,0:T(8,128)} %get-tuple-element.81) | copy-start | bytes 4718596
  378.1 2.6 collective-permute-start.10
  381.6 35.4 %copy-start.27 = (f32[1,768]{1,0:T(1,128)S(1)}, f32[1,768]{1,0:T(1,128)}, u32[]{:S(2)}) copy-start(f32[1,768]{1,0:T(1,128)} %get-tuple-element.115) | copy-start | bytes 9220
  381.6 36.4 %copy-start.24 = (f32[5,384]{1,0:T(8,128)S(1)}, f32[5,384]{1,0:T(8,128)}, u32[]{:S(2)}) copy-start(f32[5,384]{1,0:T(8,128)} %get-tuple-element.118) | copy-start | bytes 23044
  416.9 3.6 collective-permute-start.11
  424.1 157.1 %collective-permute-start.12 = (f32[1,512,768]{2,1,0:T(8,128)S(1)}, f32[1,512,768]{2,1,0:T(8,128)}, u32[]{:S(2)}, u32[]{:S(2)}) collective-permute-start(f32[1,512,768]{2,1,0:T(8,128)S(1)} %add_bitcast_fusion), channel_id=1, source_target_pairs={{1,2},{2,1},{5,6},{6,5},{9,10},{10,9},{13,14},{14,13},{17,18},{18,... | collective-permute-start | bytes 4718600 | tf_op jit(solution)/shard_map/ppermute | solution.py:858
  569.9 7.2 %copy-start.18 = (bf16[2,24,3072]{2,1,0:T(8,128)(2,1)S(1)}, bf16[2,24,3072]{2,1,0:T(8,128)(2,1)}, u32[]{:S(2)}) copy-start(bf16[2,24,3072]{2,1,0:T(8,128)(2,1)} %get-tuple-element.124) | copy-start | bytes 884740
  572.5 5.2 copy-start.21
  573.6 4.4 copy-start.20
  (16 other events, 29.7 us)
Sparse Core Ops, SparseCore 0:
  150.5 83.0 all-gather.2
  305.0 135.0 reduce-scatter.1

commit v3 on v2

--- a/solution.py
+++ b/solution.py
@@ -17,9 +17,9 @@
 VMEM_LIMIT = 60 * 2**20
 STRIP = 128
 LANES = 128
-BINS = 448
+BINS = 224
 ROWS = 256
-CHUNK = 64
+CHUNK = 128
 
 
 def transform_matrix(length):
@@ -78,13 +78,29 @@
             body(row0, [None] * 5)
 
 
-def weigh(rows, w_ref, cols, flip):
+def tap_loads(layer, core, ch_hbm, st_hbm, ct_ref, st_ref):
+    width = ct_ref.shape[0]
+    own = pl.multiple_of(core * width, STRIP)
+    pairs = [(ch_hbm.at[layer, pl.ds(own, width), :], ct_ref)]
+    for part in range(3):
+        rows = pl.ds(pl.multiple_of(part * 2 * width + own, STRIP), width)
+        pairs.append((st_hbm.at[layer, rows, :], st_ref.at[pl.ds(part * width, width), :]))
+    return pairs
+
+
+def weigh(rows, w_ref, base, cols, flip):
     total = None
     for off, x in enumerate(rows):
-        tap = 4 - off if flip else off
+        tap = base + (4 - off if flip else off)
         term = x * w_ref[tap : tap + 1, cols]
         total = term if total is None else total + term
     return total
+
+
+def by_corner(split, length, body):
+    for corner in range(length // ROWS):
+        spans = (slice(0, (corner + 1) * ROWS), slice(corner * ROWS, length))
+        pl.when(split // ROWS == corner)(functools.partial(body, spans))
 
 
 def clear_ends(ref, length):
@@ -100,10 +116,10 @@
 
 
 def mixer_forward_kernel(
-    scalar_ref, own_ref, other_ref, sw_ref, cw_ref, iw_hbm, decay_hbm, fwd_hbm, inv_hbm,
+    layer, scalar_ref, own_ref, other_ref, ch_hbm, st_hbm, iw_hbm, decay_hbm, fwd_hbm, inv_hbm,
     gated_ref, mine_ref, send_ref, br_hbm, q_hbm, key_hbm, conv_hbm, fh_hbm, uh_hbm,
     iw_ref, decay_ref, fwd_ref, inv_ref, br_ref, q_ref, key_ref, conv_ref, fh_ref, uh_ref,
-    pad, kpad, filt, u, prod, in_sems, out_sems,
+    ct_ref, st_ref, cw_ref, sw_ref, pad, kpad, filt, u, prod, in_sems, out_sems,
 ):
     length, width = q_ref.shape
     rows_own = own_ref.shape[0]
@@ -116,7 +132,8 @@
             (decay_hbm, decay_ref),
             (fwd_hbm, fwd_ref),
             (inv_hbm, inv_ref),
-        ],
+        ]
+        + tap_loads(layer, core, ch_hbm, st_hbm, ct_ref, st_ref),
         in_sems,
     )
     outs = [(br_ref, br_hbm), (q_ref, q_hbm), (key_ref, key_hbm), (fh_ref, fh_hbm), (uh_ref, uh_hbm), (conv_ref, conv_hbm)]
@@ -134,6 +151,10 @@
             pad[pl.ds(row0 + 8, ROWS), :] = low.astype(F32)
 
     stores[0].start()
+    for copy in loads[4:]:
+        copy.wait()
+    cw_ref[...] = ct_ref[...].astype(F32).T
+    sw_ref[...] = st_ref[...].astype(F32).T
 
     def mix(row0, same):
         rows = pl.ds(row0, CHUNK)
@@ -142,7 +163,7 @@
             for strip in range(strips):
                 cols = pl.ds(part * width + strip * STRIP, STRIP)
                 own = pl.ds(strip * STRIP, STRIP)
-                low = weigh(shifted(pad, row0, cols, same), sw_ref, cols, False).astype(BF)
+                low = weigh(shifted(pad, row0, cols, same), sw_ref, 0, cols, False).astype(BF)
                 if part == 0:
                     q_ref[rows, own] = low
                 elif part == 1:
@@ -162,27 +183,29 @@
         rows = pl.ds(row0, CHUNK)
         for strip in range(strips):
             cols = pl.ds(strip * STRIP, STRIP)
-            total = weigh(shifted(kpad, row0, cols, same), cw_ref, cols, False)
+            total = weigh(shifted(kpad, row0, cols, same), cw_ref, 2, cols, False)
             filt[rows, cols] = (total * decay_ref[rows, cols]).astype(BF)
 
     over_chunks(length, split, make_filter)
     scale = 1.0 / half
     loads[2].wait()
 
-    @pl.loop(0, half // BINS)
-    def _(i):
-        rows = pl.ds(pl.multiple_of(i * 2 * BINS, 2 * BINS), 2 * BINS)
-        f = dot(fwd_ref[rows, pl.ds(0, half)], filt[pl.ds(0, half), :])
-        fr, fi = f[:BINS], f[BINS:]
-        fh_ref[rows, :] = f.astype(BF)
-        for m in range(2):
-            s = dot(fwd_ref[rows, :], u[m])
-            uh_ref[m, rows, :] = s.astype(BF)
-            sr, si = s[:BINS], s[BINS:]
-            prod[m, rows, :] = jnp.concatenate(
-                [(fr * sr - fi * si) * scale, (fr * si + fi * sr) * scale], axis=0
-            ).astype(BF)
-
+    def transform(spans):
+        @pl.loop(0, half // BINS)
+        def _(i):
+            rows = pl.ds(pl.multiple_of(i * 2 * BINS, 2 * BINS), 2 * BINS)
+            f = dot(fwd_ref[rows, 0:half], filt[0:half, :])
+            fr, fi = f[:BINS], f[BINS:]
+            fh_ref[rows, :] = f.astype(BF)
+            for m in range(2):
+                s = dot(fwd_ref[rows, spans[m]], u[m, spans[m], :])
+                uh_ref[m, rows, :] = s.astype(BF)
+                sr, si = s[:BINS], s[BINS:]
+                prod[m, rows, :] = jnp.concatenate(
+                    [(fr * sr - fi * si) * scale, (fr * si + fi * sr) * scale], axis=0
+                ).astype(BF)
+
+    by_corner(split, length, transform)
     stores[3].start()
     stores[4].start()
     corner = split // ROWS
@@ -210,11 +233,12 @@
 
 
 def mixer_backward_kernel(
-    scalar_ref, mid_own_ref, mid_other_ref, sw_ref, cw_ref,
+    layer, scalar_ref, mid_own_ref, mid_other_ref, dmg_ref, ch_hbm, st_hbm,
     w_hbm, own_hbm, other_hbm, gated_hbm, br_hbm, decay_hbm, fwd_hbm, inv_hbm, q_hbm, key_hbm, conv_hbm, fh_hbm, uh_hbm,
-    rest_ref, dn_ref, dn_send_ref, dsw_ref, dcw_ref,
+    rest_ref, dn_ref, dn_send_ref, dch_ref, dst_ref,
     ow_ref, iw_ref, own_ref, other_ref, gated_ref, br_ref, decay_ref, fwd_ref, inv_ref, q_ref, key_ref, conv_ref, fh_ref,
-    uh_ref, pad, epad, kpad, g, prod, mid_ref, dbr_ref, dsw_sum, dcw_sum, in_sems,
+    uh_ref, ct_ref, st_ref, cw_ref, sw_ref, pad, epad, kpad, g, prod, mid_ref, dbr_ref, dsw_sum, dcw_sum, ch_rows, st_rows,
+    in_sems,
 ):
     length, width = q_ref.shape
     rows_own, features = own_ref.shape
@@ -243,7 +267,8 @@
             (own_hbm, own_ref),
             (other_hbm, other_ref),
             (w_hbm.at[core, :, pl.ds(0, 3 * width)], iw_ref),
-        ],
+        ]
+        + tap_loads(layer, core, ch_hbm, st_hbm, ct_ref, st_ref),
         in_sems,
     )
     mid_ref[near, :] = mid_own_ref[...]
@@ -253,6 +278,11 @@
     clear_ends(kpad, length)
     dsw_sum[...] = jnp.zeros(dsw_sum.shape, F32)
     dcw_sum[...] = jnp.zeros(dcw_sum.shape, F32)
+    ch_rows[...] = jnp.zeros(ch_rows.shape, F32)
+    st_rows[...] = jnp.zeros(st_rows.shape, F32)
+    for p in range(3):
+        rows = pl.ds(pl.multiple_of(p * features + (1 - core) * width, STRIP), width)
+        dst_ref[rows, :] = jnp.zeros((width, LANES), BF)
     rest_ref[1 - core, :, pl.ds(0, 3 * width)] = jnp.zeros((features, 3 * width), BF)
     for h in range(2):
         rest_ref[h, apart, out_cols] = jnp.zeros((width, width), BF)
@@ -275,25 +305,29 @@
     for copy in loads[4:7]:
         copy.wait()
 
-    @pl.loop(0, half // BINS)
-    def _(i):
-        rows = pl.ds(pl.multiple_of(i * 2 * BINS, 2 * BINS), 2 * BINS)
-        f = fh_ref[rows, :].astype(F32)
-        fr, fi = f[:BINS], f[BINS:]
-        er = None
-        for m in range(2):
-            s = dot(fwd_ref[rows, :], g[m])
-            sr, si = s[:BINS], s[BINS:]
-            prod[m, rows, :] = jnp.concatenate(
-                [(fr * sr + fi * si) * scale, (fr * si - fi * sr) * scale], axis=0
-            ).astype(BF)
-            w = uh_ref[m, rows, :].astype(F32)
-            wr, wi = w[:BINS], w[BINS:]
-            tr = wr * sr + wi * si
-            ti = wr * si - wi * sr
-            er, ei = (tr, ti) if er is None else (er + tr, ei + ti)
-        prod[2, rows, :] = jnp.concatenate([er * scale, ei * scale], axis=0).astype(BF)
-
+    def transform(spans):
+        @pl.loop(0, half // BINS)
+        def _(i):
+            rows = pl.ds(pl.multiple_of(i * 2 * BINS, 2 * BINS), 2 * BINS)
+            f = fh_ref[rows, :].astype(F32)
+            fr, fi = f[:BINS], f[BINS:]
+            er = None
+            for m in range(2):
+                s = dot(fwd_ref[rows, spans[m]], g[m, spans[m], :])
+                sr, si = s[:BINS], s[BINS:]
+                prod[m, rows, 0:width] = jnp.concatenate(
+                    [(fr * sr + fi * si) * scale, (fr * si - fi * sr) * scale], axis=0
+                ).astype(BF)
+                w = uh_ref[m, rows, :].astype(F32)
+                wr, wi = w[:BINS], w[BINS:]
+                tr = wr * sr + wi * si
+                ti = wr * si - wi * sr
+                er, ei = (tr, ti) if er is None else (er + tr, ei + ti)
+            e = jnp.concatenate([er * scale, ei * scale], axis=0).astype(BF)
+            for m in range(2):
+                prod[m, rows, width : 2 * width] = e
+
+    by_corner(split, length, transform)
     corner = split // ROWS
     value_cols = pl.ds(2 * width, width)
     for copy in loads[7:10]:
@@ -306,27 +340,31 @@
         rows = pl.ds(row0, ROWS)
         spot = pl.ds(row0 + 8, ROWS)
         pick = (i > corner).astype(jnp.int32)
-        pad[spot, value_cols] = dot(inv_ref[rows, :], prod[pick])
+        both = dot(inv_ref[rows, :], prod[pick])
+        pad[spot, value_cols] = both[:, :width]
 
         @pl.when(i == corner)
         def _():
             later = i * ROWS + lax.broadcasted_iota(jnp.int32, (ROWS, width), 0) >= split
-            other = dot(inv_ref[rows, :], prod[1])
+            other = dot(inv_ref[rows, :], prod[1, :, 0:width])
             pad[spot, value_cols] = jnp.where(later, other, pad[spot, value_cols])
 
         inside = row0 + lax.broadcasted_iota(jnp.int32, (ROWS, width), 0) < half
-        d_filt = dot(inv_ref[rows, :], prod[2])
-        epad[spot, :] = jnp.where(inside, d_filt, 0.0) * decay_ref[rows, :]
+        epad[spot, :] = jnp.where(inside, both[:, width:], 0.0) * decay_ref[rows, :]
 
     def key_taps(row0, same):
         spot = pl.ds(row0 + 8, CHUNK)
         for strip in range(strips):
             cols = pl.ds(strip * STRIP, STRIP)
             e = epad[spot, cols]
-            pad[spot, pl.ds(width + strip * STRIP, STRIP)] = weigh(shifted(epad, row0, cols, same), cw_ref, cols, True)
+            pad[spot, pl.ds(width + strip * STRIP, STRIP)] = weigh(shifted(epad, row0, cols, same), cw_ref, 2, cols, True)
             for off, x in enumerate(shifted(kpad, row0, cols, same)):
                 dcw_sum[off, :, cols] += (x * e).reshape(CHUNK // 8, 8, STRIP).sum(0)
 
+    for copy in loads[15:]:
+        copy.wait()
+    cw_ref[...] = ct_ref[...].astype(F32).T
+    sw_ref[...] = st_ref[...].astype(F32).T
     over_chunks(length, split, key_taps)
     loads[10].wait()
 
@@ -337,26 +375,30 @@
 
         def branch_taps(row0, same):
             e = pad[pl.ds(row0 + 8, CHUNK), cols]
-            total = weigh(shifted(pad, row0, cols, same), sw_ref, cols, True)
+            total = weigh(shifted(pad, row0, cols, same), sw_ref, 0, cols, True)
             dbr_ref[pl.ds(row0, CHUNK), cols] = total.astype(BF)
             for off, x in enumerate(shifted(kpad, row0, pl.ds(0, STRIP), same)):
                 dsw_sum[off, :, cols] += (x * e).reshape(CHUNK // 8, 8, STRIP).sum(0)
 
         over_chunks(length, split, branch_taps)
 
-    dsw_ref[...] = jnp.sum(dsw_sum[...], axis=1)
-    dcw_ref[...] = jnp.sum(dcw_sum[...], axis=1)
-    for copy in loads[11:]:
+    ch_rows[1:2, :] = dmg_ref[...]
+    st_rows[0:5, :] = jnp.sum(dsw_sum[...], axis=1)
+    ch_rows[2:7, part] = jnp.sum(dcw_sum[...], axis=1)
+    dch_ref[...] = ch_rows[...].T.astype(BF)
+    for p in range(3):
+        rows = pl.ds(pl.multiple_of(p * features + core * width, STRIP), width)
+        dst_ref[rows, :] = st_rows[:, p * width : (p + 1) * width].T.astype(BF)
+    for copy in loads[11:15]:
         copy.wait()
     d_out = dot(gated_ref[...], mid_ref[...], ((0,), (0,))).astype(BF)
     for h in range(2):
         rest_ref[h, part, out_cols] = d_out[:, h * width : (h + 1) * width]
-    for p in range(3):
-        cols = pl.ds(p * width, width)
+    for cols in (pl.ds(0, 2 * width), pl.ds(2 * width, width)):
         d_in = dot(own_ref[...], dbr_ref[near, cols], ((0,), (0,)))
         d_in += dot(other_ref[...], dbr_ref[far, cols], ((0,), (0,)))
         rest_ref[core, :, cols] = d_in.astype(BF)
-    dn_ref[...] = dot(dbr_ref[near, :], iw_ref[...], ((1,), (1,)))
+    dn_ref[...] = dot(dbr_ref[near, :], iw_ref[...], ((1,), (1,))).astype(BF)
     dn_send_ref[...] = dot(dbr_ref[far, :], iw_ref[...], ((1,), (1,))).astype(BF)
 
 
@@ -374,13 +416,17 @@
     )(*args)
 
 
-def mixer_forward(scalars, own, other, sw, cw, weight, decay, fwd, inv):
+def tap_scratch(width):
+    return [((width, LANES), BF), ((3 * width, LANES), BF), ((LANES, width), F32), ((LANES, 3 * width), F32)]
+
+
+def mixer_forward(layer, scalars, own, other, ch, st, weight, decay, fwd, inv):
     length, width = decay.shape
     features = own.shape[1]
     bins = fwd.shape[0]
     tall, short, wide = (length, width), (own.shape[0], width), (length, 3 * width)
     kept = [(wide, BF), (tall, BF), (tall, BF), (tall, BF), ((bins, width), BF), ((2, bins, width), BF)]
-    scratch = [((features, 3 * width), BF), (tall, F32), (fwd.shape, BF), (inv.shape, BF)] + kept
+    scratch = [((features, 3 * width), BF), (tall, F32), (fwd.shape, BF), (inv.shape, BF)] + kept + tap_scratch(width)
     scratch += [
         ((length + 16, 3 * width), F32),
         ((length + 16, width), F32),
@@ -389,45 +435,49 @@
         ((2, bins, width), BF),
     ]
     return local_call(
-        mixer_forward_kernel,
-        (scalars, own, other, sw, cw, weight, decay, fwd, inv),
-        5,
+        functools.partial(mixer_forward_kernel, layer),
+        (scalars, own, other, ch, st, weight, decay, fwd, inv),
+        3,
         [(tall, BF), (short, BF), (short, BF)] + kept,
         3,
-        [pltpu.VMEM(*x) for x in scratch] + [pltpu.SemaphoreType.DMA((4,)), pltpu.SemaphoreType.DMA((6,))],
+        [pltpu.VMEM(*x) for x in scratch] + [pltpu.SemaphoreType.DMA((8,)), pltpu.SemaphoreType.DMA((6,))],
     )
 
 
-def mixer_backward(scalars, mid_own, mid_other, sw, cw, weight, own, other, gated, br, decay, fwd, inv, q, key, conv, fh, uh):
+def mixer_backward(
+    layer, scalars, mid_own, mid_other, dmg, ch, st, weight, own, other, gated, br, decay, fwd, inv, q, key, conv, fh, uh
+):
     length, width = decay.shape
     bins = fwd.shape[0]
     rows, features = mid_own.shape
     held = (own, other, gated, br, decay, fwd, inv, q, key, conv, fh, uh)
-    scratch = [((2, width, width), BF), ((features, 3 * width), BF)] + [(x.shape, x.dtype) for x in held]
+    scratch = [((2, width, width), BF), ((features, 3 * width), BF)] + [(x.shape, x.dtype) for x in held] + tap_scratch(width)
     scratch += [
         ((length + 16, 3 * width), F32),
         ((length + 16, width), F32),
         ((length + 16, width), F32),
         ((2, length, width), BF),
-        ((3, bins, width), BF),
+        ((2, bins, 2 * width), BF),
         ((length, features), BF),
         ((length, 3 * width), BF),
         ((5, 8, 3 * width), F32),
         ((5, 8, width), F32),
+        ((LANES, features), F32),
+        ((LANES, 3 * width), F32),
     ]
     return local_call(
-        mixer_backward_kernel,
-        (scalars, mid_own, mid_other, sw, cw, weight) + held,
-        5,
+        functools.partial(mixer_backward_kernel, layer),
+        (scalars, mid_own, mid_other, dmg, ch, st, weight) + held,
+        4,
         [
             ((2, features, 4 * width), BF),
-            ((rows, features), F32),
             ((rows, features), BF),
-            ((5, 3 * width), F32),
-            ((5, width), F32),
+            ((rows, features), BF),
+            ((features, LANES), BF),
+            ((3 * features, LANES), BF),
         ],
         5,
-        [pltpu.VMEM(*x) for x in scratch] + [pltpu.SemaphoreType.DMA((15,))],
+        [pltpu.VMEM(*x) for x in scratch] + [pltpu.SemaphoreType.DMA((19,))],
     )
 
 
@@ -459,11 +509,35 @@
     return tuple(fixed[d] if d in fixed else slice(None) for d in range(dims))
 
 
+def across(coords, bits):
+    dp = lax.axis_index("dp")
+    core, seq = coords[bits], coords[bits + 1]
+    return core != seq, (dp + 1 - 2 * core, 1 - seq)
+
+
 def greet(neighbours):
     barrier = pltpu.get_barrier_semaphore()
     for device in neighbours:
         pl.semaphore_signal(barrier, inc=1, device_id=device, device_id_type=pl.DeviceIdType.MESH)
     pl.semaphore_wait(barrier, len(neighbours))
+
+
+class Swap:
+    def __init__(self, src, dst, send, recv, local, moves, partner):
+        self.stays, self.moves = jnp.logical_not(moves), moves
+        self.away = pltpu.make_async_remote_copy(
+            src_ref=src, dst_ref=dst, send_sem=send, recv_sem=recv,
+            device_id=partner, device_id_type=pl.DeviceIdType.MESH,
+        )
+        self.here = pltpu.make_async_copy(src, dst, local)
+
+    def start(self):
+        pl.when(self.moves)(lambda: self.away.start())
+        pl.when(self.stays)(lambda: self.here.start())
+
+    def wait(self):
+        pl.when(self.moves)(lambda: self.away.wait())
+        pl.when(self.stays)(lambda: self.here.wait())
 
 
 def remote(src, dst, send, recv, device):
@@ -476,10 +550,10 @@
 
 
 GATHER_UNITS = (
-    (3, 0, 640, 0, 0), (3, 640, 640, 1, 0), (3, 1280, 384, 2, 0),
+    (3, 0, 640, 0, 0), (3, 640, 512, 1, 0), (3, 1152, 384, 2, 0), (5, 0, 128, 2, 0), (6, 0, 128, 1, 0),
     (0, 0, 768, 0, 1), (0, 768, 768, 1, 1), (2, 2, 2, 2, 1),
     (0, 1536, 768, 0, 2), (0, 2304, 768, 1, 2),
-    (1, 0, 2, 0, 3), (1, 2, 2, 1, 3), (4, 1280, 384, 2, 3),
+    (1, 0, 2, 0, 3), (1, 2, 2, 1, 3), (4, 1280, 256, 2, 3),
     (4, 0, 640, 0, 4), (4, 640, 640, 1, 4),
     (2, 0, 1, 0, 5), (2, 1, 1, 1, 5),
 )
@@ -487,9 +561,9 @@
     (0, 0, 768, 0, 0), (0, 768, 768, 1, 0), (2, 2, 2, 2, 0),
     (0, 1536, 768, 0, 1), (0, 2304, 768, 1, 1), (3, 1280, 256, 2, 1),
     (1, 0, 2, 0, 2), (1, 2, 2, 1, 2), (4, 1280, 256, 2, 2),
-    (3, 0, 640, 0, 3), (3, 640, 640, 1, 3), (5, 0, 128, 2, 3),
-    (4, 0, 640, 0, 4), (4, 640, 640, 1, 4),
-    (2, 0, 1, 0, 5), (2, 1, 1, 1, 5),
+    (3, 0, 640, 0, 3), (3, 640, 640, 2, 3), (5, 0, 128, 2, 3), (6, 0, 128, 2, 3),
+    (4, 0, 640, 0, 4), (4, 640, 640, 1, 4), (7, 0, 128, 2, 4),
+    (2, 0, 1, 0, 5), (2, 1, 1, 0, 5),
 )
 
 
@@ -511,15 +585,20 @@
     return [(i, t) for _, i, t in sorted(due)]
 
 
-def gather_kernel(dp_count, units, own, full, sems):
+def gather_kernel(dp_count, units, rows_in, rows_out, own, full, sems):
     bits, core_dim, _, orders = cube(dp_count)
     dims = bits + 2
     stages = dims - 1
     coords, neighbour = place(bits)
     core = coords[core_dim]
     sibling = neighbour(core_dim)
-    greet([neighbour(d) for d in range(dims)])
-    ici_send, ici_recv, core_send, core_recv, local = sems
+    moves, partner = across(coords, bits)
+    greet([neighbour(d) for d in range(dims)] + [partner])
+    ici_send, ici_recv, core_send, core_recv, local, swap_send, swap_recv, swap_local = sems
+    swaps = [
+        Swap(src, dst, swap_send.at[i], swap_recv.at[i], swap_local.at[i], moves, partner)
+        for i, (src, dst) in enumerate(zip(rows_in, rows_out))
+    ]
     mine = region(dict(enumerate(coords)), dims)
     firsts, forwards, sends = [], [], []
     last = [None] * len(units)
@@ -530,7 +609,10 @@
         keep = pltpu.make_async_copy(piece, here, local.at[u])
         keep.start()
         firsts.append((keep, remote(piece, here, core_send.at[u, 0], core_recv.at[u, 0], sibling)))
-    for u, t in ticks(units, stages, False):
+    for number, (u, t) in enumerate(ticks(units, stages, False)):
+        if number == 10:
+            for swap in swaps:
+                swap.start()
         unit = units[u]
         array, tail, order = unit[0], piece_of(unit, len(own[unit[0]].shape) == 4), orders[unit[3]]
         fixed = {e: coords[e] for e in order[t:]}
@@ -546,15 +628,19 @@
             sends.append(last[u])
         if t > 0:
             forwards.append(remote(got, got, core_send.at[u, t], core_recv.at[u, t], sibling))
+    for swap in swaps:
+        swap.wait()
+    beside = remote(rows_out[0], rows_out[-1], swap_send.at[len(swaps)], swap_recv.at[len(swaps)], sibling)
     for keep, copy in firsts:
         copy.wait_send()
     for copy in forwards:
         copy.wait()
     for copy in sends:
         copy.wait_send()
-
-
-def gather_weights(own, dp_count, number):
+    beside.wait()
+
+
+def gather_weights(rows, own, dp_count, number):
     bits = cube(dp_count)[0]
     stages = bits + 1
     units = GATHER_UNITS
@@ -562,31 +648,70 @@
     count = len(units)
 
     def body(*refs):
-        gather_kernel(dp_count, units, refs[:arrays], refs[arrays : 2 * arrays], refs[2 * arrays :])
+        rows_in, refs = refs[: len(rows)], refs[len(rows) :]
+        own_refs, refs = refs[:arrays], refs[arrays:]
+        rows_out, refs = refs[: len(rows) + 1], refs[len(rows) + 1 :]
+        gather_kernel(dp_count, units, rows_in, rows_out, own_refs, refs[:arrays], refs[arrays:])
 
     grid = (2,) * (bits + 2)
     anywhere = pl.BlockSpec(memory_space=pl.ANY)
     return pl.pallas_call(
         body,
-        out_shape=[jax.ShapeDtypeStruct(x.shape[:1] + grid + x.shape[1:], x.dtype) for x in own],
-        in_specs=[anywhere] * arrays,
-        out_specs=[anywhere] * arrays,
+        out_shape=[jax.ShapeDtypeStruct(x.shape, x.dtype) for x in (*rows, rows[0])]
+        + [jax.ShapeDtypeStruct(x.shape[:1] + grid + x.shape[1:], x.dtype) for x in own],
+        in_specs=[anywhere] * (len(rows) + arrays),
+        out_specs=[anywhere] * (len(rows) + 1 + arrays),
         scratch_shapes=[pltpu.SemaphoreType.DMA((count, stages))] * 2
         + [pltpu.SemaphoreType.DMA((count, stages + 1))] * 2
-        + [pltpu.SemaphoreType.DMA((count,))],
+        + [pltpu.SemaphoreType.DMA((count,))]
+        + [pltpu.SemaphoreType.DMA((len(rows) + 1,))] * 3,
         compiler_params=pltpu.CompilerParams(collective_id=number, has_side_effects=True),
-    )(*own)
-
-
-def scatter_kernel(dp_count, units, grads, outs, held, first, arrived, final, sems):
+    )(*rows, *own)
+
+
+def scatter_kernel(dp_count, units, ends_in, token_ref, grads, outs, held, first, arrived, final, work, sems):
     bits, core_dim, _, orders = cube(dp_count)
     dims = bits + 2
     stages = dims - 1
     coords, neighbour = place(bits)
     core = coords[core_dim]
     sibling = neighbour(core_dim)
-    greet([neighbour(d) for d in range(dims)])
-    ici_send, ici_recv, core_send, core_recv, local = sems
+    moves, partner = across(coords, bits)
+    greet([neighbour(d) for d in range(dims)] + [partner])
+    ici_send, ici_recv, core_send, core_recv, local, end_send, end_recv, end_local = sems
+    x_ref, dn_ref, away_ref, dmid_ref, gain_ref, dng_ref = ends_in
+    other_ref, grad_ref, sum_ref, flat_ref, tall_ref, slab_ref = work
+    grads = list(grads) + [slab_ref]
+    exchange = remote(away_ref, other_ref, end_send.at[0], end_recv.at[0], sibling)
+    begin = pltpu.make_async_copy(dmid_ref, grad_ref, end_local.at[1])
+    begin.start()
+    swap = Swap(grad_ref, token_ref, end_send.at[1], end_recv.at[1], end_local.at[0], moves, partner)
+
+    def finish_rows():
+        exchange.wait()
+        begin.wait()
+        sum_ref[...] = jnp.zeros(sum_ref.shape, F32)
+        share = slab_ref.shape[-2]
+
+        @pl.loop(0, x_ref.shape[0] // 128)
+        def _(i):
+            rows = pl.ds(pl.multiple_of(i * 128, 128), 128)
+            d = dn_ref[rows, :].astype(F32) + other_ref[rows, :].astype(F32)
+            dx, dg = norm_back(x_ref[rows, :].astype(F32), gain_ref[...], d)
+            grad_ref[rows, :] += dx
+            sum_ref[0:1, :] += dg
+
+        swap.start()
+        flat_ref[...] = jnp.zeros(flat_ref.shape, F32)
+        for layer, row in enumerate((sum_ref, dng_ref)):
+            for c in range(tall_ref.shape[0] // LANES):
+                cols = slice(c * LANES, (c + 1) * LANES)
+                flat_ref[0:1, :] = row[0:1, cols]
+                tall_ref[cols, :] = flat_ref[...].T
+            for i in range(2**dims):
+                at = tuple((i >> (dims - 1 - d)) % 2 for d in range(dims))
+                slab_ref[(layer,) + at] = tall_ref[i * share : (i + 1) * share, :].astype(BF)
+
     everything = region({}, dims)
 
     def add(u, fixed, extra):
@@ -601,6 +726,8 @@
     starts, sends = [None] * len(units), []
     last = [None] * len(units)
     for u, t in ticks(units, stages, True):
+        if t < 0 and units[u][0] == len(grads) - 1:
+            finish_rows()
         if t < 0:
             array, tail = units[u][0], piece_of(units[u], len(outs[units[u][0]].shape) == 4)
             load = pltpu.make_async_copy(grads[array].at[(core,) + everything + tail], held[u], local.at[u, 0])
@@ -634,48 +761,63 @@
         other = pltpu.make_async_copy(final[u], outs[array].at[(1 - core,) + tail], local.at[u, 2])
         other.start()
         ends += [own, other]
+    swap.wait()
     for copy in ends:
         copy.wait()
     for copy in sends + last + [s[1] for s in starts]:
         copy.wait_send()
 
 
-def scatter_grads(grads, dp_count, number):
+def scatter_grads(ends, grads, units, dp_count, number):
     bits = cube(dp_count)[0]
     dims = bits + 2
     stages = dims - 1
-    units = SCATTER_UNITS
-    arrays = len(grads)
     count = len(units)
     grid = (2,) * dims
+    rows, features = ends[0].shape
+    share = grads[0].shape[1 + dims]
+    tails = [x.shape[1 + dims :] for x in grads] + [(share, LANES)]
+    arrays = len(tails)
     slabs = []
     for array, _, size, _, _ in units:
-        shape = grads[array].shape[1 + dims :]
+        shape = tails[array]
         slabs.append((size,) + shape[1:] if len(shape) == 3 else shape[:-1] + (size,))
+    work = [((rows, features), BF), ((rows, features), F32), ((8, features), F32), ((LANES, LANES), F32)]
+    work += [((features, LANES), F32), ((2,) + grid + (share, LANES), BF)]
 
     def body(*refs):
-        grads_in, outs, refs = refs[:arrays], refs[arrays : 2 * arrays], refs[2 * arrays :]
+        ends_in, refs = refs[: len(ends)], refs[len(ends) :]
+        grads_in, refs = refs[: len(grads)], refs[len(grads) :]
+        token, outs, refs = refs[0], refs[1 : 1 + arrays], refs[1 + arrays :]
         held, first, final = refs[:count], refs[count : 2 * count], refs[2 * count : 3 * count]
         refs = refs[3 * count :]
         arrived = [refs[u * stages : (u + 1) * stages] for u in range(count)]
-        scatter_kernel(dp_count, units, grads_in, outs, held, first, arrived, final, refs[count * stages :])
-
-    anywhere = pl.BlockSpec(memory_space=pl.ANY)
+        refs = refs[count * stages :]
+        scatter_kernel(
+            dp_count, units, ends_in, token, grads_in, outs, held, first, arrived, final,
+            refs[: len(work)], refs[len(work) :],
+        )
+
+    anywhere, vmem = pl.BlockSpec(memory_space=pl.ANY), pl.BlockSpec(memory_space=pltpu.VMEM)
     return pl.pallas_call(
         body,
-        out_shape=[jax.ShapeDtypeStruct(x.shape[:1] + x.shape[1 + dims :], x.dtype) for x in grads],
-        in_specs=[anywhere] * arrays,
-        out_specs=[anywhere] * arrays,
+        out_shape=[jax.ShapeDtypeStruct((rows, features), F32)]
+        + [jax.ShapeDtypeStruct((2,) + tail, BF) for tail in tails],
+        in_specs=[vmem, vmem, anywhere, anywhere, vmem, vmem] + [anywhere] * len(grads),
+        out_specs=[anywhere] * (1 + arrays),
         scratch_shapes=[pltpu.VMEM(grid + slab, BF) for slab in slabs] * 2
         + [pltpu.VMEM(slab, BF) for slab in slabs]
         + [pltpu.VMEM((2,) * (dims - 1 - t) + slab, BF) for slab in slabs for t in range(stages)]
+        + [pltpu.VMEM(*x) for x in work]
         + [pltpu.SemaphoreType.DMA((count, stages))] * 2
         + [pltpu.SemaphoreType.DMA((count, 2))] * 2
-        + [pltpu.SemaphoreType.DMA((count, 3))],
+        + [pltpu.SemaphoreType.DMA((count, 3))]
+        + [pltpu.SemaphoreType.DMA((2,))] * 2
+        + [pltpu.SemaphoreType.DMA((2,))],
         compiler_params=pltpu.CompilerParams(
             collective_id=number, has_side_effects=True, vmem_limit_bytes=VMEM_LIMIT
         ),
-    )(*grads)
+    )(*ends, *grads)
 
 
 def norm_parts(x):
@@ -703,7 +845,7 @@
 
 
 def mlp_forward_kernel(
-    scalar_ref, x_ref, g0_ref, g1_ref, o0_ref, o1_ref, mg_ref, ng_ref, wg_ref, wu_ref, d0_ref, d1_ref,
+    gain, next_gain, scalar_ref, x_ref, g0_ref, g1_ref, o0_ref, o1_ref, gains_ref, wg_ref, wu_ref, d0_ref, d1_ref,
     mid_ref, hm_ref, pre_ref, out_ref, next_ref,
 ):
     j = pl.program_id(0)
@@ -717,23 +859,27 @@
             mid += dot(ref[...], jnp.concatenate([o0_ref[rows, :], o1_ref[rows, :]], axis=1))
         mid_ref[...] = mid
         out_ref[...] = mid
-        hm_ref[...] = (norm_parts(mid)[0] * mg_ref[...]).astype(BF)
-
-    gate = dot(hm_ref[...], wg_ref[...])
-    up = dot(hm_ref[...], wu_ref[...])
-    pre_ref[0] = gate.astype(BF)
-    pre_ref[1] = up.astype(BF)
-    hid = (gelu_parts(gate)[0] * up).astype(BF)
-    down = jnp.concatenate([d0_ref[...], d1_ref[...]], axis=1)
-    out_ref[...] += dot(hid, down)
+        hm_ref[...] = (norm_parts(mid)[0] * gains_ref[gain : gain + 1, :]).astype(BF)
+
+    hm = hm_ref[...]
+    total = out_ref[...]
+    for i in range(TILE // PART_F):
+        part = slice(i * PART_F, (i + 1) * PART_F)
+        gate = dot(hm, wg_ref[:, part])
+        up = dot(hm, wu_ref[:, part])
+        pre_ref[0, :, part] = gate.astype(BF)
+        pre_ref[1, :, part] = up.astype(BF)
+        hid = (gelu_parts(gate)[0] * up).astype(BF)
+        total += dot(hid, jnp.concatenate([d0_ref[part, :], d1_ref[part, :]], axis=1))
+    out_ref[...] = total
 
     @pl.when(j == pl.num_programs(0) - 1)
     def _():
-        next_ref[...] = (norm_parts(out_ref[...])[0] * ng_ref[...]).astype(BF)
+        next_ref[...] = (norm_parts(out_ref[...])[0] * gains_ref[next_gain : next_gain + 1, :]).astype(BF)
 
 
 def mlp_backward_kernel(
-    g_ref, hm_ref, mid_ref, mg_ref, pre_ref, wg_ref, wu_ref, d0_ref, d1_ref,
+    gain, g_ref, hm_ref, mid_ref, gains_ref, pre_ref, wg_ref, wu_ref, d0_ref, d1_ref,
     dgu_ref, ddn_ref, dmid_ref, mlow_ref, dmg_ref,
     glow, hm_t, acc,
 ):
@@ -746,27 +892,31 @@
         hm_t[...] = hm_ref[...].T
         acc[...] = jnp.zeros(acc.shape, F32)
 
-    down = jnp.concatenate([d0_ref[...], d1_ref[...]], axis=1)
-    dh = dot(glow[...], down, ((1,), (1,)))
-    value, slope = gelu_parts(pre_ref[0].astype(F32))
-    up = pre_ref[1].astype(F32)
-    hid = (value * up).astype(BF)
-    d_gate = (dh * up * slope).astype(BF)
-    d_up = (dh * value).astype(BF)
-    d_down = dot(hid, glow[...], ((0,), (0,))).astype(BF)
-    ddn_ref[0] = d_down[:, :width]
-    ddn_ref[1] = d_down[:, width:]
-    for h, d in enumerate((d_gate, d_up)):
-        grad = dot(hm_t[...], d).astype(BF)
-        if len(dgu_ref.shape) == 3:
-            dgu_ref[h] = grad
-        else:
-            dgu_ref[:, h * TILE : (h + 1) * TILE] = grad
-    acc[...] += dot(d_gate, wg_ref[...], ((1,), (1,))) + dot(d_up, wu_ref[...], ((1,), (1,)))
+    low, hm = glow[...], hm_t[...]
+    total = acc[...]
+    for i in range(TILE // PART_B):
+        part = slice(i * PART_B, (i + 1) * PART_B)
+        dh = dot(low, jnp.concatenate([d0_ref[part, :], d1_ref[part, :]], axis=1), ((1,), (1,)))
+        value, slope = gelu_parts(pre_ref[0, :, part].astype(F32))
+        up = pre_ref[1, :, part].astype(F32)
+        hid = (value * up).astype(BF)
+        d_gate = (dh * up * slope).astype(BF)
+        d_up = (dh * value).astype(BF)
+        d_down = dot(hid, low, ((0,), (0,))).astype(BF)
+        ddn_ref[0, part, :] = d_down[:, :width]
+        ddn_ref[1, part, :] = d_down[:, width:]
+        for h, d in enumerate((d_gate, d_up)):
+            grad = dot(hm, d).astype(BF)
+            if len(dgu_ref.shape) == 3:
+                dgu_ref[h, :, part] = grad
+            else:
+                dgu_ref[:, h * TILE + i * PART_B : h * TILE + (i + 1) * PART_B] = grad
+        total += dot(d_gate, wg_ref[:, part], ((1,), (1,))) + dot(d_up, wu_ref[:, part], ((1,), (1,)))
+    acc[...] = total
 
     @pl.when(j == pl.num_programs(0) - 1)
     def _():
-        dx, dg = norm_back(mid_ref[...], mg_ref[...], acc[...])
+        dx, dg = norm_back(mid_ref[...], gains_ref[gain : gain + 1, :], acc[...])
         dmid = g_ref[...] + dx
         dmid_ref[...] = dmid
         mlow_ref[...] = dmid.astype(BF)
@@ -774,6 +924,8 @@
 
 
 TILE = 512
+PART_F = 512
+PART_B = 512
 
 
 def whole(shape):
@@ -791,25 +943,25 @@
     return [gate_up, up] + down
 
 
-def mlp_forward(scalars, x, g0, g1, weight, mg, ng, weights):
+def mlp_forward(scalars, x, g0, g1, weight, gains, gain, next_gain, weights):
     layout, gu, dn = weights
     rows, features = x.shape
     hidden = dn.shape[0] // 2
-    square, vector = whole((rows, features)), whole((1, features))
+    square = whole((rows, features))
     narrow = [whole(a.shape) for a in (g0, g1)]
     narrow += [pl.BlockSpec((features, features // 2), lambda j, h=h: (h, 3)) for h in range(2)]
     shapes = [((rows, features), F32), ((rows, features), BF), ((2, rows, hidden), BF), ((rows, features), F32), ((rows, features), BF)]
     return pl.pallas_call(
-        mlp_forward_kernel,
+        functools.partial(mlp_forward_kernel, gain, next_gain),
         grid=(hidden // TILE,),
         out_shape=[jax.ShapeDtypeStruct(*s) for s in shapes],
-        in_specs=[pl.BlockSpec(memory_space=pltpu.SMEM), square] + narrow + [vector] * 2 + weight_specs(layout, hidden, features),
+        in_specs=[pl.BlockSpec(memory_space=pltpu.SMEM), square] + narrow + [whole(gains.shape)] + weight_specs(layout, hidden, features),
         out_specs=[square, square, pl.BlockSpec((2, rows, TILE), lambda j: (0, 0, j)), square, square],
         compiler_params=pltpu.CompilerParams(vmem_limit_bytes=VMEM_LIMIT),
-    )(scalars, x, g0, g1, weight, weight, mg, ng, gu, gu, dn, dn)
-
-
-def mlp_backward(g, hm, mid, mg, pre, weights, side_by_side):
+    )(scalars, x, g0, g1, weight, weight, gains, gu, gu, dn, dn)
+
+
+def mlp_backward(g, hm, mid, gains, gain, pre, weights, side_by_side):
     layout, gu, dn = weights
     rows, features = g.shape
     hidden = pre.shape[2]
@@ -818,11 +970,11 @@
     both = (features, 2 * hidden) if side_by_side else (2, features, hidden)
     shapes = [(both, BF), ((2, hidden, width), BF), ((rows, features), F32), ((rows, features), BF), ((1, features), F32)]
     return pl.pallas_call(
-        mlp_backward_kernel,
+        functools.partial(mlp_backward_kernel, gain),
         grid=(hidden // TILE,),
         out_shape=[jax.ShapeDtypeStruct(*s) for s in shapes],
         in_specs=[square] * 3
-        + [vector, pl.BlockSpec((2, rows, TILE), lambda j: (0, 0, j))]
+        + [whole(gains.shape), pl.BlockSpec((2, rows, TILE), lambda j: (0, 0, j))]
         + weight_specs(layout, hidden, features),
         out_specs=[
             pl.BlockSpec((features, 2 * TILE), lambda j: (0, j))
@@ -833,7 +985,7 @@
         ],
         scratch_shapes=[pltpu.VMEM((rows, features), BF), pltpu.VMEM((features, rows), BF), pltpu.VMEM((rows, features), F32)],
         compiler_params=pltpu.CompilerParams(vmem_limit_bytes=VMEM_LIMIT),
-    )(g, hm, mid, mg, pre, gu, gu, dn, dn)
+    )(g, hm, mid, gains, pre, gu, gu, dn, dn)
 
 
 def shards(
@@ -877,9 +1029,6 @@
         x = lax.dynamic_index_in_dim(x, core, x.ndim - 2, keepdims=False)
         return x.reshape(x.shape[:-2] + (parts * width,))
 
-    split = swap_rows(split_points)
-    stream = swap_rows(tokens).reshape(rows, features).astype(F32)
-    grad = swap_rows(cotangent).reshape(rows, features).astype(F32)
     table = transform_matrix(length)
     fwd = jnp.asarray(table, BF)
     inv = jnp.asarray(np.ascontiguousarray(table.T), BF)
@@ -893,47 +1042,36 @@
 
     grid = (2,) * (cube(dp_count)[0] + 2)
 
-    small = jnp.concatenate(
-        [
-            norm_gain[:, :, None],
-            mlp_gain[:, :, None],
-            cond_taps.transpose(0, 2, 1),
-            short_taps.reshape(layers, 5, share, 3).transpose(0, 2, 3, 1).reshape(layers, share, 15),
-        ],
-        axis=2,
-    )
-    small = jnp.pad(small, ((0, 0), (0, 0), (0, LANES - 22)))
+    ch = jnp.concatenate([norm_gain[:, :, None], mlp_gain[:, :, None], cond_taps.transpose(0, 2, 1)], axis=2)
+    ch = jnp.pad(ch, ((0, 0), (0, 0), (0, LANES - 7)))
+    st = jnp.pad(short_taps.transpose(0, 2, 1), ((0, 0), (0, 0), (0, LANES - 5)))
     own = [gate_up[0].reshape(share, 2, hidden).transpose(1, 0, 2)]
     own += [halves(down_weight[layer]).reshape(2, hidden // features, share, width) for layer in range(layers)]
     for layer in range(layers):
-        pair = jnp.stack([small[layer], jnp.zeros_like(small[layer])])
-        own.append(jnp.concatenate([halves(in_weight[layer]), halves(out_weight[layer]), pair], axis=2))
-    full = gather_weights(own, dp_count, 0)
+        own.append(jnp.concatenate([halves(in_weight[layer]), halves(out_weight[layer])], axis=2))
+    place_rows = [tokens[0], jnp.broadcast_to(split_points, (8, LANES))]
+    x_low, split, x_far, *full = gather_weights(place_rows, own + [ch, st], dp_count, 0)
     downs = [x.reshape(2 * hidden, width) for x in full[1 : 1 + layers]]
-    mixer_w = [x.reshape(2, features, 4 * width + LANES) for x in full[1 + layers :]]
+    mixer_w = [x.reshape(2, features, 4 * width) for x in full[1 + layers : 1 + 2 * layers]]
+    ch, st = full[-2].reshape(layers, features, LANES), full[-1].reshape(layers, 3 * features, LANES)
     late, _ = lax.optimization_barrier((gate_up[1:], full[0]))
     gate_ups = [("halves", full[0].reshape(2 * features, hidden))]
     gate_ups += [("plain", lax.all_gather(x, AXES, axis=0, tiled=True)) for x in late]
-    ng, mg, ct, st = [], [], [], []
-    for layer in range(layers):
-        small = mixer_w[layer][0, :, 4 * width :].astype(F32).T
-        ng.append(small[0:1])
-        mg.append(small[1:2])
-        ct.append(own_channels(small[2:7]))
-        taps = small[7:22].reshape(3, 5, features).transpose(1, 2, 0).reshape(5, 3 * features)
-        st.append(own_channels(taps))
-
-    scalars = jnp.concatenate([split, core[None].astype(jnp.int32)])
-    normed = (norm_parts(stream)[0] * ng[0]).astype(BF)
+    gains = ch[:, :, :2].astype(F32).transpose(0, 2, 1).reshape(2 * layers, features)
+    scalars = jnp.stack([split[0, 0], core.astype(jnp.int32)])
+    stream, far = x_low.astype(F32), x_far.astype(F32)
+    grad = swap_rows(cotangent)[0].astype(F32)
+    normed, normed_far = [(norm_parts(x)[0] * gains[0]).astype(BF) for x in (stream, far)]
     kept = []
     for layer in range(layers):
-        normed_far = sibling(normed)
+        if layer > 0:
+            normed_far = sibling(normed)
         gated, mine, away, branches, q, key, conv, fh, uh = mixer_forward(
-            scalars, normed, normed_far, st[layer], ct[layer], mixer_w[layer], decay, fwd, inv
+            layer, scalars, normed, normed_far, ch, st, mixer_w[layer], decay, fwd, inv
         )
         middle, normed_mlp, pre, out, normed_next = mlp_forward(
-            scalars, stream, mine, sibling(away), mixer_w[layer].reshape(2 * features, -1), mg[layer],
-            ng[(layer + 1) % layers], gate_ups[layer] + (downs[layer],),
+            scalars, stream, mine, sibling(away), mixer_w[layer].reshape(2 * features, -1), gains,
+            2 * layer + 1, (2 * layer + 2) % (2 * layers), gate_ups[layer] + (downs[layer],),
         )
         kept.append((stream, normed, normed_far, gated, branches, q, key, conv, fh, uh, middle, normed_mlp, pre))
         stream, normed = out, normed_next
@@ -944,33 +1082,29 @@
     for layer in reversed(range(layers)):
         x, normed, normed_far, gated, branches, q, key, conv, fh, uh, middle, normed_mlp, pre = kept[layer]
         d_gu, d_down, d_middle, m_low, d_mg = mlp_backward(
-            grad, normed_mlp, middle, mg[layer], pre, gate_ups[layer] + (downs[layer],), layer > 0
+            grad, normed_mlp, middle, gains, 2 * layer + 1, pre, gate_ups[layer] + (downs[layer],), layer > 0
         )
-        rest, d_normed, d_away, d_st, d_ct = mixer_backward(
-            scalars, m_low, sibling(m_low), st[layer], ct[layer], mixer_w[layer], normed, normed_far, gated, branches,
+        rest, d_normed, d_away, d_ch, d_st = mixer_backward(
+            layer, scalars, m_low, sibling(m_low), d_mg, ch, st, mixer_w[layer], normed, normed_far, gated, branches,
             decay, fwd, inv, q, key, conv, fh, uh,
         )
-        d_part, d_ng = norm_back(x, ng[layer], d_normed + sibling(d_away).astype(F32))
-        grad = d_middle + d_part
-
         if layer > 0:
             early[layer] = lax.psum_scatter(d_gu, AXES, scatter_dimension=0, tiled=True)
-        summed.append((d_gu, d_down, rest, d_ng, d_mg, d_ct, d_st))
-    token_grad = swap_rows(grad[None])
+            d_part, d_ng = norm_back(x, gains[2 * layer], d_normed.astype(F32) + sibling(d_away).astype(F32))
+            grad = d_middle + d_part
+        summed.append((d_gu, d_down, rest, d_ch, d_st))
     d_gus, d_downs, rests, *smalls = zip(*summed[::-1])
-    d_ng, d_mg, d_ct, d_st = [jnp.stack(x) for x in smalls]
-    other = jnp.zeros_like(d_ct)
-    d_ct = beside(d_ct, other, 2)
-    d_st = d_st.reshape(layers, 5, 3, width)
-    d_st = beside(d_st, jnp.zeros_like(d_st), 3).reshape(layers, 5, features, 3)
-    d_st = d_st.transpose(0, 3, 1, 2).reshape(layers, 15, features)
-    small = jnp.concatenate([d_ng, d_mg, d_ct, d_st, jnp.zeros((layers, LANES - 22, features), F32)], axis=1)
-    small = small.astype(BF).transpose(0, 2, 1)
     pieces = [d_gus[0].reshape((2,) + grid + (share, hidden))]
     pieces += [x.reshape((2,) + grid + (hidden // features, share, width)) for x in d_downs]
     pieces += [x.reshape((2,) + grid + (share, 4 * width)) for x in rests]
-    pieces.append(small.reshape((2,) + grid + (share, LANES)))
-    outs = scatter_grads(pieces, dp_count, 1)
+    pieces += [jnp.stack(x).reshape((2,) + grid + (-1, LANES)) for x in smalls]
+    ends = [x_low, d_normed, d_away, d_middle, gains[:1], d_ng]
+    fits = share % 8 == 0
+    units = tuple(unit for unit in SCATTER_UNITS if fits or unit[0] != 2)
+    token_grad, *outs = scatter_grads(ends, pieces, units, dp_count, 1)
+    if not fits:
+        outs[2] = lax.psum_scatter(d_downs[1], AXES, scatter_dimension=1, tiled=True)
+    token_grad = token_grad[None]
 
     def joined(x):
         parts = x.shape[-1] // width
@@ -985,15 +1119,14 @@
     rest = outs[1 + layers : 1 + 2 * layers]
     g_in = jnp.stack([joined(x[:, :, : 3 * width]) for x in rest]).astype(F32)
     g_out = jnp.stack([joined(x[:, :, 3 * width :]) for x in rest]).astype(F32)
-    small = outs[-1].astype(F32)
-    g_ng, g_mg, g_ct = small[:, :, 0], small[:, :, 1], small[:, :, 2:7].transpose(0, 2, 1)
-    g_st = small[:, :, 7:22].reshape(layers, share, 3, 5).transpose(0, 3, 1, 2)
+    s_ch, s_st, s_ng = [x.astype(F32) for x in outs[1 + 2 * layers :]]
+    g_ng, g_mg, g_ct, g_st = s_ng[:, :, 0], s_ch[:, :, 1], s_ch[:, :, 2:7].transpose(0, 2, 1), s_st[:, :, :5].transpose(0, 2, 1)
     return (
         activations,
         token_grad,
         g_ng,
         g_in,
-        g_st.reshape(layers, 5, 3 * share),
+        g_st,
         g_ct,
         g_out,
         g_mg,

time: 601 us -> 582 us (0.968)
  local copies, waits for them, and re-layouts: 52.3 us -> 25.4 us
  Pallas kernels: 472 us -> 488 us
  starting transfers between devices: 16 us -> 6.38 us
    pallas_call x6, Pallas kernels: 356 us -> 380 us  [the longest x1 147 us: scatter_grads(): pl.pallas_call(body, out_shape=[jax.ShapeDtypeStruct((rows, features), F3...]
    ppermute x5 -> x2, starting transfers between devices: 14.2 us -> 5.2 us  [swap_rows(): return jnp.where(core == seq, x, lax.ppermute(x, AXES, swap))]
    all_gather x1, waiting for transfers between devices: 0.01 us -> 8.93 us  [shards(): lax.all_gather(x, AXES, axis=0, tiled=True)]
    pallas_call x4, Pallas kernels: 116 us -> 108 us  [local_call(): pl.pallas_call(kernel, out_shape=[jax.ShapeDtypeStruct(shape, dtype) for...]
    reshape x7 -> x2, local copies, waits for them, and re-layouts: 7.59 us -> 0.28 us  [shards(): ch[:, :, :2].astype(F32).transpose(0, 2, 1).reshape(2 * layers, features)]
  transfers between devices with their start and end apart: 15 -> 10, of which waited for: 3 -> 4; matrix products, arithmetic and copies ran while one was open for 11% -> 6% of each run, Pallas kernels for 49% -> 52%
where the time goes in v3:
time: 582 us; the launch traced here: 572 us
  Pallas kernels  488 us (84%)
  local copies, waits for them, and re-layouts  25.4 us (4%)
  other arithmetic  25.1 us (4%)
  between operations  16 us (3%)
  waiting for transfers between devices  11.8 us (2%)
  starting transfers between devices  6.38 us (1%)
    pallas_call x1, Pallas kernels, scatter_grads(): pl.pallas_call(body, out_shape=[jax.ShapeDtypeStruct((rows, features), F3...  147 us
    pallas_call x1, Pallas kernels, gather_weights(): pl.pallas_call(body, out_shape=[jax.ShapeDtypeStruct(x.shape, x.dtype) fo...  145 us
    pallas_call x4, Pallas kernels, local_call(): pl.pallas_call(kernel, out_shape=[jax.ShapeDtypeStruct(shape, dtype) for...  108 us
    pallas_call x2, Pallas kernels, mlp_backward(): pl.pallas_call(functools.partial(mlp_backward_kernel, gain), grid=(hidden...  52.8 us
    pallas_call x2, Pallas kernels, mlp_forward(): pl.pallas_call(functools.partial(mlp_forward_kernel, gain, next_gain), gr...  35.2 us
  transfers between devices with their start and end apart: 10, of which 4 were waited for; matrix products, arithmetic and copies ran while one was open for 6% of the time, Pallas kernels for 52%

profile of v3, /device:TPU:1, one launch (start us, length us, event | category | flops | bytes accessed | tf_op | source)
XLA Modules:
  0.0 572.2 jit_solution(6487192682900769727)
XLA Ops:
  7.9 1.8 fusion.7
  16.2 144.5 %shard_map.207 = (bf16[512,768]{1,0:T(8,128)(2,1)}, s32[8,128]{1,0:T(8,128)}, bf16[512,768]{1,0:T(8,128)(2,1)}, bf16[2,2,2,2,2,2,24,3072]{7,6,5,4,3,2,1,0:T(8,12...) custom-call(bf16[512,768]{1,0:T(8,128)(2,1)} %bitcast.138, ...), custom_call_target="tpu_custom_call" | custom-call | tf_op jit(solution)/shard_map/pallas_call | solution.py:658
  160.8 1.2 slice.71
  162.0 1.1 convert_bitcast_fusion
  164.0 1.2 pad_add_fusion.scalar_ref
  166.9 1.5 multiply_bitcast_fusion.decay_hbm
  168.4 1.7 fusion.4
  170.0 21.4 %shard_map.208 = (bf16[1024,384]{1,0:T(8,128)(2,1)}, bf16[512,384]{1,0:T(8,128)(2,1)}, bf16[512,384]{1,0:T(8,128)(2,1)}, bf16[1024,1152]{1,0:T(8,128)(2,1)}, bf1...) custom-call(s32[2]{0:T(128)} %pad_add_fusion.scalar_ref, ...), custom_call_target="tpu_custom_call" | custom-call | tf_op jit(solution)/shard_map/pallas_call | solution.py:407
  191.7 1.3 convert_element_type.70.x_ref
  194.2 17.6 %shard_map.209 = (f32[512,768]{1,0:T(8,128)}, bf16[512,768]{1,0:T(8,128)(2,1)}, bf16[2,512,3072]{2,1,0:T(8,128)(2,1)}, f32[512,768]{1,0:T(8,128)}, bf16[512,768]{1,0:T(8,128)(2,1)}) custom-call(s32[2]{0:T(128)} %pad_add_fusion.scalar_ref, f32[512,768]{1,0:T(8,128)} %convert_element_type.70.x_ref, bf16[512,384]{1,0:T(8,128)(2,1)} %get-tuple-element.83.g0_ref, ...), custom_call_target="tpu_custom_call" | custom-call | tf_op jit(solution)/shard_map/pallas_call | solution.py:954
  212.1 3.0 collective-permute-start.4
  216.0 21.6 %shard_map.210 = (bf16[1024,384]{1,0:T(8,128)(2,1)}, bf16[512,384]{1,0:T(8,128)(2,1)}, bf16[512,384]{1,0:T(8,128)(2,1)}, bf16[1024,1152]{1,0:T(8,128)(2,1)}, bf1...) custom-call(s32[2]{0:T(128)} %pad_add_fusion.scalar_ref, ...), custom_call_target="tpu_custom_call" | custom-call | tf_op jit(solution)/shard_map/pallas_call | solution.py:407
  237.7 1.3 bitcast_convert_fusion.g_ref
  239.6 8.9 %all-gather.3.cloned.1.call-done = bf16[1,768,6144]{2,1,0:T(8,128)(2,1)} async-done(((bf16[1,24,6144]{2,1,0:T(8,128)(2,1)}), bf16[1,768,6144]{2,1,0:T(8,128)(2,1)}) %all-gather.3.cloned.1.call-update) | async-done | bytes 9437200 | tf_op jit(solution)/shard_map/all_gather | solution.py:1059
  248.5 17.6 %shard_map.211 = (f32[512,768]{1,0:T(8,128)}, bf16[512,768]{1,0:T(8,128)(2,1)}, bf16[2,512,3072]{2,1,0:T(8,128)(2,1)}, f32[512,768]{1,0:T(8,128)}, bf16[512,768]{1,0:T(8,128)(2,1)}) custom-call(s32[2]{0:T(128)} %pad_add_fusion.scalar_ref, f32[512,768]{1,0:T(8,128)} %get-tuple-element.87.x_ref, bf16[512,384]{1,0:T(8,128)(2,1)} %get-tuple-element.90.g0_ref, ...), custom_call_target="tpu_custom_call" | custom-call | tf_op jit(solution)/shard_map/pallas_call | solution.py:954
  266.1 26.4 %shard_map.212 = (bf16[768,6144]{1,0:T(8,128)(2,1)}, bf16[2,3072,384]{2,1,0:T(8,128)(2,1)}, f32[512,768]{1,0:T(8,128)}, bf16[512,768]{1,0:T(8,128)(2,1)}, f32[1,768]{1,0:T(1,128)}) custom-call(f32[512,768]{1,0:T(8,128)} %bitcast_convert_fusion.g_ref, bf16[512,768]{1,0:T(8,128)(2,1)} %get-tuple-element.95.hm_ref, f32[512,768]{1,0:T(8,128)} %get-tuple-element.96.mid_ref, ...), custom_call_target="tpu_custom_call" | custom-call | tf_op jit(solution)/shard_map/pallas_call | solution.py:972
  292.6 1.1 copy-done.8
  294.4 1.6 collective-permute-done.5.mid_other_ref
  296.8 32.3 %shard_map.213 = (bf16[2,768,1536]{2,1,0:T(8,128)(2,1)}, bf16[512,768]{1,0:T(8,128)(2,1)}, bf16[512,768]{1,0:T(8,128)(2,1)}, bf16[768,128]{1,0:T(8,128)(2,1)}, bf16[2304,128]{1,0:T(8,128)(2,1)}) custom-call(s32[2]{0:T(128)} %pad_add_fusion.scalar_ref, bf16[512,768]{1,0:T(8,128)(2,1)} %get-tuple-element.99.mid_own_ref, bf16[512,768]{1,0:T(8,128)(2,1)} %copy-done.10, ...), custom_call_target="tpu_custom_call" | custom-call | tf_op jit(solution)/shard_map/pallas_call | solution.py:407
  330.6 1.0 convert_bitcast_fusion.1
  331.6 2.2 collective-permute-start.3
  335.3 1.8 multiply_add_fusion.g_ref
  337.1 26.3 %shard_map.214 = (bf16[2,768,3072]{2,1,0:T(8,128)(2,1)}, bf16[2,3072,384]{2,1,0:T(8,128)(2,1)}, f32[512,768]{1,0:T(8,128)}, bf16[512,768]{1,0:T(8,128)(2,1)}, f32[1,768]{1,0:T(1,128)}) custom-call(f32[512,768]{1,0:T(8,128)} %multiply_add_fusion.g_ref, bf16[512,768]{1,0:T(8,128)(2,1)} %get-tuple-element.110.hm_ref, f32[512,768]{1,0:T(8,128)} %get-tuple-element.111.mid_ref, ...), custom_call_target="tpu_custom_call" | custom-call | tf_op jit(solution)/shard_map/pallas_call | solution.py:972
  363.5 2.2 broadcast_select_fusion
  367.1 32.3 %shard_map.215 = (bf16[2,768,1536]{2,1,0:T(8,128)(2,1)}, bf16[512,768]{1,0:T(8,128)(2,1)}, bf16[512,768]{1,0:T(8,128)(2,1)}, bf16[768,128]{1,0:T(8,128)(2,1)}, bf16[2304,128]{1,0:T(8,128)(2,1)}) custom-call(s32[2]{0:T(128)} %pad_add_fusion.scalar_ref, bf16[512,768]{1,0:T(8,128)(2,1)} %get-tuple-element.113.mid_own_ref, bf16[512,768]{1,0:T(8,128)(2,1)} %copy-done.9, ...), custom_call_target="tpu_custom_call" | custom-call | tf_op jit(solution)/shard_map/pallas_call | solution.py:407
  399.4 1.7 pad_maximum_fusion.1.refs_11_
  401.1 2.2 pad_maximum_fusion.refs_12_
  403.3 147.4 %shard_map.216 = (f32[512,768]{1,0:T(8,128)}, bf16[2,24,3072]{2,1,0:T(8,128)(2,1)}, bf16[2,4,24,384]{3,2,1,0:T(8,128)(2,1)}, bf16[2,4,24,384]{3,2,1,0:T(8,128)(2...) custom-call(bf16[512,768]{1,0:T(8,128)(2,1)} %get-tuple-element.78.r, ...), custom_call_target="tpu_custom_call" | custom-call | tf_op jit(solution)/shard_map/pallas_call | solution.py:802
  550.8 1.0 slice.78
  561.0 1.2 reshape.225
  562.6 1.1 maximum_convert_fusion
  563.7 1.1 copy.135
  (161 shorter events, 27.6 us)
Async XLA Ops:
  7.2 3.5 copy-start.16
  7.2 241.3 %all-gather.3.cloned.1.call-start = ((), (), s32[]{:S(2)}) async-start(), calls=%async_computation.2 | async-start | bytes 9732096 | tf_op jit(solution)/shard_map/all_gather | solution.py:1059
  9.7 2.5 copy-start.22
  9.7 2.5 copy-start.18
  10.8 2.0 copy-start.27
  10.8 2.0 copy-start.28
  10.8 2.0 copy-start.29
  10.8 2.1 copy-start.26
  160.7 400.2 %reduce-scatter.2.cloned.1.call-start = ((), (), s32[]{:S(2)}) async-start(), calls=%async_computation.1 | async-start | bytes 9732096 | tf_op jit(solution)/shard_map/reduce_scatter | solution.py:1092
  162.0 3.2 copy-start.1
  163.1 2.3 copy-start.2
  163.4 2.8 copy-start.15
  191.5 2.0 collective-permute-start
  194.2 17.9 %copy-start.11 = (bf16[1,512,768]{2,1,0:T(8,128)(2,1)S(1)}, bf16[1,512,768]{2,1,0:T(8,128)(2,1)}, u32[]{:S(2)}) copy-start(bf16[1,512,768]{2,1,0:T(8,128)(2,1)} %param.15) | copy-start | bytes 2359300
  211.9 3.2 collective-permute-start.1
  212.1 25.6 %collective-permute-start.4 = (bf16[1,512,768]{2,1,0:T(8,128)(2,1)S(1)}, bf16[1,512,768]{2,1,0:T(8,128)(2,1)S(1)}, u32[]{:S(2)}, u32[]{:S(2)}) collective-permute-start(bf16[1,512,768]{2,1,0:T(8,128)(2,1)S(1)} %copy-done.11), channel_id=1, source_target_pairs={{1,2},{2,1},{5,6},{6,5},{9,10},{10,9},{13,14},{14,13},{17,18},{18,... | collective-permute-start | bytes 2359304 | tf_op jit(solution)/shard_map/ppermute | solution.py:1010
  237.6 2.0 collective-permute-start.2
  239.6 8.9 %copy-start.13 = (bf16[512,384]{1,0:T(8,128)(2,1)}, bf16[512,384]{1,0:T(8,128)(2,1)S(1)}, u32[]{:S(2)}) copy-start(bf16[512,384]{1,0:T(8,128)(2,1)S(1)} %collective-permute-done.2.g1_ref) | copy-start | bytes 1179652
  292.6 1.6 copy-start
  293.7 2.3 collective-permute-start.5
  329.2 4.7 collective-permute-start.6
  329.8 4.1 copy-start.5
  331.6 31.8 %collective-permute-start.3 = (bf16[1,512,768]{2,1,0:T(8,128)(2,1)}, bf16[1,512,768]{2,1,0:T(8,128)(2,1)}, u32[]{:S(2)}, u32[]{:S(2)}) collective-permute-start(bf16[1,512,768]{2,1,0:T(8,128)(2,1)} %convert_bitcast_fusion.1), channel_id=1, source_target_pairs={{1,2},{2,1},{5,6},{6,5},{9,10},{10,9},{13,14},{14,13},{17,18},{18,... | collective-permute-start | bytes 2359304 | tf_op jit(solution)/shard_map/ppermute | solution.py:1010
  363.4 2.8 collective-permute-start.7
  367.1 32.3 %copy-start.19 = (bf16[768,128]{1,0:T(8,128)(2,1)S(1)}, bf16[768,128]{1,0:T(8,128)(2,1)}, u32[]{:S(2)}) copy-start(bf16[768,128]{1,0:T(8,128)(2,1)} %get-tuple-element.131) | copy-start | bytes 589828
  367.1 34.0 %copy-start.12 = (bf16[2304,128]{1,0:T(8,128)(2,1)S(1)}, bf16[2304,128]{1,0:T(8,128)(2,1)}, u32[]{:S(2)}) copy-start(bf16[2304,128]{1,0:T(8,128)(2,1)} %get-tuple-element.133) | copy-start | bytes 1769476
  550.7 2.4 copy-start.23
  550.7 3.1 copy-start.25
  550.8 5.5 copy-start.17
  551.9 4.9 copy-start.21
  552.9 4.2 copy-start.20
  553.1 4.2 copy-start.24
  (8 other events, 9.0 us)
Sparse Core Ops, SparseCore 0:
  160.8 87.6 all-gather.2
  292.7 134.8 reduce-scatter.1

commit v4 on v3

--- a/solution.py
+++ b/solution.py
@@ -561,7 +561,7 @@
     (0, 0, 768, 0, 0), (0, 768, 768, 1, 0), (2, 2, 2, 2, 0),
     (0, 1536, 768, 0, 1), (0, 2304, 768, 1, 1), (3, 1280, 256, 2, 1),
     (1, 0, 2, 0, 2), (1, 2, 2, 1, 2), (4, 1280, 256, 2, 2),
-    (3, 0, 640, 0, 3), (3, 640, 640, 2, 3), (5, 0, 128, 2, 3), (6, 0, 128, 2, 3),
+    (3, 0, 640, 0, 3), (3, 640, 640, 1, 3), (5, 0, 128, 2, 3), (6, 0, 128, 2, 3),
     (4, 0, 640, 0, 4), (4, 640, 640, 1, 4), (7, 0, 128, 2, 4),
     (2, 0, 1, 0, 5), (2, 1, 1, 0, 5),
 )
@@ -610,7 +610,7 @@
         keep.start()
         firsts.append((keep, remote(piece, here, core_send.at[u, 0], core_recv.at[u, 0], sibling)))
     for number, (u, t) in enumerate(ticks(units, stages, False)):
-        if number == 10:
+        if number == 4:
             for swap in swaps:
                 swap.start()
         unit = units[u]
@@ -685,7 +685,7 @@
     exchange = remote(away_ref, other_ref, end_send.at[0], end_recv.at[0], sibling)
     begin = pltpu.make_async_copy(dmid_ref, grad_ref, end_local.at[1])
     begin.start()
-    swap = Swap(grad_ref, token_ref, end_send.at[1], end_recv.at[1], end_local.at[0], moves, partner)
+    swap = Swap(other_ref, token_ref, end_send.at[1], end_recv.at[1], end_local.at[0], moves, partner)
 
     def finish_rows():
         exchange.wait()
@@ -698,7 +698,7 @@
             rows = pl.ds(pl.multiple_of(i * 128, 128), 128)
             d = dn_ref[rows, :].astype(F32) + other_ref[rows, :].astype(F32)
             dx, dg = norm_back(x_ref[rows, :].astype(F32), gain_ref[...], d)
-            grad_ref[rows, :] += dx
+            other_ref[rows, :] = (grad_ref[rows, :] + dx).astype(BF)
             sum_ref[0:1, :] += dg
 
         swap.start()
@@ -801,7 +801,7 @@
     anywhere, vmem = pl.BlockSpec(memory_space=pl.ANY), pl.BlockSpec(memory_space=pltpu.VMEM)
     return pl.pallas_call(
         body,
-        out_shape=[jax.ShapeDtypeStruct((rows, features), F32)]
+        out_shape=[jax.ShapeDtypeStruct((rows, features), BF)]
         + [jax.ShapeDtypeStruct((2,) + tail, BF) for tail in tails],
         in_specs=[vmem, vmem, anywhere, anywhere, vmem, vmem] + [anywhere] * len(grads),
         out_specs=[anywhere] * (1 + arrays),
@@ -1104,7 +1104,7 @@
     token_grad, *outs = scatter_grads(ends, pieces, units, dp_count, 1)
     if not fits:
         outs[2] = lax.psum_scatter(d_downs[1], AXES, scatter_dimension=1, tiled=True)
-    token_grad = token_grad[None]
+    token_grad = token_grad[None].astype(F32)
 
     def joined(x):
         parts = x.shape[-1] // width

time: 582 us -> 573 us (0.985)
  Pallas kernels: 488 us -> 481 us
  transfers between devices with their start and end apart: 10 -> 10, of which waited for: 4 -> 5; matrix products, arithmetic and copies ran while one was open for 6% -> 6% of each run, Pallas kernels for 52% -> 52%
where the time goes in v4:
time: 573 us; the launch traced here: 564 us
  Pallas kernels  481 us (84%)
  other arithmetic  26.4 us (5%)
  local copies, waits for them, and re-layouts  24.3 us (4%)
  between operations  16 us (3%)
  waiting for transfers between devices  11.3 us (2%)
    pallas_call x1, Pallas kernels, scatter_grads(): pl.pallas_call(body, out_shape=[jax.ShapeDtypeStruct((rows, features), BF...  143 us
    pallas_call x1, Pallas kernels, gather_weights(): pl.pallas_call(body, out_shape=[jax.ShapeDtypeStruct(x.shape, x.dtype) fo...  142 us
    pallas_call x4, Pallas kernels, local_call(): pl.pallas_call(kernel, out_shape=[jax.ShapeDtypeStruct(shape, dtype) for...  107 us
    pallas_call x2, Pallas kernels, mlp_backward(): pl.pallas_call(functools.partial(mlp_backward_kernel, gain), grid=(hidden...  52.8 us
    pallas_call x2, Pallas kernels, mlp_forward(): pl.pallas_call(functools.partial(mlp_forward_kernel, gain, next_gain), gr...  35.2 us
  transfers between devices with their start and end apart: 10, of which 5 were waited for; matrix products, arithmetic and copies ran while one was open for 6% of the time, Pallas kernels for 52%

profile of v4, /device:TPU:1, one launch (start us, length us, event | category | flops | bytes accessed | tf_op | source)
XLA Modules:
  0.0 564.1 jit_solution(14538642992959787125)
XLA Ops:
  7.9 1.8 fusion.7
  16.2 142.1 %shard_map.207 = (bf16[512,768]{1,0:T(8,128)(2,1)}, s32[8,128]{1,0:T(8,128)}, bf16[512,768]{1,0:T(8,128)(2,1)}, bf16[2,2,2,2,2,2,24,3072]{7,6,5,4,3,2,1,0:T(8,12...) custom-call(bf16[512,768]{1,0:T(8,128)(2,1)} %bitcast.139, ...), custom_call_target="tpu_custom_call" | custom-call | tf_op jit(solution)/shard_map/pallas_call | solution.py:658
  158.4 1.2 slice.71
  159.6 1.1 convert_bitcast_fusion
  161.6 1.2 pad_add_fusion.scalar_ref
  164.4 1.5 multiply_bitcast_fusion.decay_hbm
  165.9 1.7 fusion.4
  167.6 21.4 %shard_map.208 = (bf16[1024,384]{1,0:T(8,128)(2,1)}, bf16[512,384]{1,0:T(8,128)(2,1)}, bf16[512,384]{1,0:T(8,128)(2,1)}, bf16[1024,1152]{1,0:T(8,128)(2,1)}, bf1...) custom-call(s32[2]{0:T(128)} %pad_add_fusion.scalar_ref, ...), custom_call_target="tpu_custom_call" | custom-call | tf_op jit(solution)/shard_map/pallas_call | solution.py:407
  189.2 1.3 convert_element_type.76.x_ref
  191.7 17.7 %shard_map.209 = (f32[512,768]{1,0:T(8,128)}, bf16[512,768]{1,0:T(8,128)(2,1)}, bf16[2,512,3072]{2,1,0:T(8,128)(2,1)}, f32[512,768]{1,0:T(8,128)}, bf16[512,768]{1,0:T(8,128)(2,1)}) custom-call(s32[2]{0:T(128)} %pad_add_fusion.scalar_ref, f32[512,768]{1,0:T(8,128)} %convert_element_type.76.x_ref, bf16[512,384]{1,0:T(8,128)(2,1)} %get-tuple-element.83.g0_ref, ...), custom_call_target="tpu_custom_call" | custom-call | tf_op jit(solution)/shard_map/pallas_call | solution.py:954
  209.6 2.0 collective-permute-start.4
  212.9 21.6 %shard_map.210 = (bf16[1024,384]{1,0:T(8,128)(2,1)}, bf16[512,384]{1,0:T(8,128)(2,1)}, bf16[512,384]{1,0:T(8,128)(2,1)}, bf16[1024,1152]{1,0:T(8,128)(2,1)}, bf1...) custom-call(s32[2]{0:T(128)} %pad_add_fusion.scalar_ref, ...), custom_call_target="tpu_custom_call" | custom-call | tf_op jit(solution)/shard_map/pallas_call | solution.py:407
  234.6 1.3 bitcast_convert_fusion.1.g_ref
  236.5 8.1 %all-gather.3.cloned.1.call-done = bf16[1,768,6144]{2,1,0:T(8,128)(2,1)} async-done(((bf16[1,24,6144]{2,1,0:T(8,128)(2,1)}), bf16[1,768,6144]{2,1,0:T(8,128)(2,1)}) %all-gather.3.cloned.1.call-update) | async-done | bytes 9437200 | tf_op jit(solution)/shard_map/all_gather | solution.py:1059
  244.6 17.6 %shard_map.211 = (f32[512,768]{1,0:T(8,128)}, bf16[512,768]{1,0:T(8,128)(2,1)}, bf16[2,512,3072]{2,1,0:T(8,128)(2,1)}, f32[512,768]{1,0:T(8,128)}, bf16[512,768]{1,0:T(8,128)(2,1)}) custom-call(s32[2]{0:T(128)} %pad_add_fusion.scalar_ref, f32[512,768]{1,0:T(8,128)} %get-tuple-element.87.x_ref, bf16[512,384]{1,0:T(8,128)(2,1)} %get-tuple-element.90.g0_ref, ...), custom_call_target="tpu_custom_call" | custom-call | tf_op jit(solution)/shard_map/pallas_call | solution.py:954
  262.2 26.4 %shard_map.212 = (bf16[768,6144]{1,0:T(8,128)(2,1)}, bf16[2,3072,384]{2,1,0:T(8,128)(2,1)}, f32[512,768]{1,0:T(8,128)}, bf16[512,768]{1,0:T(8,128)(2,1)}, f32[1,768]{1,0:T(1,128)}) custom-call(f32[512,768]{1,0:T(8,128)} %bitcast_convert_fusion.1.g_ref, bf16[512,768]{1,0:T(8,128)(2,1)} %get-tuple-element.95.hm_ref, f32[512,768]{1,0:T(8,128)} %get-tuple-element.96.mid_ref, ...), custom_call_target="tpu_custom_call" | custom-call | tf_op jit(solution)/shard_map/pallas_call | solution.py:972
  288.6 1.1 copy-done.7
  290.4 1.6 collective-permute-done.5.mid_other_ref
  292.9 32.4 %shard_map.213 = (bf16[2,768,1536]{2,1,0:T(8,128)(2,1)}, bf16[512,768]{1,0:T(8,128)(2,1)}, bf16[512,768]{1,0:T(8,128)(2,1)}, bf16[768,128]{1,0:T(8,128)(2,1)}, bf16[2304,128]{1,0:T(8,128)(2,1)}) custom-call(s32[2]{0:T(128)} %pad_add_fusion.scalar_ref, bf16[512,768]{1,0:T(8,128)(2,1)} %get-tuple-element.99.mid_own_ref, bf16[512,768]{1,0:T(8,128)(2,1)} %copy-done.9, ...), custom_call_target="tpu_custom_call" | custom-call | tf_op jit(solution)/shard_map/pallas_call | solution.py:407
  326.8 1.0 convert_bitcast_fusion.1
  327.8 2.1 collective-permute-start.3
  331.4 1.8 multiply_add_fusion.g_ref
  333.1 26.4 %shard_map.214 = (bf16[2,768,3072]{2,1,0:T(8,128)(2,1)}, bf16[2,3072,384]{2,1,0:T(8,128)(2,1)}, f32[512,768]{1,0:T(8,128)}, bf16[512,768]{1,0:T(8,128)(2,1)}, f32[1,768]{1,0:T(1,128)}) custom-call(f32[512,768]{1,0:T(8,128)} %multiply_add_fusion.g_ref, bf16[512,768]{1,0:T(8,128)(2,1)} %get-tuple-element.110.hm_ref, f32[512,768]{1,0:T(8,128)} %get-tuple-element.111.mid_ref, ...), custom_call_target="tpu_custom_call" | custom-call | tf_op jit(solution)/shard_map/pallas_call | solution.py:972
  359.6 2.2 broadcast_select_fusion
  363.2 32.1 %shard_map.215 = (bf16[2,768,1536]{2,1,0:T(8,128)(2,1)}, bf16[512,768]{1,0:T(8,128)(2,1)}, bf16[512,768]{1,0:T(8,128)(2,1)}, bf16[768,128]{1,0:T(8,128)(2,1)}, bf16[2304,128]{1,0:T(8,128)(2,1)}) custom-call(s32[2]{0:T(128)} %pad_add_fusion.scalar_ref, bf16[512,768]{1,0:T(8,128)(2,1)} %get-tuple-element.113.mid_own_ref, bf16[512,768]{1,0:T(8,128)(2,1)} %copy-done.8, ...), custom_call_target="tpu_custom_call" | custom-call | tf_op jit(solution)/shard_map/pallas_call | solution.py:407
  395.4 1.7 pad_maximum_fusion.1.refs_11_
  397.1 2.2 pad_maximum_fusion.refs_12_
  399.3 143.3 %shard_map.216 = (bf16[512,768]{1,0:T(8,128)(2,1)}, bf16[2,24,3072]{2,1,0:T(8,128)(2,1)}, bf16[2,4,24,384]{3,2,1,0:T(8,128)(2,1)}, bf16[2,4,24,384]{3,2,1,0:T(8,...) custom-call(bf16[512,768]{1,0:T(8,128)(2,1)} %get-tuple-element.78.r, ...), custom_call_target="tpu_custom_call" | custom-call | tf_op jit(solution)/shard_map/pallas_call | solution.py:802
  542.6 1.0 slice.78
  552.0 1.3 bitcast_convert_fusion
  554.1 1.2 reshape.227
  555.7 1.1 maximum_convert_fusion
  (161 shorter events, 28.0 us)
Async XLA Ops:
  7.2 3.5 copy-start.16
  7.2 237.4 %all-gather.3.cloned.1.call-start = ((), (), s32[]{:S(2)}) async-start(), calls=%async_computation.2 | async-start | bytes 9732096 | tf_op jit(solution)/shard_map/all_gather | solution.py:1059
  9.7 2.5 copy-start.22
  9.7 2.5 copy-start.18
  10.8 2.0 copy-start.27
  10.8 2.0 copy-start.28
  10.8 2.0 copy-start.29
  10.8 2.1 copy-start.26
  158.3 395.8 %reduce-scatter.2.cloned.1.call-start = ((), (), s32[]{:S(2)}) async-start(), calls=%async_computation.1 | async-start | bytes 9732096 | tf_op jit(solution)/shard_map/reduce_scatter | solution.py:1092
  159.6 3.2 copy-start.1
  160.7 2.3 copy-start.2
  161.0 2.8 copy-start.15
  189.0 2.0 collective-permute-start
  191.7 17.9 %copy-start.11 = (bf16[1,512,768]{2,1,0:T(8,128)(2,1)S(1)}, bf16[1,512,768]{2,1,0:T(8,128)(2,1)}, u32[]{:S(2)}) copy-start(bf16[1,512,768]{2,1,0:T(8,128)(2,1)} %param.15) | copy-start | bytes 2359300
  209.4 2.6 collective-permute-start.1
  209.6 25.0 %collective-permute-start.4 = (bf16[1,512,768]{2,1,0:T(8,128)(2,1)S(1)}, bf16[1,512,768]{2,1,0:T(8,128)(2,1)S(1)}, u32[]{:S(2)}, u32[]{:S(2)}) collective-permute-start(bf16[1,512,768]{2,1,0:T(8,128)(2,1)S(1)} %copy-done.11), channel_id=1, source_target_pairs={{1,2},{2,1},{5,6},{6,5},{9,10},{10,9},{13,14},{14,13},{17,18},{18,... | collective-permute-start | bytes 2359304 | tf_op jit(solution)/shard_map/ppermute | solution.py:1010
  234.4 2.0 collective-permute-start.2
  236.5 8.1 %copy-start.13 = (bf16[512,384]{1,0:T(8,128)(2,1)}, bf16[512,384]{1,0:T(8,128)(2,1)S(1)}, u32[]{:S(2)}) copy-start(bf16[512,384]{1,0:T(8,128)(2,1)S(1)} %collective-permute-done.2.g1_ref) | copy-start | bytes 1179652
  289.7 2.3 collective-permute-start.5
  325.3 4.6 collective-permute-start.6
  325.9 4.0 copy-start.5
  327.8 31.8 %collective-permute-start.3 = (bf16[1,512,768]{2,1,0:T(8,128)(2,1)}, bf16[1,512,768]{2,1,0:T(8,128)(2,1)}, u32[]{:S(2)}, u32[]{:S(2)}) collective-permute-start(bf16[1,512,768]{2,1,0:T(8,128)(2,1)} %convert_bitcast_fusion.1), channel_id=1, source_target_pairs={{1,2},{2,1},{5,6},{6,5},{9,10},{10,9},{13,14},{14,13},{17,18},{18,... | collective-permute-start | bytes 2359304 | tf_op jit(solution)/shard_map/ppermute | solution.py:1010
  359.5 2.8 collective-permute-start.7
  363.2 32.2 %copy-start.19 = (bf16[768,128]{1,0:T(8,128)(2,1)S(1)}, bf16[768,128]{1,0:T(8,128)(2,1)}, u32[]{:S(2)}) copy-start(bf16[768,128]{1,0:T(8,128)(2,1)} %get-tuple-element.131) | copy-start | bytes 589828
  363.2 33.9 %copy-start.12 = (bf16[2304,128]{1,0:T(8,128)(2,1)S(1)}, bf16[2304,128]{1,0:T(8,128)(2,1)}, u32[]{:S(2)}) copy-start(bf16[2304,128]{1,0:T(8,128)(2,1)} %get-tuple-element.133) | copy-start | bytes 1769476
  542.6 2.4 copy-start.23
  542.6 3.1 copy-start.25
  542.6 5.5 copy-start.17
  543.7 4.9 copy-start.21
  544.7 4.2 copy-start.20
  544.9 4.2 copy-start.24
  548.4 3.6 copy-start.10
  (8 other events, 9.1 us)
Sparse Core Ops, SparseCore 0:
  158.4 86.1 all-gather.2
  288.8 135.6 reduce-scatter.1

commit v5 on v4

--- a/solution.py
+++ b/solution.py
@@ -33,11 +33,11 @@
 
 
 def decay_table(length, features):
-    channels = jnp.arange(features).astype(F32)
-    positions = jnp.arange(length).astype(F32)
-    rates = jnp.exp(math.log(1.0 / length) + channels / (features - 1) * math.log(4.0))
-    scales = lax.rsqrt(jnp.sum(jnp.exp(-2.0 * positions[:, None] * rates[None, :]), axis=0))
-    return jnp.exp(-positions[:, None] * rates[None, :]) * scales[None, :]
+    positions = np.arange(length)
+    rates = np.exp(math.log(1.0 / length) + np.arange(features) / (features - 1) * math.log(4.0))
+    scales = np.sum(np.exp(-2.0 * positions[:, None] * rates[None, :]), axis=0) ** -0.5
+    table = np.exp(-positions[:, None] * rates[None, :]) * scales[None, :]
+    return np.stack(np.split(table, 2, axis=1)).astype(np.float32)
 
 
 def dot(a, b, dims=((1,), (0,))):
@@ -116,7 +116,7 @@
 
 
 def mixer_forward_kernel(
-    layer, scalar_ref, own_ref, other_ref, ch_hbm, st_hbm, iw_hbm, decay_hbm, fwd_hbm, inv_hbm,
+    layer, split_ref, own_ref, other_ref, ch_hbm, st_hbm, iw_hbm, decay_hbm, fwd_hbm, inv_hbm,
     gated_ref, mine_ref, send_ref, br_hbm, q_hbm, key_hbm, conv_hbm, fh_hbm, uh_hbm,
     iw_ref, decay_ref, fwd_ref, inv_ref, br_ref, q_ref, key_ref, conv_ref, fh_ref, uh_ref,
     ct_ref, st_ref, cw_ref, sw_ref, pad, kpad, filt, u, prod, in_sems, out_sems,
@@ -124,12 +124,12 @@
     length, width = q_ref.shape
     rows_own = own_ref.shape[0]
     half = length - GAP
-    split, core = scalar_ref[0], scalar_ref[1]
+    split, core = split_ref[0, 0], lax.axis_index("dp") % 2
     strips = width // STRIP
     loads = fetch(
         [
             (iw_hbm.at[core, :, pl.ds(0, 3 * width)], iw_ref),
-            (decay_hbm, decay_ref),
+            (decay_hbm.at[core], decay_ref),
             (fwd_hbm, fwd_ref),
             (inv_hbm, inv_ref),
         ]
@@ -233,7 +233,7 @@
 
 
 def mixer_backward_kernel(
-    layer, scalar_ref, mid_own_ref, mid_other_ref, dmg_ref, ch_hbm, st_hbm,
+    layer, split_ref, mid_own_ref, mid_other_ref, dmg_ref, ch_hbm, st_hbm,
     w_hbm, own_hbm, other_hbm, gated_hbm, br_hbm, decay_hbm, fwd_hbm, inv_hbm, q_hbm, key_hbm, conv_hbm, fh_hbm, uh_hbm,
     rest_ref, dn_ref, dn_send_ref, dch_ref, dst_ref,
     ow_ref, iw_ref, own_ref, other_ref, gated_ref, br_ref, decay_ref, fwd_ref, inv_ref, q_ref, key_ref, conv_ref, fh_ref,
@@ -243,7 +243,7 @@
     length, width = q_ref.shape
     rows_own, features = own_ref.shape
     half = length - GAP
-    split, core = scalar_ref[0], scalar_ref[1]
+    split, core = split_ref[0, 0], lax.axis_index("dp") % 2
     strips = width // STRIP
     part = pl.ds(pl.multiple_of(core * width, STRIP), width)
     apart = pl.ds(pl.multiple_of((1 - core) * width, STRIP), width)
@@ -260,7 +260,7 @@
             (fh_hbm, fh_ref),
             (uh_hbm, uh_ref),
             (inv_hbm, inv_ref),
-            (decay_hbm, decay_ref),
+            (decay_hbm.at[core], decay_ref),
             (key_hbm, key_ref),
             (br_hbm, br_ref),
             (gated_hbm, gated_ref),
@@ -420,8 +420,8 @@
     return [((width, LANES), BF), ((3 * width, LANES), BF), ((LANES, width), F32), ((LANES, 3 * width), F32)]
 
 
-def mixer_forward(layer, scalars, own, other, ch, st, weight, decay, fwd, inv):
-    length, width = decay.shape
+def mixer_forward(layer, split, own, other, ch, st, weight, decay, fwd, inv):
+    _, length, width = decay.shape
     features = own.shape[1]
     bins = fwd.shape[0]
     tall, short, wide = (length, width), (own.shape[0], width), (length, 3 * width)
@@ -436,7 +436,7 @@
     ]
     return local_call(
         functools.partial(mixer_forward_kernel, layer),
-        (scalars, own, other, ch, st, weight, decay, fwd, inv),
+        (split, own, other, ch, st, weight, decay, fwd, inv),
         3,
         [(tall, BF), (short, BF), (short, BF)] + kept,
         3,
@@ -445,13 +445,14 @@
 
 
 def mixer_backward(
-    layer, scalars, mid_own, mid_other, dmg, ch, st, weight, own, other, gated, br, decay, fwd, inv, q, key, conv, fh, uh
+    layer, split, mid_own, mid_other, dmg, ch, st, weight, own, other, gated, br, decay, fwd, inv, q, key, conv, fh, uh
 ):
-    length, width = decay.shape
+    _, length, width = decay.shape
     bins = fwd.shape[0]
     rows, features = mid_own.shape
     held = (own, other, gated, br, decay, fwd, inv, q, key, conv, fh, uh)
-    scratch = [((2, width, width), BF), ((features, 3 * width), BF)] + [(x.shape, x.dtype) for x in held] + tap_scratch(width)
+    scratch = [((2, width, width), BF), ((features, 3 * width), BF)]
+    scratch += [(x.shape[1:] if x is decay else x.shape, x.dtype) for x in held] + tap_scratch(width)
     scratch += [
         ((length + 16, 3 * width), F32),
         ((length + 16, width), F32),
@@ -467,7 +468,7 @@
     ]
     return local_call(
         functools.partial(mixer_backward_kernel, layer),
-        (scalars, mid_own, mid_other, dmg, ch, st, weight) + held,
+        (split, mid_own, mid_other, dmg, ch, st, weight) + held,
         4,
         [
             ((2, features, 4 * width), BF),
@@ -845,7 +846,7 @@
 
 
 def mlp_forward_kernel(
-    gain, next_gain, scalar_ref, x_ref, g0_ref, g1_ref, o0_ref, o1_ref, gains_ref, wg_ref, wu_ref, d0_ref, d1_ref,
+    gain, next_gain, x_ref, g0_ref, g1_ref, o0_ref, o1_ref, gains_ref, wg_ref, wu_ref, d0_ref, d1_ref,
     mid_ref, hm_ref, pre_ref, out_ref, next_ref,
 ):
     j = pl.program_id(0)
@@ -854,7 +855,8 @@
     def _():
         width = g0_ref.shape[1]
         mid = x_ref[...]
-        for ref, side in ((g0_ref, scalar_ref[1]), (g1_ref, 1 - scalar_ref[1])):
+        core = lax.axis_index("dp") % 2
+        for ref, side in ((g0_ref, core), (g1_ref, 1 - core)):
             rows = pl.ds(pl.multiple_of(side * width, STRIP), width)
             mid += dot(ref[...], jnp.concatenate([o0_ref[rows, :], o1_ref[rows, :]], axis=1))
         mid_ref[...] = mid
@@ -943,7 +945,7 @@
     return [gate_up, up] + down
 
 
-def mlp_forward(scalars, x, g0, g1, weight, gains, gain, next_gain, weights):
+def mlp_forward(x, g0, g1, weight, gains, gain, next_gain, weights):
     layout, gu, dn = weights
     rows, features = x.shape
     hidden = dn.shape[0] // 2
@@ -955,10 +957,10 @@
         functools.partial(mlp_forward_kernel, gain, next_gain),
         grid=(hidden // TILE,),
         out_shape=[jax.ShapeDtypeStruct(*s) for s in shapes],
-        in_specs=[pl.BlockSpec(memory_space=pltpu.SMEM), square] + narrow + [whole(gains.shape)] + weight_specs(layout, hidden, features),
+        in_specs=[square] + narrow + [whole(gains.shape)] + weight_specs(layout, hidden, features),
         out_specs=[square, square, pl.BlockSpec((2, rows, TILE), lambda j: (0, 0, j)), square, square],
         compiler_params=pltpu.CompilerParams(vmem_limit_bytes=VMEM_LIMIT),
-    )(scalars, x, g0, g1, weight, weight, gains, gu, gu, dn, dn)
+    )(x, g0, g1, weight, weight, gains, gu, gu, dn, dn)
 
 
 def mlp_backward(g, hm, mid, gains, gain, pre, weights, side_by_side):
@@ -1023,16 +1025,10 @@
         size = x.shape[axis] // 2
         return lax.dynamic_slice_in_dim(x, which * size, size, axis)
 
-    def own_channels(x):
-        parts = x.shape[-1] // features
-        x = x.reshape(x.shape[:-1] + (parts, 2, width))
-        x = lax.dynamic_index_in_dim(x, core, x.ndim - 2, keepdims=False)
-        return x.reshape(x.shape[:-2] + (parts * width,))
-
     table = transform_matrix(length)
     fwd = jnp.asarray(table, BF)
     inv = jnp.asarray(np.ascontiguousarray(table.T), BF)
-    decay = own_channels(decay_table(length, features))
+    decay = jnp.asarray(decay_table(length, features))
 
     def halves(x):
         parts = x.shape[-1] // features
@@ -1058,7 +1054,6 @@
     gate_ups = [("halves", full[0].reshape(2 * features, hidden))]
     gate_ups += [("plain", lax.all_gather(x, AXES, axis=0, tiled=True)) for x in late]
     gains = ch[:, :, :2].astype(F32).transpose(0, 2, 1).reshape(2 * layers, features)
-    scalars = jnp.stack([split[0, 0], core.astype(jnp.int32)])
     stream, far = x_low.astype(F32), x_far.astype(F32)
     grad = swap_rows(cotangent)[0].astype(F32)
     normed, normed_far = [(norm_parts(x)[0] * gains[0]).astype(BF) for x in (stream, far)]
@@ -1067,10 +1062,10 @@
         if layer > 0:
             normed_far = sibling(normed)
         gated, mine, away, branches, q, key, conv, fh, uh = mixer_forward(
-            layer, scalars, normed, normed_far, ch, st, mixer_w[layer], decay, fwd, inv
+            layer, split, normed, normed_far, ch, st, mixer_w[layer], decay, fwd, inv
         )
         middle, normed_mlp, pre, out, normed_next = mlp_forward(
-            scalars, stream, mine, sibling(away), mixer_w[layer].reshape(2 * features, -1), gains,
+            stream, mine, sibling(away), mixer_w[layer].reshape(2 * features, -1), gains,
             2 * layer + 1, (2 * layer + 2) % (2 * layers), gate_ups[layer] + (downs[layer],),
         )
         kept.append((stream, normed, normed_far, gated, branches, q, key, conv, fh, uh, middle, normed_mlp, pre))
@@ -1085,7 +1080,7 @@
             grad, normed_mlp, middle, gains, 2 * layer + 1, pre, gate_ups[layer] + (downs[layer],), layer > 0
         )
         rest, d_normed, d_away, d_ch, d_st = mixer_backward(
-            layer, scalars, m_low, sibling(m_low), d_mg, ch, st, mixer_w[layer], normed, normed_far, gated, branches,
+            layer, split, m_low, sibling(m_low), d_mg, ch, st, mixer_w[layer], normed, normed_far, gated, branches,
             decay, fwd, inv, q, key, conv, fh, uh,
         )
         if layer > 0:

time: 573 us -> 574 us (level)
  transfers between devices with their start and end apart: 10 -> 10, of which waited for: 5 -> 5; matrix products, arithmetic and copies ran while one was open for 6% -> 5% of each run, Pallas kernels for 52% -> 52%
where the time goes in v5:
time: 574 us; the launch traced here: 563 us
  Pallas kernels  477 us (83%)
  local copies, waits for them, and re-layouts  23.1 us (4%)
  other arithmetic  23.1 us (4%)
  waiting for transfers between devices  16.9 us (3%)
  between operations  15.9 us (3%)
  starting transfers between devices  6.81 us (1%)
    pallas_call x1, Pallas kernels, gather_weights(): pl.pallas_call(body, out_shape=[jax.ShapeDtypeStruct(x.shape, x.dtype) fo...  142 us
    pallas_call x1, Pallas kernels, scatter_grads(): pl.pallas_call(body, out_shape=[jax.ShapeDtypeStruct((rows, features), BF...  140 us
    pallas_call x4, Pallas kernels, local_call(): pl.pallas_call(kernel, out_shape=[jax.ShapeDtypeStruct(shape, dtype) for...  107 us
    pallas_call x2, Pallas kernels, mlp_backward(): pl.pallas_call(functools.partial(mlp_backward_kernel, gain), grid=(hidden...  52.6 us
    pallas_call x2, Pallas kernels, mlp_forward(): pl.pallas_call(functools.partial(mlp_forward_kernel, gain, next_gain), gr...  35.3 us
    all_gather x1, waiting for transfers between devices, shards(): lax.all_gather(x, AXES, axis=0, tiled=True)  12.2 us
  transfers between devices with their start and end apart: 10, of which 5 were waited for; matrix products, arithmetic and copies ran while one was open for 5% of the time, Pallas kernels for 52%

profile of v5, /device:TPU:1, one launch (start us, length us, event | category | flops | bytes accessed | tf_op | source)
XLA Modules:
  0.0 563.2 jit_solution(8386321531566052566)
XLA Ops:
  7.9 1.8 fusion.7
  16.2 142.1 %shard_map.216 = (bf16[512,768]{1,0:T(8,128)(2,1)}, s32[8,128]{1,0:T(8,128)}, bf16[512,768]{1,0:T(8,128)(2,1)}, bf16[2,2,2,2,2,2,24,3072]{7,6,5,4,3,2,1,0:T(8,12...) custom-call(bf16[512,768]{1,0:T(8,128)(2,1)} %bitcast.135, ...), custom_call_target="tpu_custom_call" | custom-call | tf_op jit(solution)/shard_map/pallas_call | solution.py:659
  158.4 1.2 convert_bitcast_fusion
  161.5 1.7 fusion.4
  163.1 21.4 %shard_map.217 = (bf16[1024,384]{1,0:T(8,128)(2,1)}, bf16[512,384]{1,0:T(8,128)(2,1)}, bf16[512,384]{1,0:T(8,128)(2,1)}, bf16[1024,1152]{1,0:T(8,128)(2,1)}, bf1...) custom-call(s32[8,128]{1,0:T(8,128)} %get-tuple-element.78.split_ref, ...), custom_call_target="tpu_custom_call" | custom-call | tf_op jit(solution)/shard_map/pallas_call | solution.py:407
  184.8 1.3 convert_element_type.54.x_ref
  187.3 17.7 %shard_map.218 = (f32[512,768]{1,0:T(8,128)}, bf16[512,768]{1,0:T(8,128)(2,1)}, bf16[2,512,3072]{2,1,0:T(8,128)(2,1)}, f32[512,768]{1,0:T(8,128)}, bf16[512,768]{1,0:T(8,128)(2,1)}) custom-call(f32[512,768]{1,0:T(8,128)} %convert_element_type.54.x_ref, bf16[512,384]{1,0:T(8,128)(2,1)} %get-tuple-element.83.g0_ref, bf16[512,384]{1,0:T(8,128)(2,1)} %copy-done.14, ...), custom_call_target="tpu_custom_call" | custom-call | tf_op jit(solution)/shard_map/pallas_call | solution.py:956
  205.2 1.9 collective-permute-start.4
  207.1 1.5 collective-permute-done.1.other_ref.other_hbm
  208.7 0.9 copy-done.4
  209.6 21.5 %shard_map.219 = (bf16[1024,384]{1,0:T(8,128)(2,1)}, bf16[512,384]{1,0:T(8,128)(2,1)}, bf16[512,384]{1,0:T(8,128)(2,1)}, bf16[1024,1152]{1,0:T(8,128)(2,1)}, bf1...) custom-call(s32[8,128]{1,0:T(8,128)} %get-tuple-element.78.split_ref, ...), custom_call_target="tpu_custom_call" | custom-call | tf_op jit(solution)/shard_map/pallas_call | solution.py:407
  231.3 1.0 collective-permute-done.4
  232.3 1.2 bitcast_convert_fusion.1.g_ref
  233.6 12.2 %all-gather.3.cloned.1.call-done = bf16[1,768,6144]{2,1,0:T(8,128)(2,1)} async-done(((bf16[1,24,6144]{2,1,0:T(8,128)(2,1)}), bf16[1,768,6144]{2,1,0:T(8,128)(2,1)}) %all-gather.3.cloned.1.call-update) | async-done | bytes 9437200 | tf_op jit(solution)/shard_map/all_gather | solution.py:1055
  245.8 17.6 %shard_map.220 = (f32[512,768]{1,0:T(8,128)}, bf16[512,768]{1,0:T(8,128)(2,1)}, bf16[2,512,3072]{2,1,0:T(8,128)(2,1)}, f32[512,768]{1,0:T(8,128)}, bf16[512,768]{1,0:T(8,128)(2,1)}) custom-call(f32[512,768]{1,0:T(8,128)} %get-tuple-element.87.x_ref, bf16[512,384]{1,0:T(8,128)(2,1)} %get-tuple-element.90.g0_ref, bf16[512,384]{1,0:T(8,128)(2,1)} %copy-done.13, ...), custom_call_target="tpu_custom_call" | custom-call | tf_op jit(solution)/shard_map/pallas_call | solution.py:956
  263.4 26.4 %shard_map.221 = (bf16[768,6144]{1,0:T(8,128)(2,1)}, bf16[2,3072,384]{2,1,0:T(8,128)(2,1)}, f32[512,768]{1,0:T(8,128)}, bf16[512,768]{1,0:T(8,128)(2,1)}, f32[1,768]{1,0:T(1,128)}) custom-call(f32[512,768]{1,0:T(8,128)} %bitcast_convert_fusion.1.g_ref, bf16[512,768]{1,0:T(8,128)(2,1)} %get-tuple-element.95.hm_ref, f32[512,768]{1,0:T(8,128)} %get-tuple-element.96.mid_ref, ...), custom_call_target="tpu_custom_call" | custom-call | tf_op jit(solution)/shard_map/pallas_call | solution.py:974
  289.8 1.1 copy-done.9
  291.6 1.6 collective-permute-done.5.mid_other_ref
  294.1 32.3 %shard_map.222 = (bf16[2,768,1536]{2,1,0:T(8,128)(2,1)}, bf16[512,768]{1,0:T(8,128)(2,1)}, bf16[512,768]{1,0:T(8,128)(2,1)}, bf16[768,128]{1,0:T(8,128)(2,1)}, bf16[2304,128]{1,0:T(8,128)(2,1)}) custom-call(s32[8,128]{1,0:T(8,128)} %get-tuple-element.78.split_ref, bf16[512,768]{1,0:T(8,128)(2,1)} %get-tuple-element.99.mid_own_ref, ...), custom_call_target="tpu_custom_call" | custom-call | tf_op jit(solution)/shard_map/pallas_call | solution.py:407
  327.8 1.0 convert_bitcast_fusion.1
  328.8 3.6 collective-permute-start.3
  333.8 1.8 multiply_add_fusion.g_ref
  335.6 26.2 %shard_map.223 = (bf16[2,768,3072]{2,1,0:T(8,128)(2,1)}, bf16[2,3072,384]{2,1,0:T(8,128)(2,1)}, f32[512,768]{1,0:T(8,128)}, bf16[512,768]{1,0:T(8,128)(2,1)}, f32[1,768]{1,0:T(1,128)}) custom-call(f32[512,768]{1,0:T(8,128)} %multiply_add_fusion.g_ref, bf16[512,768]{1,0:T(8,128)(2,1)} %get-tuple-element.110.hm_ref, f32[512,768]{1,0:T(8,128)} %get-tuple-element.111.mid_ref, ...), custom_call_target="tpu_custom_call" | custom-call | tf_op jit(solution)/shard_map/pallas_call | solution.py:974
  361.9 2.2 broadcast_select_fusion
  365.5 32.2 %shard_map.224 = (bf16[2,768,1536]{2,1,0:T(8,128)(2,1)}, bf16[512,768]{1,0:T(8,128)(2,1)}, bf16[512,768]{1,0:T(8,128)(2,1)}, bf16[768,128]{1,0:T(8,128)(2,1)}, bf16[2304,128]{1,0:T(8,128)(2,1)}) custom-call(s32[8,128]{1,0:T(8,128)} %get-tuple-element.78.split_ref, bf16[512,768]{1,0:T(8,128)(2,1)} %get-tuple-element.113.mid_own_ref, ...), custom_call_target="tpu_custom_call" | custom-call | tf_op jit(solution)/shard_map/pallas_call | solution.py:407
  397.7 1.7 pad_maximum_fusion.1.refs_11_
  399.4 2.2 pad_maximum_fusion.refs_12_
  401.6 140.0 %shard_map.225 = (bf16[512,768]{1,0:T(8,128)(2,1)}, bf16[2,24,3072]{2,1,0:T(8,128)(2,1)}, bf16[2,4,24,384]{3,2,1,0:T(8,128)(2,1)}, bf16[2,4,24,384]{3,2,1,0:T(8,...) custom-call(bf16[512,768]{1,0:T(8,128)(2,1)} %get-tuple-element.77.r, ...), custom_call_target="tpu_custom_call" | custom-call | tf_op jit(solution)/shard_map/pallas_call | solution.py:803
  541.7 1.0 slice.74
  551.1 1.3 bitcast_convert_fusion
  553.1 1.2 reshape.169
  554.8 1.1 maximum_convert_fusion
  (150 shorter events, 25.6 us)
Async XLA Ops:
  7.2 3.5 copy-start.16
  7.2 238.6 %all-gather.3.cloned.1.call-start = ((), (), s32[]{:S(2)}) async-start(), calls=%async_computation.2 | async-start | bytes 9732096 | tf_op jit(solution)/shard_map/all_gather | solution.py:1055
  9.7 2.5 copy-start.22
  9.7 2.5 copy-start.18
  10.8 2.0 copy-start.27
  10.8 2.0 copy-start.28
  10.8 2.0 copy-start.29
  10.8 2.1 copy-start.26
  158.3 1.6 copy-start.1
  158.3 1.7 copy-start.2
  158.3 394.8 %reduce-scatter.2.cloned.1.call-start = ((), (), s32[]{:S(2)}) async-start(), calls=%async_computation.1 | async-start | bytes 9732096 | tf_op jit(solution)/shard_map/reduce_scatter | solution.py:1087
  184.6 2.0 collective-permute-start
  187.3 17.9 %copy-start.8 = (bf16[1,512,768]{2,1,0:T(8,128)(2,1)S(1)}, bf16[1,512,768]{2,1,0:T(8,128)(2,1)}, u32[]{:S(2)}) copy-start(bf16[1,512,768]{2,1,0:T(8,128)(2,1)} %param.16) | copy-start | bytes 2359300
  205.0 3.7 collective-permute-start.1
  205.2 27.1 %collective-permute-start.4 = (bf16[1,512,768]{2,1,0:T(8,128)(2,1)S(1)}, bf16[1,512,768]{2,1,0:T(8,128)(2,1)S(1)}, u32[]{:S(2)}, u32[]{:S(2)}) collective-permute-start(bf16[1,512,768]{2,1,0:T(8,128)(2,1)S(1)} %copy-done.8), channel_id=1, source_target_pairs={{1,2},{2,1},{5,6},{6,5},{9,10},{10,9},{13,14},{14,13},{17,18},{18,... | collective-permute-start | bytes 2359304 | tf_op jit(solution)/shard_map/ppermute | solution.py:1012
  231.1 2.4 collective-permute-start.2
  233.6 12.2 %copy-start.13 = (bf16[512,384]{1,0:T(8,128)(2,1)}, bf16[512,384]{1,0:T(8,128)(2,1)S(1)}, u32[]{:S(2)}) copy-start(bf16[512,384]{1,0:T(8,128)(2,1)S(1)} %collective-permute-done.2.g1_ref) | copy-start | bytes 1179652
  289.8 1.6 copy-start
  290.9 2.3 collective-permute-start.5
  326.4 6.0 %collective-permute-start.6 = (bf16[512,768]{1,0:T(8,128)(2,1)}, bf16[512,768]{1,0:T(8,128)(2,1)S(1)}, u32[]{:S(2)}, u32[]{:S(2)}) collective-permute-start(bf16[512,768]{1,0:T(8,128)(2,1)} %get-tuple-element.109), channel_id=1, source_target_pairs={{0,2},{2,0},{4,6},{6,4},{8,10},{10,8},{12,14},{14,12},{16,18},{18,... | collective-permute-start | bytes 2359304 | tf_op jit(solution)/shard_map/ppermute | solution.py:1015
  327.0 5.4 copy-start.5
  328.8 33.1 %collective-permute-start.3 = (bf16[1,512,768]{2,1,0:T(8,128)(2,1)}, bf16[1,512,768]{2,1,0:T(8,128)(2,1)}, u32[]{:S(2)}, u32[]{:S(2)}) collective-permute-start(bf16[1,512,768]{2,1,0:T(8,128)(2,1)} %convert_bitcast_fusion.1), channel_id=1, source_target_pairs={{1,2},{2,1},{5,6},{6,5},{9,10},{10,9},{13,14},{14,13},{17,18},{18,... | collective-permute-start | bytes 2359304 | tf_op jit(solution)/shard_map/ppermute | solution.py:1012
  361.8 2.8 collective-permute-start.7
  365.5 32.2 %copy-start.19 = (bf16[768,128]{1,0:T(8,128)(2,1)S(1)}, bf16[768,128]{1,0:T(8,128)(2,1)}, u32[]{:S(2)}) copy-start(bf16[768,128]{1,0:T(8,128)(2,1)} %get-tuple-element.131) | copy-start | bytes 589828
  365.5 33.9 %copy-start.12 = (bf16[2304,128]{1,0:T(8,128)(2,1)S(1)}, bf16[2304,128]{1,0:T(8,128)(2,1)}, u32[]{:S(2)}) copy-start(bf16[2304,128]{1,0:T(8,128)(2,1)} %get-tuple-element.133) | copy-start | bytes 1769476
  541.6 2.4 copy-start.23
  541.7 3.1 copy-start.25
  541.7 5.5 copy-start.17
  542.8 4.9 copy-start.21
  543.8 4.2 copy-start.20
  544.0 4.2 copy-start.24
  547.5 3.6 copy-start.7
  (8 other events, 8.5 us)
Sparse Core Ops, SparseCore 0:
  158.5 87.2 all-gather.2
  289.9 135.3 reduce-scatter.1

commit v6 on v5

--- a/solution.py
+++ b/solution.py
@@ -1055,7 +1055,8 @@
     gate_ups += [("plain", lax.all_gather(x, AXES, axis=0, tiled=True)) for x in late]
     gains = ch[:, :, :2].astype(F32).transpose(0, 2, 1).reshape(2 * layers, features)
     stream, far = x_low.astype(F32), x_far.astype(F32)
-    grad = swap_rows(cotangent)[0].astype(F32)
+    arrived, _ = lax.optimization_barrier((cotangent, gate_ups[-1][1]))
+    grad = swap_rows(arrived)[0].astype(F32)
     normed, normed_far = [(norm_parts(x)[0] * gains[0]).astype(BF) for x in (stream, far)]
     kept = []
     for layer in range(layers):

time: 574 us -> 595 us (1.037)
  waiting for transfers between devices: 16.9 us -> 37 us
    all_gather x1, waiting for transfers between devices: 12.2 us -> 32.9 us  [shards(): lax.all_gather(x, AXES, axis=0, tiled=True)]
  transfers between devices with their start and end apart: 10 -> 10, of which waited for: 5 -> 4; matrix products, arithmetic and copies ran while one was open for 5% -> 5% of each run, Pallas kernels for 52% -> 53%
where the time goes in v6:
time: 595 us; the launch traced here: 585 us
  Pallas kernels  478 us (80%)
  waiting for transfers between devices  37 us (6%)
  local copies, waits for them, and re-layouts  24 us (4%)
  other arithmetic  23.1 us (4%)
  between operations  16 us (3%)
  starting transfers between devices  6.99 us (1%)
    pallas_call x1, Pallas kernels, gather_weights(): pl.pallas_call(body, out_shape=[jax.ShapeDtypeStruct(x.shape, x.dtype) fo...  142 us
    pallas_call x1, Pallas kernels, scatter_grads(): pl.pallas_call(body, out_shape=[jax.ShapeDtypeStruct((rows, features), BF...  140 us
    pallas_call x4, Pallas kernels, local_call(): pl.pallas_call(kernel, out_shape=[jax.ShapeDtypeStruct(shape, dtype) for...  108 us
    pallas_call x2, Pallas kernels, mlp_backward(): pl.pallas_call(functools.partial(mlp_backward_kernel, gain), grid=(hidden...  52.6 us
    pallas_call x2, Pallas kernels, mlp_forward(): pl.pallas_call(functools.partial(mlp_forward_kernel, gain, next_gain), gr...  35.3 us
    all_gather x1, waiting for transfers between devices, shards(): lax.all_gather(x, AXES, axis=0, tiled=True)  32.9 us
  transfers between devices with their start and end apart: 10, of which 4 were waited for; matrix products, arithmetic and copies ran while one was open for 5% of the time, Pallas kernels for 53%

profile of v6, /device:TPU:1, one launch (start us, length us, event | category | flops | bytes accessed | tf_op | source)
XLA Modules:
  0.0 584.8 jit_solution(8600435761485516426)
XLA Ops:
  7.9 1.8 fusion.7
  16.2 142.1 %shard_map.216 = (bf16[512,768]{1,0:T(8,128)(2,1)}, s32[8,128]{1,0:T(8,128)}, bf16[512,768]{1,0:T(8,128)(2,1)}, bf16[2,2,2,2,2,2,24,3072]{7,6,5,4,3,2,1,0:T(8,12...) custom-call(bf16[512,768]{1,0:T(8,128)(2,1)} %bitcast.135, ...), custom_call_target="tpu_custom_call" | custom-call | tf_op jit(solution)/shard_map/pallas_call | solution.py:659
  158.4 1.2 convert_bitcast_fusion
  161.5 1.7 fusion.4
  163.2 21.4 %shard_map.217 = (bf16[1024,384]{1,0:T(8,128)(2,1)}, bf16[512,384]{1,0:T(8,128)(2,1)}, bf16[512,384]{1,0:T(8,128)(2,1)}, bf16[1024,1152]{1,0:T(8,128)(2,1)}, bf1...) custom-call(s32[8,128]{1,0:T(8,128)} %get-tuple-element.79.split_ref, ...), custom_call_target="tpu_custom_call" | custom-call | tf_op jit(solution)/shard_map/pallas_call | solution.py:407
  184.8 1.3 convert_element_type.54.x_ref
  187.3 17.7 %shard_map.218 = (f32[512,768]{1,0:T(8,128)}, bf16[512,768]{1,0:T(8,128)(2,1)}, bf16[2,512,3072]{2,1,0:T(8,128)(2,1)}, f32[512,768]{1,0:T(8,128)}, bf16[512,768]{1,0:T(8,128)(2,1)}) custom-call(f32[512,768]{1,0:T(8,128)} %convert_element_type.54.x_ref, bf16[512,384]{1,0:T(8,128)(2,1)} %get-tuple-element.84.g0_ref, bf16[512,384]{1,0:T(8,128)(2,1)} %copy-done.14, ...), custom_call_target="tpu_custom_call" | custom-call | tf_op jit(solution)/shard_map/pallas_call | solution.py:956
  205.2 32.9 %all-gather.3.cloned.1.call-done = bf16[1,768,6144]{2,1,0:T(8,128)(2,1)} async-done(((bf16[1,24,6144]{2,1,0:T(8,128)(2,1)}), bf16[1,768,6144]{2,1,0:T(8,128)(2,1)}) %all-gather.3.cloned.1.call-update) | async-done | bytes 9437200 | tf_op jit(solution)/shard_map/all_gather | solution.py:1055
  238.1 3.2 collective-permute-start.4
  241.4 0.9 copy-done.4
  242.3 21.5 %shard_map.219 = (bf16[1024,384]{1,0:T(8,128)(2,1)}, bf16[512,384]{1,0:T(8,128)(2,1)}, bf16[512,384]{1,0:T(8,128)(2,1)}, bf16[1024,1152]{1,0:T(8,128)(2,1)}, bf1...) custom-call(s32[8,128]{1,0:T(8,128)} %get-tuple-element.79.split_ref, ...), custom_call_target="tpu_custom_call" | custom-call | tf_op jit(solution)/shard_map/pallas_call | solution.py:407
  263.9 1.9 collective-permute-done.2.g1_ref
  266.6 17.6 %shard_map.220 = (f32[512,768]{1,0:T(8,128)}, bf16[512,768]{1,0:T(8,128)(2,1)}, bf16[2,512,3072]{2,1,0:T(8,128)(2,1)}, f32[512,768]{1,0:T(8,128)}, bf16[512,768]{1,0:T(8,128)(2,1)}) custom-call(f32[512,768]{1,0:T(8,128)} %get-tuple-element.88.x_ref, bf16[512,384]{1,0:T(8,128)(2,1)} %get-tuple-element.91.g0_ref, bf16[512,384]{1,0:T(8,128)(2,1)} %copy-done.13, ...), custom_call_target="tpu_custom_call" | custom-call | tf_op jit(solution)/shard_map/pallas_call | solution.py:956
  284.2 1.2 bitcast_convert_fusion.1.g_ref
  285.4 26.4 %shard_map.221 = (bf16[768,6144]{1,0:T(8,128)(2,1)}, bf16[2,3072,384]{2,1,0:T(8,128)(2,1)}, f32[512,768]{1,0:T(8,128)}, bf16[512,768]{1,0:T(8,128)(2,1)}, f32[1,768]{1,0:T(1,128)}) custom-call(f32[512,768]{1,0:T(8,128)} %bitcast_convert_fusion.1.g_ref, bf16[512,768]{1,0:T(8,128)(2,1)} %get-tuple-element.97.hm_ref, f32[512,768]{1,0:T(8,128)} %get-tuple-element.98.mid_ref, ...), custom_call_target="tpu_custom_call" | custom-call | tf_op jit(solution)/shard_map/pallas_call | solution.py:974
  311.8 1.1 copy-done.9
  313.6 1.6 collective-permute-done.5.mid_other_ref
  316.1 32.3 %shard_map.222 = (bf16[2,768,1536]{2,1,0:T(8,128)(2,1)}, bf16[512,768]{1,0:T(8,128)(2,1)}, bf16[512,768]{1,0:T(8,128)(2,1)}, bf16[768,128]{1,0:T(8,128)(2,1)}, bf16[2304,128]{1,0:T(8,128)(2,1)}) custom-call(s32[8,128]{1,0:T(8,128)} %get-tuple-element.79.split_ref, bf16[512,768]{1,0:T(8,128)(2,1)} %get-tuple-element.101.mid_own_ref, ...), custom_call_target="tpu_custom_call" | custom-call | tf_op jit(solution)/shard_map/pallas_call | solution.py:407
  348.9 0.9 copy-done.3
  349.9 1.0 convert_bitcast_fusion.1
  350.8 2.8 collective-permute-start.3
  355.1 1.8 multiply_add_fusion.g_ref
  356.8 26.2 %shard_map.223 = (bf16[2,768,3072]{2,1,0:T(8,128)(2,1)}, bf16[2,3072,384]{2,1,0:T(8,128)(2,1)}, f32[512,768]{1,0:T(8,128)}, bf16[512,768]{1,0:T(8,128)(2,1)}, f32[1,768]{1,0:T(1,128)}) custom-call(f32[512,768]{1,0:T(8,128)} %multiply_add_fusion.g_ref, bf16[512,768]{1,0:T(8,128)(2,1)} %get-tuple-element.112.hm_ref, f32[512,768]{1,0:T(8,128)} %get-tuple-element.113.mid_ref, ...), custom_call_target="tpu_custom_call" | custom-call | tf_op jit(solution)/shard_map/pallas_call | solution.py:974
  383.2 2.2 broadcast_select_fusion
  386.8 32.3 %shard_map.224 = (bf16[2,768,1536]{2,1,0:T(8,128)(2,1)}, bf16[512,768]{1,0:T(8,128)(2,1)}, bf16[512,768]{1,0:T(8,128)(2,1)}, bf16[768,128]{1,0:T(8,128)(2,1)}, bf16[2304,128]{1,0:T(8,128)(2,1)}) custom-call(s32[8,128]{1,0:T(8,128)} %get-tuple-element.79.split_ref, bf16[512,768]{1,0:T(8,128)(2,1)} %get-tuple-element.115.mid_own_ref, ...), custom_call_target="tpu_custom_call" | custom-call | tf_op jit(solution)/shard_map/pallas_call | solution.py:407
  419.1 1.7 pad_maximum_fusion.1.refs_11_
  420.8 2.2 pad_maximum_fusion.refs_12_
  423.0 140.2 %shard_map.225 = (bf16[512,768]{1,0:T(8,128)(2,1)}, bf16[2,24,3072]{2,1,0:T(8,128)(2,1)}, bf16[2,4,24,384]{3,2,1,0:T(8,128)(2,1)}, bf16[2,4,24,384]{3,2,1,0:T(8,...) custom-call(bf16[512,768]{1,0:T(8,128)(2,1)} %get-tuple-element.78.r, ...), custom_call_target="tpu_custom_call" | custom-call | tf_op jit(solution)/shard_map/pallas_call | solution.py:803
  563.3 1.0 slice.74
  572.7 1.3 bitcast_convert_fusion
  574.8 1.2 reshape.169
  576.4 1.1 maximum_convert_fusion
  (150 shorter events, 25.3 us)
Async XLA Ops:
  7.2 3.5 copy-start.16
  7.2 230.9 %all-gather.3.cloned.1.call-start = ((), (), s32[]{:S(2)}) async-start(), calls=%async_computation.2 | async-start | bytes 9732096 | tf_op jit(solution)/shard_map/all_gather | solution.py:1055
  9.7 2.5 copy-start.22
  9.7 2.5 copy-start.18
  10.8 2.0 copy-start.27
  10.8 2.0 copy-start.28
  10.8 2.0 copy-start.29
  10.8 2.1 copy-start.26
  158.3 1.6 copy-start.1
  158.3 1.7 copy-start.2
  158.4 416.4 %reduce-scatter.2.cloned.1.call-start = ((), (), s32[]{:S(2)}) async-start(), calls=%async_computation.1 | async-start | bytes 9732096 | tf_op jit(solution)/shard_map/reduce_scatter | solution.py:1088
  184.6 2.0 collective-permute-start
  187.3 50.8 %copy-start.8 = (bf16[1,512,768]{2,1,0:T(8,128)(2,1)S(1)}, bf16[1,512,768]{2,1,0:T(8,128)(2,1)}, u32[]{:S(2)}) copy-start(bf16[1,512,768]{2,1,0:T(8,128)(2,1)} %param.16) | copy-start | bytes 2359300
  205.0 36.4 %collective-permute-start.1 = (bf16[512,768]{1,0:T(8,128)(2,1)}, bf16[512,768]{1,0:T(8,128)(2,1)S(1)}, u32[]{:S(2)}, u32[]{:S(2)}) collective-permute-start(bf16[512,768]{1,0:T(8,128)(2,1)} %get-tuple-element.89.own_ref.own_hbm), channel_id=1, source_target_pairs={{0,2},{2,0},{4,6},{6,4},{8,10},{10,8},{12,14},{14,12},{16,18},{18,... | collective-permute-start | bytes 2359304 | tf_op jit(solution)/shard_map/ppermute | solution.py:1015
  238.1 46.0 %collective-permute-start.4 = (bf16[1,512,768]{2,1,0:T(8,128)(2,1)S(1)}, bf16[1,512,768]{2,1,0:T(8,128)(2,1)S(1)}, u32[]{:S(2)}, u32[]{:S(2)}) collective-permute-start(bf16[1,512,768]{2,1,0:T(8,128)(2,1)S(1)} %copy-done.8), channel_id=1, source_target_pairs={{1,2},{2,1},{5,6},{6,5},{9,10},{10,9},{13,14},{14,13},{17,18},{18,... | collective-permute-start | bytes 2359304 | tf_op jit(solution)/shard_map/ppermute | solution.py:1012
  263.8 2.0 collective-permute-start.2
  311.8 1.6 copy-start
  312.9 2.3 collective-permute-start.5
  348.4 1.5 copy-start.3
  348.4 5.3 collective-permute-start.6
  348.9 4.7 copy-start.5
  350.8 32.3 %collective-permute-start.3 = (bf16[1,512,768]{2,1,0:T(8,128)(2,1)}, bf16[1,512,768]{2,1,0:T(8,128)(2,1)}, u32[]{:S(2)}, u32[]{:S(2)}) collective-permute-start(bf16[1,512,768]{2,1,0:T(8,128)(2,1)} %convert_bitcast_fusion.1), channel_id=1, source_target_pairs={{1,2},{2,1},{5,6},{6,5},{9,10},{10,9},{13,14},{14,13},{17,18},{18,... | collective-permute-start | bytes 2359304 | tf_op jit(solution)/shard_map/ppermute | solution.py:1012
  383.1 2.8 collective-permute-start.7
  386.8 32.3 %copy-start.19 = (bf16[768,128]{1,0:T(8,128)(2,1)S(1)}, bf16[768,128]{1,0:T(8,128)(2,1)}, u32[]{:S(2)}) copy-start(bf16[768,128]{1,0:T(8,128)(2,1)} %get-tuple-element.133) | copy-start | bytes 589828
  386.8 34.1 %copy-start.12 = (bf16[2304,128]{1,0:T(8,128)(2,1)S(1)}, bf16[2304,128]{1,0:T(8,128)(2,1)}, u32[]{:S(2)}) copy-start(bf16[2304,128]{1,0:T(8,128)(2,1)} %get-tuple-element.135) | copy-start | bytes 1769476
  563.3 2.4 copy-start.23
  563.3 3.1 copy-start.25
  563.3 5.5 copy-start.17
  564.4 4.9 copy-start.21
  565.4 4.2 copy-start.20
  565.7 4.2 copy-start.24
  569.1 3.6 copy-start.7
  (8 other events, 7.8 us)
Sparse Core Ops, SparseCore 0:
  158.5 79.6 all-gather.2
  312.0 135.3 reduce-scatter.1

commit v7 on v5

--- a/solution.py
+++ b/solution.py
@@ -1055,7 +1055,6 @@
     gate_ups += [("plain", lax.all_gather(x, AXES, axis=0, tiled=True)) for x in late]
     gains = ch[:, :, :2].astype(F32).transpose(0, 2, 1).reshape(2 * layers, features)
     stream, far = x_low.astype(F32), x_far.astype(F32)
-    grad = swap_rows(cotangent)[0].astype(F32)
     normed, normed_far = [(norm_parts(x)[0] * gains[0]).astype(BF) for x in (stream, far)]
     kept = []
     for layer in range(layers):
@@ -1064,6 +1063,9 @@
         gated, mine, away, branches, q, key, conv, fh, uh = mixer_forward(
             layer, split, normed, normed_far, ch, st, mixer_w[layer], decay, fwd, inv
         )
+        if layer == layers - 1:
+            arrived, _, _ = lax.optimization_barrier((cotangent, gate_ups[-1][1], mine))
+            grad = swap_rows(arrived)[0].astype(F32)
         middle, normed_mlp, pre, out, normed_next = mlp_forward(
             stream, mine, sibling(away), mixer_w[layer].reshape(2 * features, -1), gains,
             2 * layer + 1, (2 * layer + 2) % (2 * layers), gate_ups[layer] + (downs[layer],),

time: 574 us -> 573 us (level)
  transfers between devices with their start and end apart: 10 -> 10, of which waited for: 5 -> 5; matrix products, arithmetic and copies ran while one was open for 5% -> 5% of each run, Pallas kernels for 52% -> 55%
where the time goes in v7:
time: 573 us; the launch traced here: 563 us
  Pallas kernels  479 us (84%)
  local copies, waits for them, and re-layouts  24 us (4%)
  other arithmetic  23.1 us (4%)
  between operations  15.9 us (3%)
  waiting for transfers between devices  14.5 us (3%)
  starting transfers between devices  6.97 us (1%)
    pallas_call x1, Pallas kernels, gather_weights(): pl.pallas_call(body, out_shape=[jax.ShapeDtypeStruct(x.shape, x.dtype) fo...  142 us
    pallas_call x1, Pallas kernels, scatter_grads(): pl.pallas_call(body, out_shape=[jax.ShapeDtypeStruct((rows, features), BF...  141 us
    pallas_call x4, Pallas kernels, local_call(): pl.pallas_call(kernel, out_shape=[jax.ShapeDtypeStruct(shape, dtype) for...  108 us
    pallas_call x2, Pallas kernels, mlp_backward(): pl.pallas_call(functools.partial(mlp_backward_kernel, gain), grid=(hidden...  52.6 us
    pallas_call x2, Pallas kernels, mlp_forward(): pl.pallas_call(functools.partial(mlp_forward_kernel, gain, next_gain), gr...  35.2 us
  transfers between devices with their start and end apart: 10, of which 5 were waited for; matrix products, arithmetic and copies ran while one was open for 5% of the time, Pallas kernels for 55%

profile of v7, /device:TPU:1, one launch (start us, length us, event | category | flops | bytes accessed | tf_op | source)
XLA Modules:
  0.0 563.1 jit_solution(2471969985204262918)
XLA Ops:
  7.9 1.8 fusion.7
  16.2 142.1 %shard_map.216 = (bf16[512,768]{1,0:T(8,128)(2,1)}, s32[8,128]{1,0:T(8,128)}, bf16[512,768]{1,0:T(8,128)(2,1)}, bf16[2,2,2,2,2,2,24,3072]{7,6,5,4,3,2,1,0:T(8,12...) custom-call(bf16[512,768]{1,0:T(8,128)(2,1)} %bitcast.135, ...), custom_call_target="tpu_custom_call" | custom-call | tf_op jit(solution)/shard_map/pallas_call | solution.py:659
  158.4 1.2 convert_bitcast_fusion
  161.5 1.7 fusion.4
  163.1 21.5 %shard_map.217 = (bf16[1024,384]{1,0:T(8,128)(2,1)}, bf16[512,384]{1,0:T(8,128)(2,1)}, bf16[512,384]{1,0:T(8,128)(2,1)}, bf16[1024,1152]{1,0:T(8,128)(2,1)}, bf1...) custom-call(s32[8,128]{1,0:T(8,128)} %get-tuple-element.79.split_ref, ...), custom_call_target="tpu_custom_call" | custom-call | tf_op jit(solution)/shard_map/pallas_call | solution.py:407
  184.8 1.3 convert_element_type.54.x_ref
  187.4 17.6 %shard_map.218 = (f32[512,768]{1,0:T(8,128)}, bf16[512,768]{1,0:T(8,128)(2,1)}, bf16[2,512,3072]{2,1,0:T(8,128)(2,1)}, f32[512,768]{1,0:T(8,128)}, bf16[512,768]{1,0:T(8,128)(2,1)}) custom-call(f32[512,768]{1,0:T(8,128)} %convert_element_type.54.x_ref, bf16[512,384]{1,0:T(8,128)(2,1)} %get-tuple-element.84.g0_ref, bf16[512,384]{1,0:T(8,128)(2,1)} %copy-done.14, ...), custom_call_target="tpu_custom_call" | custom-call | tf_op jit(solution)/shard_map/pallas_call | solution.py:956
  205.2 3.5 collective-permute-done.1.other_ref.other_hbm
  209.6 21.7 %shard_map.219 = (bf16[1024,384]{1,0:T(8,128)(2,1)}, bf16[512,384]{1,0:T(8,128)(2,1)}, bf16[512,384]{1,0:T(8,128)(2,1)}, bf16[1024,1152]{1,0:T(8,128)(2,1)}, bf1...) custom-call(s32[8,128]{1,0:T(8,128)} %get-tuple-element.79.split_ref, ...), custom_call_target="tpu_custom_call" | custom-call | tf_op jit(solution)/shard_map/pallas_call | solution.py:407
  231.3 6.9 %all-gather.3.cloned.1.call-done = bf16[1,768,6144]{2,1,0:T(8,128)(2,1)} async-done(((bf16[1,24,6144]{2,1,0:T(8,128)(2,1)}), bf16[1,768,6144]{2,1,0:T(8,128)(2,1)}) %all-gather.3.cloned.1.call-update) | async-done | bytes 9437200 | tf_op jit(solution)/shard_map/all_gather | solution.py:1055
  238.2 3.2 collective-permute-start.4
  241.5 1.9 collective-permute-done.2.g1_ref
  244.1 17.6 %shard_map.220 = (f32[512,768]{1,0:T(8,128)}, bf16[512,768]{1,0:T(8,128)(2,1)}, bf16[2,512,3072]{2,1,0:T(8,128)(2,1)}, f32[512,768]{1,0:T(8,128)}, bf16[512,768]{1,0:T(8,128)(2,1)}) custom-call(f32[512,768]{1,0:T(8,128)} %get-tuple-element.88.x_ref, bf16[512,384]{1,0:T(8,128)(2,1)} %get-tuple-element.91.g0_ref, bf16[512,384]{1,0:T(8,128)(2,1)} %copy-done.13, ...), custom_call_target="tpu_custom_call" | custom-call | tf_op jit(solution)/shard_map/pallas_call | solution.py:956
  261.7 1.2 bitcast_convert_fusion.1.g_ref
  263.0 26.4 %shard_map.221 = (bf16[768,6144]{1,0:T(8,128)(2,1)}, bf16[2,3072,384]{2,1,0:T(8,128)(2,1)}, f32[512,768]{1,0:T(8,128)}, bf16[512,768]{1,0:T(8,128)(2,1)}, f32[1,768]{1,0:T(1,128)}) custom-call(f32[512,768]{1,0:T(8,128)} %bitcast_convert_fusion.1.g_ref, bf16[512,768]{1,0:T(8,128)(2,1)} %get-tuple-element.97.hm_ref, f32[512,768]{1,0:T(8,128)} %get-tuple-element.98.mid_ref, ...), custom_call_target="tpu_custom_call" | custom-call | tf_op jit(solution)/shard_map/pallas_call | solution.py:974
  289.4 1.1 copy-done.9
  291.2 1.6 collective-permute-done.5.mid_other_ref
  293.7 32.2 %shard_map.222 = (bf16[2,768,1536]{2,1,0:T(8,128)(2,1)}, bf16[512,768]{1,0:T(8,128)(2,1)}, bf16[512,768]{1,0:T(8,128)(2,1)}, bf16[768,128]{1,0:T(8,128)(2,1)}, bf16[2304,128]{1,0:T(8,128)(2,1)}) custom-call(s32[8,128]{1,0:T(8,128)} %get-tuple-element.79.split_ref, bf16[512,768]{1,0:T(8,128)(2,1)} %get-tuple-element.101.mid_own_ref, ...), custom_call_target="tpu_custom_call" | custom-call | tf_op jit(solution)/shard_map/pallas_call | solution.py:407
  326.4 0.9 copy-done.3
  327.4 1.0 convert_bitcast_fusion.1
  328.3 2.8 collective-permute-start.3
  332.6 1.8 multiply_add_fusion.g_ref
  334.4 26.3 %shard_map.223 = (bf16[2,768,3072]{2,1,0:T(8,128)(2,1)}, bf16[2,3072,384]{2,1,0:T(8,128)(2,1)}, f32[512,768]{1,0:T(8,128)}, bf16[512,768]{1,0:T(8,128)(2,1)}, f32[1,768]{1,0:T(1,128)}) custom-call(f32[512,768]{1,0:T(8,128)} %multiply_add_fusion.g_ref, bf16[512,768]{1,0:T(8,128)(2,1)} %get-tuple-element.112.hm_ref, f32[512,768]{1,0:T(8,128)} %get-tuple-element.113.mid_ref, ...), custom_call_target="tpu_custom_call" | custom-call | tf_op jit(solution)/shard_map/pallas_call | solution.py:974
  360.7 2.2 broadcast_select_fusion
  364.3 32.2 %shard_map.224 = (bf16[2,768,1536]{2,1,0:T(8,128)(2,1)}, bf16[512,768]{1,0:T(8,128)(2,1)}, bf16[512,768]{1,0:T(8,128)(2,1)}, bf16[768,128]{1,0:T(8,128)(2,1)}, bf16[2304,128]{1,0:T(8,128)(2,1)}) custom-call(s32[8,128]{1,0:T(8,128)} %get-tuple-element.79.split_ref, bf16[512,768]{1,0:T(8,128)(2,1)} %get-tuple-element.115.mid_own_ref, ...), custom_call_target="tpu_custom_call" | custom-call | tf_op jit(solution)/shard_map/pallas_call | solution.py:407
  396.6 1.7 pad_maximum_fusion.1.refs_11_
  398.3 2.2 pad_maximum_fusion.refs_12_
  400.5 141.0 %shard_map.225 = (bf16[512,768]{1,0:T(8,128)(2,1)}, bf16[2,24,3072]{2,1,0:T(8,128)(2,1)}, bf16[2,4,24,384]{3,2,1,0:T(8,128)(2,1)}, bf16[2,4,24,384]{3,2,1,0:T(8,...) custom-call(bf16[512,768]{1,0:T(8,128)(2,1)} %get-tuple-element.78.r, ...), custom_call_target="tpu_custom_call" | custom-call | tf_op jit(solution)/shard_map/pallas_call | solution.py:803
  541.6 1.0 slice.74
  551.0 1.3 bitcast_convert_fusion
  553.0 1.2 reshape.169
  554.7 1.1 maximum_convert_fusion
  (150 shorter events, 26.2 us)
Async XLA Ops:
  7.2 3.5 copy-start.16
  7.2 231.0 %all-gather.3.cloned.1.call-start = ((), (), s32[]{:S(2)}) async-start(), calls=%async_computation.2 | async-start | bytes 9732096 | tf_op jit(solution)/shard_map/all_gather | solution.py:1055
  9.7 2.5 copy-start.22
  9.7 2.5 copy-start.18
  10.8 2.0 copy-start.27
  10.8 2.0 copy-start.28
  10.8 2.0 copy-start.29
  10.8 2.1 copy-start.26
  158.3 1.6 copy-start.1
  158.3 1.7 copy-start.2
  158.3 394.7 %reduce-scatter.2.cloned.1.call-start = ((), (), s32[]{:S(2)}) async-start(), calls=%async_computation.1 | async-start | bytes 9732096 | tf_op jit(solution)/shard_map/reduce_scatter | solution.py:1089
  184.6 2.0 collective-permute-start
  205.0 3.7 collective-permute-start.1
  209.6 28.5 %copy-start.8 = (bf16[1,512,768]{2,1,0:T(8,128)(2,1)S(1)}, bf16[1,512,768]{2,1,0:T(8,128)(2,1)}, u32[]{:S(2)}) copy-start(bf16[1,512,768]{2,1,0:T(8,128)(2,1)} %param.16) | copy-start | bytes 2359300
  238.2 23.6 %collective-permute-start.4 = (bf16[1,512,768]{2,1,0:T(8,128)(2,1)S(1)}, bf16[1,512,768]{2,1,0:T(8,128)(2,1)S(1)}, u32[]{:S(2)}, u32[]{:S(2)}) collective-permute-start(bf16[1,512,768]{2,1,0:T(8,128)(2,1)S(1)} %copy-done.8), channel_id=1, source_target_pairs={{1,2},{2,1},{5,6},{6,5},{9,10},{10,9},{13,14},{14,13},{17,18},{18,... | collective-permute-start | bytes 2359304 | tf_op jit(solution)/shard_map/ppermute | solution.py:1012
  241.4 2.0 collective-permute-start.2
  289.4 1.6 copy-start
  290.5 2.3 collective-permute-start.5
  325.9 1.5 copy-start.3
  325.9 5.3 collective-permute-start.6
  326.4 4.8 copy-start.5
  328.3 32.4 %collective-permute-start.3 = (bf16[1,512,768]{2,1,0:T(8,128)(2,1)}, bf16[1,512,768]{2,1,0:T(8,128)(2,1)}, u32[]{:S(2)}, u32[]{:S(2)}) collective-permute-start(bf16[1,512,768]{2,1,0:T(8,128)(2,1)} %convert_bitcast_fusion.1), channel_id=1, source_target_pairs={{1,2},{2,1},{5,6},{6,5},{9,10},{10,9},{13,14},{14,13},{17,18},{18,... | collective-permute-start | bytes 2359304 | tf_op jit(solution)/shard_map/ppermute | solution.py:1012
  360.6 2.8 collective-permute-start.7
  364.3 32.2 %copy-start.19 = (bf16[768,128]{1,0:T(8,128)(2,1)S(1)}, bf16[768,128]{1,0:T(8,128)(2,1)}, u32[]{:S(2)}) copy-start(bf16[768,128]{1,0:T(8,128)(2,1)} %get-tuple-element.133) | copy-start | bytes 589828
  364.3 34.0 %copy-start.12 = (bf16[2304,128]{1,0:T(8,128)(2,1)S(1)}, bf16[2304,128]{1,0:T(8,128)(2,1)}, u32[]{:S(2)}) copy-start(bf16[2304,128]{1,0:T(8,128)(2,1)} %get-tuple-element.135) | copy-start | bytes 1769476
  541.5 2.4 copy-start.23
  541.5 3.1 copy-start.25
  541.6 5.5 copy-start.17
  542.7 4.9 copy-start.21
  543.7 4.2 copy-start.20
  543.9 4.2 copy-start.24
  547.4 3.6 copy-start.7
  (8 other events, 7.8 us)
Sparse Core Ops, SparseCore 0:
  158.5 79.6 all-gather.2
  289.5 135.2 reduce-scatter.1
